TPU v7x, 32 devices: a whole 2x2x4 slice. The times are simulated.
32 devices in a mesh: shard: 4 (over z), ctx: 2 (over x), tp: 4 (over y, core).
Axes of the slice: x: 2, y: 2, z: 4, core: 2. Of those that a mesh axis runs over, the one named last changes fastest.
Arguments:
- inputs: bfloat16 [4, 2048, 1024], P('shard', ('ctx', 'tp')), may hold values from -6 to 6
- encoded: bfloat16 [4, 512, 1024], P('shard', 'ctx'), may hold values from -6 to 6
- doc_lengths: int32 [4, 4], P('shard'), may hold values from 1 to 1025, 2048 in all within a row
- cotangent: bfloat16 [4, 2048, 1024], P('shard', ('ctx', 'tp')), may hold values from -6 to 6
- query_weight: bfloat16 [1024, 1024], P('shard', 'tp'), may hold values from -0.1875 to 0.1875
- key_weight: bfloat16 [1024, 1024], P('shard', 'tp'), may hold values from -0.1875 to 0.1875
- value_weight: bfloat16 [1024, 1024], P('shard', 'tp'), may hold values from -0.1875 to 0.1875
- out_weight: bfloat16 [1024, 1024], P('tp', 'shard'), may hold values from -3 to 3
- memory_query: bfloat16 [1024, 1024], P('shard', 'tp'), may hold values from -0.1875 to 0.1875
- memory_key: bfloat16 [1024, 1024], P('shard', 'tp'), may hold values from -0.1875 to 0.1875
- memory_value: bfloat16 [1024, 1024], P('shard', 'tp'), may hold values from -0.1875 to 0.1875
- memory_out: bfloat16 [1024, 1024], P('tp', 'shard'), may hold values from -4 to 4
- up_weight: bfloat16 [1024, 4096], P('shard', 'tp'), may hold values from -0.1875 to 0.1875
- down_weight: bfloat16 [4096, 1024], P('tp', 'shard'), may hold values from -0.09375 to 0.09375
- query_bias: float32 [1024], P('tp'), may hold values from -4 to 4
- value_bias: float32 [1024], P('tp'), may hold values from -0.75 to 0.75
- memory_qbias: float32 [1024], P('tp'), may hold values from -4 to 4
- memory_vbias: float32 [1024], P('tp'), may hold values from -0.75 to 0.75
- up_bias: float32 [4096], P('tp'), may hold values from -4 to 4
- out_bias: float32 [1024], replicated, may hold values from -4 to 4
- memory_obias: float32 [1024], replicated, may hold values from -4 to 4
- down_bias: float32 [1024], replicated, may hold values from -4 to 4
- gain_self: float32 [1024], replicated, may hold values from 0.5 to 1.5
- shift_self: float32 [1024], replicated, may hold values from -4 to 4
- gain_memory: float32 [1024], replicated, may hold values from 0.5 to 1.5
- shift_memory: float32 [1024], replicated, may hold values from -4 to 4
- gain_dense: float32 [1024], replicated, may hold values from 0.5 to 1.5
- shift_dense: float32 [1024], replicated, may hold values from -4 to 4
Outputs:
- outputs: bfloat16 [4, 2048, 1024], P('shard', ('ctx', 'tp'))
- inputs_grad: float32 [4, 2048, 1024], P('shard', ('ctx', 'tp'))
- encoded_grad: float32 [4, 512, 1024], P('shard', ('ctx', 'tp'))
- query_weight_grad: float32 [1024, 1024], P(('shard', 'ctx'), 'tp')
- key_weight_grad: float32 [1024, 1024], P(('shard', 'ctx'), 'tp')
- value_weight_grad: float32 [1024, 1024], P(('shard', 'ctx'), 'tp')
- out_weight_grad: float32 [1024, 1024], P('tp', ('shard', 'ctx'))
- memory_query_grad: float32 [1024, 1024], P(('shard', 'ctx'), 'tp')
- memory_key_grad: float32 [1024, 1024], P(('shard', 'ctx'), 'tp')
- memory_value_grad: float32 [1024, 1024], P(('shard', 'ctx'), 'tp')
- memory_out_grad: float32 [1024, 1024], P('tp', ('shard', 'ctx'))
- up_weight_grad: float32 [1024, 4096], P(('shard', 'ctx'), 'tp')
- down_weight_grad: float32 [4096, 1024], P('tp', ('shard', 'ctx'))
- query_bias_grad: float32 [1024], P('tp')
- value_bias_grad: float32 [1024], P('tp')
- memory_qbias_grad: float32 [1024], P('tp')
- memory_vbias_grad: float32 [1024], P('tp')
- up_bias_grad: float32 [4096], P('tp')
- out_bias_grad: float32 [1024], replicated
- memory_obias_grad: float32 [1024], replicated
- down_bias_grad: float32 [1024], replicated
- gain_self_grad: float32 [1024], replicated
- shift_self_grad: float32 [1024], replicated
- gain_memory_grad: float32 [1024], replicated
- shift_memory_grad: float32 [1024], replicated
- gain_dense_grad: float32 [1024], replicated
- shift_dense_grad: float32 [1024], replicated
Inputs may be any that keep to these rules, and one draw needn't show every extreme that they name: `doc_lengths`: each row holds the 4 document lengths of one packed sequence in order; they sum to 2048, and the longest is exactly 1025.
All inputs are finite; a program needn't handle non-finite values.
Results may differ from a plain program's by a relative error of at most 0.025.
Values may be sent and summed in bfloat16 or wider, within the bound.
No kernel may reach another device: no remote copies, remote signals or barrier semaphores. Data moves between devices by JAX's collectives and lax.ppermute only.
A program may use at most 192 MiB of HBM per device.

v0:
```python
from functools import partial

import jax
import jax.numpy as jnp
from jax import lax
from jax.sharding import PartitionSpec as P

HDIM = 64
W = 1024


EPSILON = 1e-05
NEGATIVE = -1e30


def from_behind(array, axis, by):
    count = lax.axis_size(axis)
    pairs = [(i, i + by) for i in range(count) if 0 <= i + by < count]
    return lax.ppermute(array, axis, pairs)


def matmul(left, right):
    return jnp.dot(left, right, preferred_element_type=jnp.float32)


def contract(form, left, right):
    return jnp.einsum(form, left, right, preferred_element_type=jnp.float32)


def rows_of(value, start, count):
    return lax.dynamic_slice_in_dim(value, start, count, 0)


def layer_norm(value, gain, shift):
    centre = value - jnp.mean(value, axis=-1, keepdims=True)
    rstd = lax.rsqrt(jnp.mean(centre * centre, axis=-1, keepdims=True) + EPSILON)
    normed = centre * rstd
    return (normed * gain + shift, normed, rstd)


def norm_back(grad_out, normed, rstd, gain):
    scaled = grad_out * gain
    inner = scaled - jnp.mean(scaled, axis=-1, keepdims=True)
    inner = inner - normed * jnp.mean(scaled * normed, axis=-1, keepdims=True)
    return (rstd * inner, jnp.sum(grad_out * normed, axis=0), jnp.sum(grad_out, axis=0))


def split_heads(value, heads):
    return value.reshape(value.shape[0], heads, -1)


def probabilities(query, keys, allowed, heads):
    scores = contract("qhd,khd->hqk", split_heads(query, heads), split_heads(keys, heads))
    if allowed is not None:
        scores = jnp.where(allowed[None], scores, NEGATIVE)
    top = jnp.max(scores, axis=-1, keepdims=True)
    expo = jnp.exp(scores - top)
    if allowed is not None:
        expo = jnp.where(allowed[None], expo, 0.0)
    return expo / jnp.sum(expo, axis=-1, keepdims=True)


def attend(query, keys, values, allowed, heads):
    probs = probabilities(query, keys, allowed, heads).astype(jnp.bfloat16)
    mixed = contract("hqk,khd->qhd", probs, split_heads(values, heads))
    return mixed.reshape(query.shape[0], -1).astype(jnp.bfloat16)


def attend_back(query, keys, values, allowed, heads, grad_mixed):
    probs = probabilities(query, keys, allowed, heads)
    grad_heads = split_heads(grad_mixed, heads)
    grad_probs = contract("qhd,khd->hqk", grad_heads, split_heads(values, heads))
    inner = jnp.sum(grad_probs * probs, axis=-1, keepdims=True)
    grad_scores = (probs * (grad_probs - inner)).astype(jnp.bfloat16)
    grad_query = contract("hqk,khd->qhd", grad_scores, split_heads(keys, heads))
    grad_keys = contract("hqk,qhd->khd", grad_scores, split_heads(query, heads))
    grad_values = contract("hqk,qhd->khd", probs.astype(jnp.bfloat16), grad_heads)
    count = keys.shape[0]
    return (
        grad_query.reshape(query.shape[0], -1),
        grad_keys.reshape(count, -1),
        grad_values.reshape(count, -1),
    )


def segment_ids(positions, ends):
    return jnp.sum((positions[:, None] >= ends[None, :]).astype(jnp.int32), axis=1)


def window_mask(pos_query, pos_key, ends):
    seg_query = segment_ids(pos_query, ends)
    seg_key = segment_ids(pos_key, ends)
    allowed = (seg_query[:, None] == seg_key[None, :]) & (pos_key[None, :] <= pos_query[:, None])
    return allowed & (pos_key[None, :] > pos_query[:, None] - W) & (pos_key[None, :] >= 0)


def column_sum(value):
    return jnp.sum(value.astype(jnp.float32), axis=0)


def per_device(
    inputs,
    encoded,
    doc_lengths,
    cotangent,
    query_weight,
    key_weight,
    value_weight,
    out_weight,
    memory_query,
    memory_key,
    memory_value,
    memory_out,
    up_weight,
    down_weight,
    query_bias,
    value_bias,
    memory_qbias,
    memory_vbias,
    up_bias,
    out_bias,
    memory_obias,
    down_bias,
    gain_self,
    shift_self,
    gain_memory,
    shift_memory,
    gain_dense,
    shift_dense,
):
    share = inputs[0]
    share_rows = share.shape[0]
    rows = share_rows * lax.axis_size("tp")
    block = min(512, rows)
    blocks = rows // block
    base = lax.axis_index("ctx") * rows
    ends = jnp.cumsum(doc_lengths[0], dtype=jnp.int32)
    block_ids = jnp.arange(blocks, dtype=jnp.int32)
    own_states = encoded[0]
    (
        query_full,
        key_full,
        value_full,
        out_full,
        mquery_full,
        mkey_full,
        mvalue_full,
        mout_full,
        up_full,
        down_full,
    ) = (
        lax.all_gather(query_weight, "shard", axis=0, tiled=True),
        lax.all_gather(key_weight, "shard", axis=0, tiled=True),
        lax.all_gather(value_weight, "shard", axis=0, tiled=True),
        lax.all_gather(out_weight, "shard", axis=1, tiled=True),
        lax.all_gather(memory_query, "shard", axis=0, tiled=True),
        lax.all_gather(memory_key, "shard", axis=0, tiled=True),
        lax.all_gather(memory_value, "shard", axis=0, tiled=True),
        lax.all_gather(memory_out, "shard", axis=1, tiled=True),
        lax.all_gather(up_weight, "shard", axis=0, tiled=True),
        lax.all_gather(down_weight, "shard", axis=1, tiled=True),
    )
    heads = query_full.shape[1] // HDIM
    width = query_full.shape[1]

    def gather_rows(piece):
        return lax.all_gather(piece, "tp", axis=0, tiled=True)

    def reduce_rows(term):
        return lax.psum_scatter(
            term(jnp.int32(0), share_rows * lax.axis_size("tp")),
            "tp",
            scatter_dimension=0,
            tiled=True,
        )

    inputs_rows = gather_rows(share)
    query_low = ((matmul(inputs_rows, query_full) + query_bias) * 0.125).astype(jnp.bfloat16)
    keys_low = matmul(inputs_rows, key_full).astype(jnp.bfloat16)
    values_low = (matmul(inputs_rows, value_full) + value_bias).astype(jnp.bfloat16)
    halo_keys, halo_values = from_behind((keys_low, values_low), "ctx", 1)
    keys_all = jnp.concatenate([halo_keys, keys_low], axis=0)
    values_all = jnp.concatenate([halo_values, values_low], axis=0)

    def self_inputs(index):
        start = index * block
        pos_query = base + start + jnp.arange(block, dtype=jnp.int32)
        pos_key = base - W + start + jnp.arange(block + W, dtype=jnp.int32)
        return (
            rows_of(query_low, start, block),
            rows_of(keys_all, start, block + W),
            rows_of(values_all, start, block + W),
            window_mask(pos_query, pos_key, ends),
        )

    self_mixed = lax.map(lambda index: attend(*self_inputs(index), heads), block_ids).reshape(
        rows, width
    )
    attn_share = reduce_rows(
        lambda start, count: matmul(rows_of(self_mixed, start, count), out_full)
    )
    first, normed_one, rstd_one = layer_norm(
        share.astype(jnp.float32) + attn_share + out_bias, gain_self, shift_self
    )
    first_rows = gather_rows(first.astype(jnp.bfloat16))
    mquery_low = ((matmul(first_rows, mquery_full) + memory_qbias) * 0.125).astype(jnp.bfloat16)
    states = lax.all_gather(own_states, "ctx", axis=0, tiled=True)
    mkeys_low = matmul(states, mkey_full).astype(jnp.bfloat16)
    mvalues_low = (matmul(states, mvalue_full) + memory_vbias).astype(jnp.bfloat16)

    def cross_block(index):
        return attend(
            rows_of(mquery_low, index * block, block), mkeys_low, mvalues_low, None, heads
        )

    cross_mixed = lax.map(cross_block, block_ids).reshape(rows, width)
    cross_share = reduce_rows(
        lambda start, count: matmul(rows_of(cross_mixed, start, count), mout_full)
    )
    second, normed_two, rstd_two = layer_norm(
        first + cross_share + memory_obias, gain_memory, shift_memory
    )
    second_rows = gather_rows(second.astype(jnp.bfloat16))
    hidden = matmul(second_rows, up_full) + up_bias
    activated, gelu_back = jax.vjp(partial(jax.nn.gelu, approximate=False), hidden)
    act_low = activated.astype(jnp.bfloat16)
    dense_share = reduce_rows(
        lambda start, count: matmul(rows_of(act_low, start, count), down_full)
    )
    result, normed_three, rstd_three = layer_norm(
        second + dense_share + down_bias, gain_dense, shift_dense
    )
    grad_three, gain_dense_grad, shift_dense_grad = norm_back(
        cotangent[0].astype(jnp.float32), normed_three, rstd_three, gain_dense
    )
    dense_low = grad_three.astype(jnp.bfloat16)
    down_bias_grad = column_sum(dense_low)
    dense_rows = gather_rows(dense_low)
    down_grad = contract("rf,rd->fd", act_low, dense_rows)
    (grad_hidden,) = gelu_back(contract("rd,fd->rf", dense_rows, down_full))
    hidden_low = grad_hidden.astype(jnp.bfloat16)
    up_bias_grad = column_sum(hidden_low)
    up_grad = contract("rd,rf->df", second_rows, hidden_low)
    second_share = reduce_rows(
        lambda start, count: contract("rf,df->rd", rows_of(hidden_low, start, count), up_full)
    )
    grad_two, gain_memory_grad, shift_memory_grad = norm_back(
        grad_three + second_share, normed_two, rstd_two, gain_memory
    )
    cross_low = grad_two.astype(jnp.bfloat16)
    memory_obias_grad = column_sum(cross_low)
    cross_rows = gather_rows(cross_low)
    mout_grad = contract("rk,rd->kd", cross_mixed, cross_rows)
    grad_cross_mixed = contract("rd,kd->rk", cross_rows, mout_full).astype(jnp.bfloat16)

    def cross_step(carry, index):
        start = index * block
        grad_query, grad_keys, grad_values = attend_back(
            rows_of(mquery_low, start, block),
            mkeys_low,
            mvalues_low,
            None,
            heads,
            rows_of(grad_cross_mixed, start, block),
        )
        return ((carry[0] + grad_keys, carry[1] + grad_values), grad_query)

    memory_empty = jnp.zeros((mkeys_low.shape[0], width), jnp.float32)
    (mkeys_sum, mvalues_sum), mquery_parts = lax.scan(
        cross_step, (memory_empty, memory_empty), block_ids
    )
    mquery_pre = mquery_parts.reshape(rows, width).astype(jnp.bfloat16) * 0.125
    mkey_rows, mvalue_rows = (
        lax.psum_scatter(
            mkeys_sum.astype(jnp.bfloat16), "ctx", scatter_dimension=0, tiled=True
        ).astype(jnp.float32),
        lax.psum_scatter(
            mvalues_sum.astype(jnp.bfloat16), "ctx", scatter_dimension=0, tiled=True
        ).astype(jnp.float32),
    )
    mkey_low = mkey_rows.astype(jnp.bfloat16)
    mvalue_low = mvalue_rows.astype(jnp.bfloat16)
    mkey_grad = contract("ed,ek->dk", own_states, mkey_low)
    mvalue_grad = contract("ed,ek->dk", own_states, mvalue_low)
    memory_vbias_grad = column_sum(mvalue_low)
    states_start = jnp.int32(0)
    states_count = own_states.shape[0] // lax.axis_size("tp") * lax.axis_size("tp")
    encoded_grad = lax.psum_scatter(
        (
            contract("ek,dk->ed", rows_of(mkey_low, states_start, states_count), mkey_full)
            + contract("ek,dk->ed", rows_of(mvalue_low, states_start, states_count), mvalue_full)
        ).astype(jnp.bfloat16),
        "tp",
        scatter_dimension=0,
        tiled=True,
    ).astype(jnp.float32)
    mquery_grad = contract("rd,rk->dk", first_rows, mquery_pre)
    memory_qbias_grad = column_sum(mquery_pre)
    first_share = reduce_rows(
        lambda start, count: contract("rk,dk->rd", rows_of(mquery_pre, start, count), mquery_full)
    )
    grad_one, gain_self_grad, shift_self_grad = norm_back(
        grad_two + first_share, normed_one, rstd_one, gain_self
    )
    self_low = grad_one.astype(jnp.bfloat16)
    out_bias_grad = column_sum(self_low)
    self_rows = gather_rows(self_low)
    out_grad = contract("rk,rd->kd", self_mixed, self_rows)
    grad_self_mixed = contract("rd,kd->rk", self_rows, out_full).astype(jnp.bfloat16)

    def self_step(carry, index):
        keys_acc, values_acc = carry
        start = index * block
        query, keys, values, allowed = self_inputs(index)
        grad_query, grad_keys, grad_values = attend_back(
            query, keys, values, allowed, heads, rows_of(grad_self_mixed, start, block)
        )
        keys_acc = lax.dynamic_update_slice_in_dim(
            keys_acc, rows_of(keys_acc, start, block + W) + grad_keys, start, 0
        )
        values_acc = lax.dynamic_update_slice_in_dim(
            values_acc, rows_of(values_acc, start, block + W) + grad_values, start, 0
        )
        return ((keys_acc, values_acc), grad_query)

    self_empty = jnp.zeros((rows + W, width), jnp.float32)
    (keys_acc, values_acc), query_parts = lax.scan(self_step, (self_empty, self_empty), block_ids)
    back_keys, back_values = (
        from_behind(keys_acc[:W].astype(jnp.bfloat16), "ctx", -1).astype(jnp.float32),
        from_behind(values_acc[:W].astype(jnp.bfloat16), "ctx", -1).astype(jnp.float32),
    )
    keys_grad_low = jnp.concatenate([keys_acc[W:rows], keys_acc[rows:] + back_keys], axis=0).astype(
        jnp.bfloat16
    )
    values_grad_low = jnp.concatenate(
        [values_acc[W:rows], values_acc[rows:] + back_values], axis=0
    ).astype(jnp.bfloat16)
    query_pre = query_parts.reshape(rows, width).astype(jnp.bfloat16) * 0.125
    query_grad = contract("rd,rk->dk", inputs_rows, query_pre)
    key_grad = contract("rd,rk->dk", inputs_rows, keys_grad_low)
    value_grad = contract("rd,rk->dk", inputs_rows, values_grad_low)
    query_bias_grad = column_sum(query_pre)
    value_bias_grad = column_sum(values_grad_low)

    def inputs_term(start, count):
        total = contract("rk,dk->rd", rows_of(query_pre, start, count), query_full)
        total = total + contract("rk,dk->rd", rows_of(keys_grad_low, start, count), key_full)
        return total + contract("rk,dk->rd", rows_of(values_grad_low, start, count), value_full)

    inputs_grad = grad_one + reduce_rows(inputs_term)
    (
        query_weight_grad,
        key_weight_grad,
        value_weight_grad,
        out_weight_grad,
        memory_query_grad,
        memory_key_grad,
        memory_value_grad,
        memory_out_grad,
        up_weight_grad,
        down_weight_grad,
    ) = (
        lax.psum_scatter(query_grad, ("shard", "ctx"), scatter_dimension=0, tiled=True),
        lax.psum_scatter(key_grad, ("shard", "ctx"), scatter_dimension=0, tiled=True),
        lax.psum_scatter(value_grad, ("shard", "ctx"), scatter_dimension=0, tiled=True),
        lax.psum_scatter(out_grad, ("shard", "ctx"), scatter_dimension=1, tiled=True),
        lax.psum_scatter(mquery_grad, ("shard", "ctx"), scatter_dimension=0, tiled=True),
        lax.psum_scatter(mkey_grad, ("shard", "ctx"), scatter_dimension=0, tiled=True),
        lax.psum_scatter(mvalue_grad, ("shard", "ctx"), scatter_dimension=0, tiled=True),
        lax.psum_scatter(mout_grad, ("shard", "ctx"), scatter_dimension=1, tiled=True),
        lax.psum_scatter(up_grad, ("shard", "ctx"), scatter_dimension=0, tiled=True),
        lax.psum_scatter(down_grad, ("shard", "ctx"), scatter_dimension=1, tiled=True),
    )
    query_bias_total, value_bias_total, memory_qbias_total, memory_vbias_total, up_bias_total = (
        lax.psum(
            (query_bias_grad, value_bias_grad, memory_qbias_grad, memory_vbias_grad, up_bias_grad),
            ("shard", "ctx"),
        )
    )
    (
        out_bias_total,
        memory_obias_total,
        down_bias_total,
        gain_self_total,
        shift_self_total,
        gain_memory_total,
        shift_memory_total,
        gain_dense_total,
        shift_dense_total,
    ) = lax.psum(
        (
            out_bias_grad,
            memory_obias_grad,
            down_bias_grad,
            gain_self_grad,
            shift_self_grad,
            gain_memory_grad,
            shift_memory_grad,
            gain_dense_grad,
            shift_dense_grad,
        ),
        ("shard", "ctx", "tp"),
    )
    return (
        result.astype(jnp.bfloat16)[None],
        inputs_grad[None],
        encoded_grad[None],
        query_weight_grad,
        key_weight_grad,
        value_weight_grad,
        out_weight_grad,
        memory_query_grad,
        memory_key_grad,
        memory_value_grad,
        memory_out_grad,
        up_weight_grad,
        down_weight_grad,
        query_bias_total,
        value_bias_total,
        memory_qbias_total,
        memory_vbias_total,
        up_bias_total,
        out_bias_total,
        memory_obias_total,
        down_bias_total,
        gain_self_total,
        shift_self_total,
        gain_memory_total,
        shift_memory_total,
        gain_dense_total,
        shift_dense_total,
    )


def solution(mesh):
    placed = (
        P("shard", ("ctx", "tp"), None),
        P("shard", "ctx", None),
        P("shard", None),
        P("shard", ("ctx", "tp"), None),
        P("shard", "tp"),
        P("shard", "tp"),
        P("shard", "tp"),
        P("tp", "shard"),
        P("shard", "tp"),
        P("shard", "tp"),
        P("shard", "tp"),
        P("tp", "shard"),
        P("shard", "tp"),
        P("tp", "shard"),
        P("tp"),
        P("tp"),
        P("tp"),
        P("tp"),
        P("tp"),
        P(),
        P(),
        P(),
        P(),
        P(),
        P(),
        P(),
        P(),
        P(),
    )
    return jax.shard_map(
        per_device,
        mesh=mesh,
        in_specs=placed,
        out_specs=(
            P("shard", ("ctx", "tp"), None),
            P("shard", ("ctx", "tp"), None),
            P("shard", ("ctx", "tp"), None),
            P(("shard", "ctx"), "tp"),
            P(("shard", "ctx"), "tp"),
            P(("shard", "ctx"), "tp"),
            P("tp", ("shard", "ctx")),
            P(("shard", "ctx"), "tp"),
            P(("shard", "ctx"), "tp"),
            P(("shard", "ctx"), "tp"),
            P("tp", ("shard", "ctx")),
            P(("shard", "ctx"), "tp"),
            P("tp", ("shard", "ctx")),
            P("tp"),
            P("tp"),
            P("tp"),
            P("tp"),
            P("tp"),
            P(),
            P(),
            P(),
            P(),
            P(),
            P(),
            P(),
            P(),
            P(),
        ),
        check_vma=False,
    )
```

profile of v0, /device:TPU:0, one launch (start us, length us, event | category | flops | bytes accessed | tf_op | source)
XLA Modules:
  0.0 1487.5 jit_solution(4711596765209247631)
XLA Ops:
  9.6 17.6 %all_gather.53 = bf16[1024,256]{1,0:T(8,128)(2,1)S(1)} all-gather(bf16[256,256]{1,0:T(8,128)(2,1)} %param.40), channel_id=1, replica_groups=mesh['shard'=4,'ctx'=2,'tp'=4] {'shard'}, dimensions={0}, use_global_device_ids=true | all-gather | bytes 655360 | tf_op jit(solution)/shard_map/all_gather | solution.py:152
  27.2 16.7 %all_gather.54 = bf16[1024,256]{1,0:T(8,128)(2,1)S(1)} all-gather(bf16[256,256]{1,0:T(8,128)(2,1)} %param.41), channel_id=1, replica_groups=mesh['shard'=4,'ctx'=2,'tp'=4] {'shard'}, dimensions={0}, use_global_device_ids=true | all-gather | bytes 655360 | tf_op jit(solution)/shard_map/all_gather | solution.py:153
  44.0 16.3 %all_gather.52 = bf16[1024,256]{1,0:T(8,128)(2,1)S(1)} all-gather(bf16[256,256]{1,0:T(8,128)(2,1)} %param.42), channel_id=1, replica_groups=mesh['shard'=4,'ctx'=2,'tp'=4] {'shard'}, dimensions={0}, use_global_device_ids=true | all-gather | bytes 655360 | tf_op jit(solution)/shard_map/all_gather | solution.py:154
  60.2 16.4 %all_gather.55 = bf16[256,1024]{1,0:T(8,128)(2,1)} all-gather(bf16[256,256]{1,0:T(8,128)(2,1)} %param.43), channel_id=1, replica_groups=mesh['shard'=4,'ctx'=2,'tp'=4] {'shard'}, dimensions={1}, use_global_device_ids=true | all-gather | bytes 655360 | tf_op jit(solution)/shard_map/all_gather | solution.py:155
  98.8 49.8 %while.55 = (s32[]{:T(128)}, bf16[2,512,256]{2,1,0:T(8,128)(2,1)}, s32[2]{0:T(128)S(1)}, bf16[2048,256]{0,1:T(8,128)(2,1)S(1)}, s32[]{:T(128)}, /*index=5*/s32[4...) while((s32[]{:T(128)}, bf16[2,512,256]{2,1,0:T(8,128)(2,1)}, ...), condition=%wide.region_6.7_spmd, body=%wide.region_1.6_spmd.sunk | while | flops 829060096 | bytes 37813608 | solution.py:196
  153.5 44.9 %reduce-scatter.20.cloned.1.call-done = f32[256,1024]{1,0:T(8,128)} async-done(((f32[1024,1024]{1,0:T(8,128)}), f32[256,1024]{1,0:T(8,128)}) %reduce-scatter.20.cloned.1.call-update) | async-done | bytes 1048592 | tf_op jit(solution)/shard_map/reduce_scatter | solution.py:170
  201.3 15.7 %all_gather.57 = bf16[1024,256]{1,0:T(8,128)(2,1)S(1)} all-gather(bf16[256,256]{1,0:T(8,128)(2,1)S(1)} %copy-done.40), channel_id=1, replica_groups=mesh['shard'=4,'ctx'=2,'tp'=4] {'shard'}, dimensions={0}, use_global_device_ids=true | all-gather | bytes 655360 | tf_op jit(solution)/shard_map/all_gather | solution.py:156
  217.0 16.8 %all_gather.59 = bf16[1024,256]{1,0:T(8,128)(2,1)S(1)} all-gather(bf16[256,256]{1,0:T(8,128)(2,1)S(1)} %copy-done.41), channel_id=1, replica_groups=mesh['shard'=4,'ctx'=2,'tp'=4] {'shard'}, dimensions={0}, use_global_device_ids=true | all-gather | bytes 655360 | tf_op jit(solution)/shard_map/all_gather | solution.py:157
  233.8 15.7 %all_gather.60 = bf16[1024,256]{1,0:T(8,128)(2,1)S(1)} all-gather(bf16[256,256]{1,0:T(8,128)(2,1)S(1)} %copy-done.42), channel_id=1, replica_groups=mesh['shard'=4,'ctx'=2,'tp'=4] {'shard'}, dimensions={0}, use_global_device_ids=true | all-gather | bytes 655360 | tf_op jit(solution)/shard_map/all_gather | solution.py:158
  249.5 15.6 %all_gather.61 = bf16[256,1024]{1,0:T(8,128)(2,1)} all-gather(bf16[256,256]{1,0:T(8,128)(2,1)S(1)} %copy-done.43), channel_id=1, replica_groups=mesh['shard'=4,'ctx'=2,'tp'=4] {'shard'}, dimensions={1}, use_global_device_ids=true | all-gather | bytes 655360 | tf_op jit(solution)/shard_map/all_gather | solution.py:159
  286.8 44.3 %reduce-scatter.22.cloned.1.call-done = f32[256,1024]{1,0:T(8,128)} async-done(((f32[1024,1024]{1,0:T(8,128)}), f32[256,1024]{1,0:T(8,128)}) %reduce-scatter.22.cloned.1.call-update) | async-done | bytes 1048592 | tf_op jit(solution)/shard_map/reduce_scatter | solution.py:170
  334.9 23.3 %all-gather.14.cloned.1.call-done = bf16[1024,1024]{1,0:T(8,128)(2,1)} async-done(((bf16[256,1024]{1,0:T(8,128)(2,1)}), bf16[1024,1024]{1,0:T(8,128)(2,1)}) %all-gather.14.cloned.1.call-update) | async-done | bytes 2097168 | tf_op jit(solution)/shard_map/all_gather | solution.py:167
  373.1 32.8 %all-gather.18.cloned.1.call-done = bf16[1024,1024]{1,0:T(8,128)(2,1)} async-done(((bf16[1024,256]{1,0:T(8,128)(2,1)}), bf16[1024,1024]{1,0:T(8,128)(2,1)}) %all-gather.18.cloned.1.call-update) | async-done | bytes 2097168 | tf_op jit(solution)/shard_map/all_gather | solution.py:161
  412.9 42.3 %reduce-scatter.24.cloned.1.call-done = f32[256,1024]{1,0:T(8,128)} async-done(((f32[1024,1024]{1,0:T(8,128)}), f32[256,1024]{1,0:T(8,128)}) %reduce-scatter.24.cloned.1.call-update) | async-done | bytes 1048592 | tf_op jit(solution)/shard_map/reduce_scatter | solution.py:170
  462.3 22.7 %all-gather.20.cloned.1.call-done = bf16[1024,1024]{1,0:T(8,128)(2,1)} async-done(((bf16[256,1024]{1,0:T(8,128)(2,1)}), bf16[1024,1024]{1,0:T(8,128)(2,1)}) %all-gather.20.cloned.1.call-update) | async-done | bytes 2097168 | tf_op jit(solution)/shard_map/all_gather | solution.py:167
  499.8 44.5 %reduce-scatter.26.cloned.1.call-done = f32[256,1024]{1,0:T(8,128)} async-done(((f32[1024,1024]{1,0:T(8,128)}), f32[256,1024]{1,0:T(8,128)}) %reduce-scatter.26.cloned.1.call-update) | async-done | bytes 1048592 | tf_op jit(solution)/shard_map/reduce_scatter | solution.py:170
  550.7 22.5 %all-gather.22.cloned.1.call-done = bf16[1024,1024]{1,0:T(8,128)(2,1)} async-done(((bf16[256,1024]{1,0:T(8,128)(2,1)}), bf16[1024,1024]{1,0:T(8,128)(2,1)}) %all-gather.22.cloned.1.call-update) | async-done | bytes 2097168 | tf_op jit(solution)/shard_map/all_gather | solution.py:167
  577.2 32.3 %while.58 = (s32[]{:T(128)}, f32[512,256]{0,1:T(8,128)}, f32[512,256]{0,1:T(8,128)S(1)}, bf16[2,512,256]{2,1,0:T(8,128)(2,1)}, s32[2]{0:T(128)S(1)}, /*index=5*/...) while((s32[]{:T(128)}, f32[512,256]{0,1:T(8,128)}, ...), condition=%wide.region_29.30_spmd.clone, body=%wide.region_25.29_spmd.clone.sunk | while | flops 818414592 | bytes 59818308 | solution.py:269
  617.6 43.0 %reduce-scatter.28.cloned.1.call-done = f32[256,1024]{1,0:T(8,128)} async-done(((f32[1024,1024]{1,0:T(8,128)}), f32[256,1024]{1,0:T(8,128)}) %reduce-scatter.28.cloned.1.call-update) | async-done | bytes 1048592 | tf_op jit(solution)/shard_map/reduce_scatter | solution.py:170
  702.1 80.8 %while.57 = (s32[]{:T(128)}, f32[2048,256]{0,1:T(8,128)}, f32[2048,256]{0,1:T(8,128)}, bf16[2,512,256]{2,1,0:T(8,128)(2,1)}, s32[2]{0:T(128)S(1)}, /*index=5*/bf...) while((s32[]{:T(128)}, f32[2048,256]{0,1:T(8,128)}, ...), condition=%wide.region_39.40_spmd, body=%wide.region_33.39_spmd.sunk | while | flops 2059693568 | bytes 170491312 | solution.py:327
  790.5 15.4 %collective-permute-done.3 = bf16[1024,256]{0,1:T(8,128)(2,1)S(1)} collective-permute-done((bf16[1024,256]{0,1:T(8,128)(2,1)S(1)}, bf16[1024,256]{0,1:T(8,128)(2,1)S(1)}, u32[]{:S(2)}, u32[]{:S(2)}) %collective-permute-start.3) | collective-permute-done | bytes 524320 | tf_op jit(solution)/shard_map/ppermute | solution.py:19
  812.1 15.0 %collective-permute-done.2 = bf16[1024,256]{0,1:T(8,128)(2,1)S(1)} collective-permute-done((bf16[1024,256]{0,1:T(8,128)(2,1)S(1)}, bf16[1024,256]{0,1:T(8,128)(2,1)S(1)}, u32[]{:S(2)}, u32[]{:S(2)}) %collective-permute-start.2) | collective-permute-done | bytes 524320 | tf_op jit(solution)/shard_map/ppermute | solution.py:19
  869.1 40.5 %all-reduce = (f32[1024]{0:T(1024)}, f32[1024]{0:T(1024)}, f32[1024]{0:T(1024)}, f32[1024]{0:T(1024)}, f32[1024]{0:T(1024)}, /*index=5*/f32[1024]{0:T(1024)}, f32[1024]{0:T(1024)}, f32[1024]{0:T(1024)}, f32[1024]{0:T(1024)}) all-reduce(f32[1024]{0:T(1024)S(1)} %copy-done.56, ...), channel_id=1, replica_groups=mesh['shard'=4,'ctx'=2,'tp'=4] {'shard','ctx','tp'}, use_global_device_ids=true, to_apply=%region_65.66 | all-reduce | flops 9216 | bytes 73728 | tf_op jit(solution)/shard_map/psum | solution.py:390
  909.6 22.1 %all-reduce.1 = (f32[256]{0:T(256)}, f32[256]{0:T(256)}, f32[256]{0:T(256)}, f32[256]{0:T(256)}, f32[1024]{0:T(1024)}) all-reduce(f32[256]{0:T(256)S(1)} %get-tuple-element.752, f32[256]{0:T(256)S(1)} %get-tuple-element.750, f32[256]{0:T(256)S(1)} %copy-done.60, ...), channel_id=1, replica_groups=mesh['shard'=4,'ctx'=2,'tp'=4] {'shard','ctx'}, use_global_device_ids=true, to_apply=%region_55.56 | all-reduce | flops 2048 | bytes 16384 | tf_op jit(solution)/shard_map/psum | solution.py:375
  933.4 47.4 %reduce-scatter.42.cloned.1.call-done = f32[128,256]{0,1:T(8,128)} async-done(((f32[1024,256]{0,1:T(8,128)}), f32[128,256]{0,1:T(8,128)}) %reduce-scatter.42.cloned.1.call-update) | async-done | bytes 131088 | tf_op jit(solution)/shard_map/reduce_scatter | solution.py:365
  982.5 64.8 %reduce-scatter.40.cloned.1.call-done = f32[128,256]{0,1:T(8,128)} async-done(((f32[1024,256]{0,1:T(8,128)}), f32[128,256]{0,1:T(8,128)}) %reduce-scatter.40.cloned.1.call-update) | async-done | bytes 131088 | tf_op jit(solution)/shard_map/reduce_scatter | solution.py:364
  1048.9 44.4 %reduce-scatter.30.cloned.1.call-done = f32[256,1024]{1,0:T(8,128)} async-done(((f32[1024,1024]{1,0:T(8,128)}), f32[256,1024]{1,0:T(8,128)}) %reduce-scatter.30.cloned.1.call-update) | async-done | bytes 1048592 | tf_op jit(solution)/shard_map/reduce_scatter | solution.py:170
  1095.7 90.2 %reduce-scatter.56.cloned.1.call-done = f32[1024,128]{1,0:T(8,128)} async-done(((f32[1024,1024]{1,0:T(8,128)}), f32[1024,128]{1,0:T(8,128)}) %reduce-scatter.56.cloned.1.call-update) | async-done | bytes 524304 | tf_op jit(solution)/shard_map/reduce_scatter | solution.py:372
  1185.8 92.1 %reduce-scatter.54.cloned.1.call-done = f32[128,1024]{1,0:T(8,128)} async-done(((f32[1024,1024]{1,0:T(8,128)}), f32[128,1024]{1,0:T(8,128)}) %reduce-scatter.54.cloned.1.call-update) | async-done | bytes 524304 | tf_op jit(solution)/shard_map/reduce_scatter | solution.py:371
  1278.0 67.7 %reduce-scatter.52.cloned.1.call-done = f32[256,128]{1,0:T(8,128)} async-done(((f32[256,1024]{1,0:T(8,128)}), f32[256,128]{1,0:T(8,128)}) %reduce-scatter.52.cloned.1.call-update) | async-done | bytes 131088 | tf_op jit(solution)/shard_map/reduce_scatter | solution.py:370
  1345.7 66.9 %reduce-scatter.46.cloned.1.call-done = f32[128,256]{1,0:T(8,128)} async-done(((f32[1024,256]{1,0:T(8,128)}), f32[128,256]{1,0:T(8,128)}) %reduce-scatter.46.cloned.1.call-update) | async-done | bytes 131088 | tf_op jit(solution)/shard_map/reduce_scatter | solution.py:367
  1412.6 67.0 %reduce-scatter.44.cloned.1.call-done = f32[256,128]{1,0:T(8,128)} async-done(((f32[256,1024]{1,0:T(8,128)}), f32[256,128]{1,0:T(8,128)}) %reduce-scatter.44.cloned.1.call-update) | async-done | bytes 131088 | tf_op jit(solution)/shard_map/reduce_scatter | solution.py:366
  (434 shorter events, 388.6 us)
Async XLA Ops:
  8.0 68.6 %all-gather.26.cloned.1.call-start = ((), (), s32[]{:S(2)}) async-start(), calls=%async_computation.45 | async-start | bytes 2621440 | tf_op jit(solution)/shard_map/all_gather | solution.py:167
  8.8 189.7 %reduce-scatter.20.cloned.1.call-start = ((), (), s32[]{:S(2)}) async-start(), calls=%async_computation.19 | async-start | bytes 5242880 | tf_op jit(solution)/shard_map/reduce_scatter | solution.py:170
  79.1 10.7 collective-permute-start
  84.0 11.4 collective-permute-start.1
  152.9 112.2 %all-gather.28.cloned.1.call-start = ((), (), s32[]{:S(2)}) async-start(), calls=%async_computation.46 | async-start | bytes 1572864 | tf_op jit(solution)/shard_map/all_gather | solution.py:207
  153.5 115.2 %all-gather.12.cloned.1.call-start = ((), (), s32[]{:S(2)}) async-start(), calls=%async_computation.20 | async-start | bytes 2621440 | tf_op jit(solution)/shard_map/all_gather | solution.py:167
  201.3 129.8 %reduce-scatter.22.cloned.1.call-start = ((), (), s32[]{:S(2)}) async-start(), calls=%async_computation.21 | async-start | bytes 5242880 | tf_op jit(solution)/shard_map/reduce_scatter | solution.py:170
  286.0 48.9 %all-gather.16.cloned.1.call-start = ((), (), s32[]{:S(2)}) async-start(), calls=%async_computation.23 | async-start | bytes 2621440 | tf_op jit(solution)/shard_map/all_gather | solution.py:160
  286.8 71.5 %all-gather.14.cloned.1.call-start = ((), (), s32[]{:S(2)}) async-start(), calls=%async_computation.22 | async-start | bytes 2621440 | tf_op jit(solution)/shard_map/all_gather | solution.py:167
  334.1 71.8 %all-gather.18.cloned.1.call-start = ((), (), s32[]{:S(2)}) async-start(), calls=%async_computation.24 | async-start | bytes 2621440 | tf_op jit(solution)/shard_map/all_gather | solution.py:161
  334.7 120.5 %reduce-scatter.24.cloned.1.call-start = ((), (), s32[]{:S(2)}) async-start(), calls=%async_computation.25 | async-start | bytes 5242880 | tf_op jit(solution)/shard_map/reduce_scatter | solution.py:170
  412.5 72.5 %all-gather.20.cloned.1.call-start = ((), (), s32[]{:S(2)}) async-start(), calls=%async_computation.26 | async-start | bytes 2621440 | tf_op jit(solution)/shard_map/all_gather | solution.py:167
  462.2 82.0 %reduce-scatter.26.cloned.1.call-start = ((), (), s32[]{:S(2)}) async-start(), calls=%async_computation.27 | async-start | bytes 5242880 | tf_op jit(solution)/shard_map/reduce_scatter | solution.py:170
  499.7 73.5 %all-gather.22.cloned.1.call-start = ((), (), s32[]{:S(2)}) async-start(), calls=%async_computation.28 | async-start | bytes 2621440 | tf_op jit(solution)/shard_map/all_gather | solution.py:167
  550.4 110.1 %reduce-scatter.28.cloned.1.call-start = ((), (), s32[]{:S(2)}) async-start(), calls=%async_computation.29 | async-start | bytes 5242880 | tf_op jit(solution)/shard_map/reduce_scatter | solution.py:170
  615.9 59.3 %reduce-scatter.32.cloned.1.call-start = ((), (), s32[]{:S(2)}) async-start(), calls=%async_computation.32 | async-start | bytes 393216 | tf_op jit(solution)/shard_map/reduce_scatter | solution.py:274
  616.7 72.2 %reduce-scatter.34.cloned.1.call-start = ((), (), s32[]{:S(2)}) async-start(), calls=%async_computation.33 | async-start | bytes 393216 | tf_op jit(solution)/shard_map/reduce_scatter | solution.py:277
  617.5 77.3 %all-gather.24.cloned.1.call-start = ((), (), s32[]{:S(2)}) async-start(), calls=%async_computation.30 | async-start | bytes 2621440 | tf_op jit(solution)/shard_map/all_gather | solution.py:167
  665.5 198.6 %reduce-scatter.36.cloned.1.call-start = ((), (), s32[]{:S(2)}) async-start(), calls=%async_computation.34 | async-start | bytes 655360 | tf_op jit(solution)/shard_map/reduce_scatter | solution.py:288
  691.0 174.7 %reduce-scatter.50.cloned.1.call-start = ((), (), s32[]{:S(2)}) async-start(), calls=%async_computation.41 | async-start | bytes 1179648 | tf_op jit(solution)/shard_map/reduce_scatter | solution.py:369
  693.3 174.1 %reduce-scatter.48.cloned.1.call-start = ((), (), s32[]{:S(2)}) async-start(), calls=%async_computation.40 | async-start | bytes 1179648 | tf_op jit(solution)/shard_map/reduce_scatter | solution.py:368
  694.7 237.0 %reduce-scatter.38.cloned.1.call-start = ((), (), s32[]{:S(2)}) async-start(), calls=%async_computation.35 | async-start | bytes 1179648 | tf_op jit(solution)/shard_map/reduce_scatter | solution.py:363
  787.5 193.4 %reduce-scatter.42.cloned.1.call-start = ((), (), s32[]{:S(2)}) async-start(), calls=%async_computation.37 | async-start | bytes 1179648 | tf_op jit(solution)/shard_map/reduce_scatter | solution.py:365
  789.0 16.9 %collective-permute-start.3 = (bf16[1024,256]{0,1:T(8,128)(2,1)S(1)}, bf16[1024,256]{0,1:T(8,128)(2,1)S(1)}, u32[]{:S(2)}, u32[]{:S(2)}) collective-permute-start(bf16[1024,256]{0,1:T(8,128)(2,1)S(1)} %slice.26), channel_id=1, source_target_pairs={{4,0},{5,1},{6,2},{7,3},{12,8},{13,9},{14,10},{15,11},{20,16},{21,... | collective-permute-start | bytes 1572872 | tf_op jit(solution)/shard_map/ppermute | solution.py:19
  810.6 236.7 %reduce-scatter.40.cloned.1.call-start = ((), (), s32[]{:S(2)}) async-start(), calls=%async_computation.36 | async-start | bytes 1179648 | tf_op jit(solution)/shard_map/reduce_scatter | solution.py:364
  810.8 16.3 %collective-permute-start.2 = (bf16[1024,256]{0,1:T(8,128)(2,1)S(1)}, bf16[1024,256]{0,1:T(8,128)(2,1)S(1)}, u32[]{:S(2)}, u32[]{:S(2)}) collective-permute-start(bf16[1024,256]{0,1:T(8,128)(2,1)S(1)} %slice.27), channel_id=1, source_target_pairs={{4,0},{5,1},{6,2},{7,3},{12,8},{13,9},{14,10},{15,11},{20,16},{21,... | collective-permute-start | bytes 1572872 | tf_op jit(solution)/shard_map/ppermute | solution.py:19
  831.3 262.0 %reduce-scatter.30.cloned.1.call-start = ((), (), s32[]{:S(2)}) async-start(), calls=%async_computation.31 | async-start | bytes 5242880 | tf_op jit(solution)/shard_map/reduce_scatter | solution.py:170
  837.1 348.7 %reduce-scatter.56.cloned.1.call-start = ((), (), s32[]{:S(2)}) async-start(), calls=%async_computation.44 | async-start | bytes 4718592 | tf_op jit(solution)/shard_map/reduce_scatter | solution.py:372
  844.6 433.3 %reduce-scatter.54.cloned.1.call-start = ((), (), s32[]{:S(2)}) async-start(), calls=%async_computation.43 | async-start | bytes 4718592 | tf_op jit(solution)/shard_map/reduce_scatter | solution.py:371
  852.2 493.5 %reduce-scatter.52.cloned.1.call-start = ((), (), s32[]{:S(2)}) async-start(), calls=%async_computation.42 | async-start | bytes 1179648 | tf_op jit(solution)/shard_map/reduce_scatter | solution.py:370
  856.6 556.0 %reduce-scatter.46.cloned.1.call-start = ((), (), s32[]{:S(2)}) async-start(), calls=%async_computation.39 | async-start | bytes 1179648 | tf_op jit(solution)/shard_map/reduce_scatter | solution.py:367
  860.2 619.4 %reduce-scatter.44.cloned.1.call-start = ((), (), s32[]{:S(2)}) async-start(), calls=%async_computation.38 | async-start | bytes 1179648 | tf_op jit(solution)/shard_map/reduce_scatter | solution.py:366
  (80 other events, 1864.1 us)
Sparse Core Ops, SparseCore 0:
  10.4 25.2 all-gather.25
  153.0 45.4 reduce-scatter.19
  288.4 46.4 all-gather.15
  336.9 21.3 all-gather.13
  359.6 46.2 all-gather.17
  462.4 22.5 all-gather.19
  550.6 22.5 all-gather.21
  616.0 44.4 reduce-scatter.27
  663.5 11.6 reduce-scatter.31
  677.2 11.6 reduce-scatter.33
Sparse Core Ops, SparseCore 1:
  154.9 22.0 all-gather.27
  201.4 22.4 all-gather.11
  286.1 44.9 reduce-scatter.21
  412.5 42.6 reduce-scatter.23
  499.8 44.4 reduce-scatter.25
  665.6 22.4 all-gather.23
  691.1 21.6 reduce-scatter.35
  716.0 64.0 reduce-scatter.49
  783.7 63.1 reduce-scatter.47
  850.8 63.1 reduce-scatter.37
  917.6 63.1 reduce-scatter.41
  984.2 63.0 reduce-scatter.39
  1049.8 43.4 reduce-scatter.29
  1097.5 88.2 reduce-scatter.55
  1190.5 87.4 reduce-scatter.53
  1282.0 63.6 reduce-scatter.51
  1350.1 62.5 reduce-scatter.45
  1416.6 63.0 reduce-scatter.43
where the time goes:
time: 1500 us; the launch traced here: 1490 us
  waiting for transfers between devices  922 us (61%)
  matrix products  215 us (14%)
  blocking collectives  193 us (13%)
  other arithmetic  62.9 us (4%)
  local copies, waits for them, and re-layouts  60.4 us (4%)
  between operations  17.1 us (1%)
    reduce_scatter x6, waiting for transfers between devices, reduce_rows(): lax.psum_scatter(term(jnp.int32(0), share_rows * lax.axis_size('tp')), 't...  263 us
    dot_general x40, matrix products, contract(): return jnp.einsum(form, left, right, preferred_element_type=jnp.float32)  128 us
    reduce_scatter x1, waiting for transfers between devices, per_device(): lax.psum_scatter(up_grad, ('shard', 'ctx'), scatter_dimension=0, tiled=True)  92.1 us
    reduce_scatter x1, waiting for transfers between devices, per_device(): lax.psum_scatter(down_grad, ('shard', 'ctx'), scatter_dimension=1, tiled=...  90.2 us
    all_gather x6, waiting for transfers between devices, gather_rows(): return lax.all_gather(piece, 'tp', axis=0, tiled=True)  68.6 us
    reduce_scatter x1, waiting for transfers between devices, per_device(): lax.psum_scatter(mout_grad, ('shard', 'ctx'), scatter_dimension=1, tiled=...  67.7 us
    reduce_scatter x1, waiting for transfers between devices, per_device(): lax.psum_scatter(out_grad, ('shard', 'ctx'), scatter_dimension=1, tiled=T...  67 us
    reduce_scatter x1, waiting for transfers between devices, per_device(): lax.psum_scatter(mquery_grad, ('shard', 'ctx'), scatter_dimension=0, tile...  66.9 us
  transfers between devices with their start and end apart: 32, of which 24 were waited for; matrix products, arithmetic and copies ran while one was open for 12% of the time, Pallas kernels for 0%

commit v1 on v0

v1 whole, which is shorter than its diff:
```python
from functools import partial

import jax
import jax.numpy as jnp
from jax import lax
from jax.experimental import pallas as pl
from jax.experimental.pallas import tpu as pltpu
from jax.sharding import PartitionSpec as P

HDIM = 64
W = 1024
TILE = 256
CHAINS = 1


EPSILON = 1e-05
NEGATIVE = -1e30
VMEM = 56 * 1024 * 1024


def matmul(left, right):
    return jnp.dot(left, right, preferred_element_type=jnp.float32)


def contract(form, left, right):
    return jnp.einsum(form, left, right, preferred_element_type=jnp.float32)


def low(value):
    return value.astype(jnp.bfloat16)


def wide(value):
    return value.astype(jnp.float32)


def swap(array, axis, bit):
    return lax.ppermute(array, axis, [(i, i ^ bit) for i in range(lax.axis_size(axis))])


def shift(array, axis, by):
    count = lax.axis_size(axis)
    pairs = [(i, i + by) for i in range(count) if 0 <= i + by < count]
    return lax.ppermute(array, axis, pairs)


def gather_direct(piece, axis):
    return [piece] + [swap(piece, axis, m) for m in range(1, lax.axis_size(axis))]


def gather_tree(piece, axis):
    count = lax.axis_size(axis)
    pieces = {0: piece}
    bit = count // 2
    while bit:
        for m in sorted(pieces):
            pieces[m | bit] = swap(pieces[m], axis, bit)
        bit //= 2
    return [pieces[m] for m in range(count)]


def scatter_tree(terms, axis):
    terms = list(terms)
    bit = 1
    while bit < len(terms):
        for m in reversed(range(bit, len(terms), 2 * bit)):
            arrived = swap(low(terms[m]), axis, bit)
            terms[m ^ bit] = wide(terms[m ^ bit]) + wide(arrived)
        bit *= 2
    return terms[0]


def scatter_direct(terms, axis):
    total = wide(terms[0])
    for m in range(1, lax.axis_size(axis)):
        total = total + wide(swap(low(terms[m]), axis, m))
    return total


def all_sum(value, axes):
    for axis in axes:
        bit = 1
        while bit < lax.axis_size(axis):
            value = value + swap(value, axis, bit)
            bit *= 2
    return value


def relative(array, dim, axis):
    count = lax.axis_size(axis)
    index = lax.axis_index(axis)
    size = array.shape[dim] // count
    blocks = [lax.slice_in_dim(array, m * size, (m + 1) * size, axis=dim) for m in range(count)]
    bit = 1
    while bit < count:
        odd = (index & bit) != 0
        blocks = [jnp.where(odd, blocks[m ^ bit], blocks[m]) for m in range(count)]
        bit *= 2
    return jnp.concatenate(blocks, axis=dim)


def stack_heads(value, heads):
    lane = lax.broadcasted_iota(jnp.int32, value.shape, 1) // HDIM
    zero = jnp.zeros_like(value)
    return jnp.concatenate([jnp.where(lane == h, value, zero) for h in range(heads)], axis=0)


def scores_of(rows, stacked, head, count):
    part = stacked[head * count : (head + 1) * count, :]
    return lax.dot_general(rows, part, (((1,), (1,)), ((), ())), preferred_element_type=jnp.float32)


def allowed_in(lower, key_start, query_start, shape):
    key = key_start + lax.broadcasted_iota(jnp.int32, shape, 0)
    query = query_start + lax.broadcasted_iota(jnp.int32, (1, shape[1]), 1)
    return (key >= lower) & (key <= query)


def attend_kernel(heads, masked, meta, *refs):
    if masked:
        lower_ref, query_ref, keys_ref, values_ref, old_keys_ref, old_values_ref = refs[:6]
        mixed_ref, mixed_t_ref, lse_ref, acc_ref = refs[6:]
        lower = lower_ref[...]
    else:
        query_ref, keys_ref, values_ref, mixed_ref, mixed_t_ref, lse_ref, acc_ref = refs
    step = pl.program_id(0)
    count = query_ref.shape[0]
    stacked = stack_heads(query_ref[...], heads)
    acc_ref[...] = jnp.zeros_like(acc_ref)
    tile = lax.bitwise_xor(step, meta[0])

    def add(carry, keys_from, values_from, place, key_tile, masking):
        rows = pl.ds(pl.multiple_of(place * count, count), count)
        keys, values_t = keys_from[rows, :], values_from[rows, :].T
        out = []
        for h in range(heads):
            top, total = carry[h]
            scores = scores_of(keys, stacked, h, count)
            if masking:
                ok = allowed_in(lower, key_tile * count, tile * count, scores.shape)
                scores = jnp.where(ok, scores, NEGATIVE)
            higher = jnp.maximum(top, jnp.max(scores, axis=0, keepdims=True))
            expo = jnp.exp(scores - higher)
            scale = jnp.exp(top - higher)
            part = slice(h * HDIM, (h + 1) * HDIM)
            acc_ref[part, :] = acc_ref[part, :] * scale + matmul(values_t[part, :], low(expo))
            out.append((higher, total * scale + jnp.sum(expo, axis=0, keepdims=True)))
        return tuple(out)

    first = jnp.full((1, count), NEGATIVE, jnp.float32)
    carry = tuple((first, jnp.zeros((1, count), jnp.float32)) for _ in range(heads))
    if masked:
        least = meta[1 + step]
        here = lambda n, c: add(
            c, keys_ref, values_ref, lax.bitwise_xor(tile - n, meta[0]), tile - n, True
        )
        carry = lax.fori_loop(0, tile - jnp.maximum(least, 0) + 1, here, carry)
        tiles = old_keys_ref.shape[0] // count
        before = lambda n, c: add(
            c, old_keys_ref, old_values_ref, lax.bitwise_xor(n + tiles, meta[0]), n, True
        )
        carry = lax.fori_loop(least, 0, before, carry)
    else:
        every = lambda n, c: add(c, keys_ref, values_ref, n, n, False)
        carry = lax.fori_loop(0, keys_ref.shape[0] // count, every, carry)
    for h in range(heads):
        top, total = carry[h]
        part = slice(h * HDIM, (h + 1) * HDIM)
        mixed_t_ref[part, :] = acc_ref[part, :] / total
        lse_ref[h : h + 1, :] = top + jnp.log(total)
    mixed_ref[...] = low(mixed_t_ref[...].T)


def attend_back_kernel(heads, masked, old, meta, *refs):
    refs = list(refs)
    lower = refs.pop(0)[...] if masked else None
    start_ref = refs.pop(0) if masked and not old else None
    query_ref, grad_ref, mixed_t_ref, lse_ref, keys_ref, values_ref = refs[:6]
    grad_query_ref, grad_keys_ref, grad_values_ref, keys_acc, values_acc, query_acc = refs[6:]
    step = pl.program_id(0)
    count = query_ref.shape[0]

    @pl.when(step == 0)
    def _():
        keys_acc[...] = jnp.zeros_like(keys_acc)
        values_acc[...] = jnp.zeros_like(values_acc)

    tile = lax.bitwise_xor(step, meta[0])
    if start_ref is None:
        query_acc[...] = jnp.zeros_like(query_acc)
    else:
        query_acc[...] = start_ref[...]
    stacked = stack_heads(query_ref[...], heads)
    grad = grad_ref[...]
    stacked_grad = stack_heads(grad, heads)
    weighed = wide(grad.T) * mixed_t_ref[...]
    lse = lse_ref[...]
    inner = [
        jnp.sum(weighed[h * HDIM : (h + 1) * HDIM, :], axis=0, keepdims=True) for h in range(heads)
    ]

    def add(place, key_tile):
        rows = pl.ds(pl.multiple_of(place * count, count), count)
        keys, values = keys_ref[rows, :], values_ref[rows, :]
        keys_t = keys.T
        probs, slopes = [], []
        if masked:
            ok = allowed_in(lower, key_tile * count, tile * count, (count, count))
        for h in range(heads):
            expo = jnp.exp(scores_of(keys, stacked, h, count) - lse[h : h + 1, :])
            if masked:
                expo = jnp.where(ok, expo, 0.0)
            slope = low(expo * (scores_of(values, stacked_grad, h, count) - inner[h]))
            part = slice(h * HDIM, (h + 1) * HDIM)
            query_acc[part, :] += matmul(keys_t[part, :], slope)
            probs.append(low(expo))
            slopes.append(slope)
        values_acc[rows, :] += matmul(jnp.concatenate(probs, axis=1), stacked_grad)
        keys_acc[rows, :] += matmul(jnp.concatenate(slopes, axis=1), stacked)

    if not masked:
        pl.loop(0, keys_ref.shape[0] // count)(lambda n: add(n, n))
    elif old:
        tiles = keys_ref.shape[0] // count
        pl.loop(meta[1 + step], 0)(lambda n: add(lax.bitwise_xor(n + tiles, meta[0]), n))
    else:
        pl.loop(jnp.maximum(meta[1 + step], 0), tile + 1)(
            lambda n: add(lax.bitwise_xor(n, meta[0]), n)
        )
    if old:
        grad_query_ref[...] = query_acc[...]
    else:
        grad_query_ref[...] = low(query_acc[...].T)

    @pl.when(step == pl.num_programs(0) - 1)
    def _():
        grad_keys_ref[...] = keys_acc[...].astype(grad_keys_ref.dtype)
        grad_values_ref[...] = values_acc[...].astype(grad_values_ref.dtype)


def tiled(width, column):
    return pl.BlockSpec((TILE, width), lambda t, meta: (t, column))


def tiled_t(height):
    return pl.BlockSpec((height, TILE), lambda t, meta: (0, t))


def entire(rows, width, column):
    return pl.BlockSpec((rows, width), lambda t, meta: (0, column))


def attend(meta, lower, query, keys, values, width, before=None):
    rows = query[0].shape[0]
    count = keys[0].shape[0]
    heads = width // HDIM
    masked = before is not None
    inputs = [query[0], keys[0], values[0]]
    specs = [
        tiled(width, query[1]),
        entire(count, width, keys[1]),
        entire(count, width, values[1]),
    ]
    if masked:
        inputs = [lower] + inputs + [before[0], before[0]]
        specs = [tiled_t(1)] + specs
        specs += [entire(before[0].shape[0], width, 0), entire(before[0].shape[0], width, 1)]
    pairs = rows * count * width
    return pl.pallas_call(
        partial(attend_kernel, heads, masked),
        grid_spec=pltpu.PrefetchScalarGridSpec(
            num_scalar_prefetch=1,
            grid=(rows // TILE,),
            in_specs=specs,
            out_specs=[tiled(width, 0), tiled_t(width), tiled_t(heads)],
            scratch_shapes=[pltpu.VMEM((width, TILE), jnp.float32)],
        ),
        out_shape=[
            jax.ShapeDtypeStruct((rows, width), jnp.bfloat16),
            jax.ShapeDtypeStruct((width, rows), jnp.float32),
            jax.ShapeDtypeStruct((heads, rows), jnp.float32),
        ],
        compiler_params=pltpu.CompilerParams(vmem_limit_bytes=VMEM),
        cost_estimate=pl.CostEstimate(
            flops=8 * pairs, bytes_accessed=2 * (rows + count) * width * 2, transcendentals=0
        ),
    )(meta, *inputs)


def attend_back(meta, lower, query, grad, mixed_t, lse, keys, values, width, kind, start=None):
    rows = query[0].shape[0]
    count = keys[0].shape[0]
    heads = width // HDIM
    masked = kind != "cross"
    old = kind == "old"
    inputs = [query[0], grad, mixed_t, lse, keys[0], values[0]]
    specs = [
        tiled(width, query[1]),
        tiled(width, 0),
        tiled_t(width),
        tiled_t(heads),
        entire(count, width, keys[1]),
        entire(count, width, values[1]),
    ]
    if start is not None:
        inputs, specs = [start] + inputs, [tiled_t(width)] + specs
    if masked:
        inputs, specs = [lower] + inputs, [tiled_t(1)] + specs
    kept = jnp.bfloat16 if masked else jnp.float32
    pairs = rows * count * width
    return pl.pallas_call(
        partial(attend_back_kernel, heads, masked, old),
        grid_spec=pltpu.PrefetchScalarGridSpec(
            num_scalar_prefetch=1,
            grid=(rows // TILE,),
            in_specs=specs,
            out_specs=[
                tiled_t(width) if old else tiled(width, 0),
                entire(count, width, 0),
                entire(count, width, 0),
            ],
            scratch_shapes=[
                pltpu.VMEM((count, width), jnp.float32),
                pltpu.VMEM((count, width), jnp.float32),
                pltpu.VMEM((width, TILE), jnp.float32),
            ],
        ),
        out_shape=[
            jax.ShapeDtypeStruct((width, rows), jnp.float32)
            if old
            else jax.ShapeDtypeStruct((rows, width), jnp.bfloat16),
            jax.ShapeDtypeStruct((count, width), kept),
            jax.ShapeDtypeStruct((count, width), kept),
        ],
        compiler_params=pltpu.CompilerParams(vmem_limit_bytes=VMEM),
        cost_estimate=pl.CostEstimate(
            flops=20 * pairs, bytes_accessed=4 * (rows + count) * width * 2, transcendentals=0
        ),
    )(meta, *inputs)


def layer_norm(value, gain, shift_by):
    centre = value - jnp.mean(value, axis=-1, keepdims=True)
    rstd = lax.rsqrt(jnp.mean(centre * centre, axis=-1, keepdims=True) + EPSILON)
    normed = centre * rstd
    return (normed * gain + shift_by, normed, rstd)


def norm_back(grad_out, normed, rstd, gain):
    scaled = grad_out * gain
    inner = scaled - jnp.mean(scaled, axis=-1, keepdims=True)
    inner = inner - normed * jnp.mean(scaled * normed, axis=-1, keepdims=True)
    return (rstd * inner, jnp.sum(grad_out * normed, axis=0), jnp.sum(grad_out, axis=0))


def gelu_and_slope(value):
    phi = 0.5 * (1.0 + lax.erf(value * 0.7071067811865476))
    bell = jnp.exp(-0.5 * value * value) * 0.3989422804014327
    return value * phi, phi + value * bell


def column_sum(value):
    return jnp.sum(wide(value), axis=0)


def scatter_rows(make, rows):
    count = lax.axis_size("tp")
    half = rows // 2
    far = low(make(slice(half, rows))).reshape(count // 2, rows // count, -1)
    near = low(make(slice(0, half))).reshape(count // 2, rows // count, -1)
    terms = [near[m] for m in range(count // 2)] + [far[m] for m in range(count // 2)]
    return scatter_tree(terms, "tp")


def gather_rows(piece):
    return jnp.concatenate(gather_tree(piece, "tp"), axis=0)


def scatter_weight(grad):
    shards, ctxs = lax.axis_size("shard"), lax.axis_size("ctx")
    blocks = low(grad).reshape(shards, ctxs, -1, grad.shape[1])
    mine = lax.axis_index("ctx")
    terms = [
        lax.dynamic_index_in_dim(blocks, mine ^ m, axis=1, keepdims=False) for m in range(ctxs)
    ]
    total = scatter_direct(terms, "ctx")
    return scatter_direct([total[m] for m in range(shards)], "shard")


def scatter_weight_t(grad):
    shards, ctxs = lax.axis_size("shard"), lax.axis_size("ctx")
    rows, columns = grad.shape
    size = columns // (shards * ctxs)
    mine = lax.axis_index("ctx")
    kept = low(grad)
    blocks = [kept[:, s * size : (s + 1) * size] for s in range(shards * ctxs)]
    bit = 1
    while bit < ctxs:
        odd = (mine & bit) != 0
        blocks = [jnp.where(odd, blocks[s ^ bit], blocks[s]) for s in range(shards * ctxs)]
        bit *= 2
    terms = [jnp.stack([blocks[s * ctxs + m] for s in range(shards)]) for m in range(ctxs)]
    total = scatter_direct(terms, "ctx")
    return scatter_direct([total[m] for m in range(shards)], "shard")


def per_device(
    inputs,
    encoded,
    doc_lengths,
    cotangent,
    query_weight,
    key_weight,
    value_weight,
    out_weight,
    memory_query,
    memory_key,
    memory_value,
    memory_out,
    up_weight,
    down_weight,
    query_bias,
    value_bias,
    memory_qbias,
    memory_vbias,
    up_bias,
    out_bias,
    memory_obias,
    down_bias,
    gain_self,
    shift_self,
    gain_memory,
    shift_memory,
    gain_dense,
    shift_dense,
):
    tps = lax.axis_size("tp")
    tp_index = lax.axis_index("tp")
    share_rows = inputs.shape[1]
    rows = share_rows * tps
    width = query_weight.shape[1]
    base = lax.axis_index("ctx") * rows

    def gather_in(weight):
        return jnp.concatenate(gather_direct(weight, "shard"), axis=0)

    def gather_out(weight):
        return jnp.concatenate(gather_direct(weight, "shard"), axis=1)

    share = relative(inputs[0], 1, "shard")
    old_share = relative(shift(inputs[0], "ctx", 1), 1, "shard")
    inputs_rows = gather_rows(share)
    old_rows = gather_rows(old_share)
    qkv_full = gather_in(jnp.concatenate([query_weight, key_weight, value_weight], axis=1))
    out_full = gather_out(out_weight)
    states = relative(relative(encoded[0], 1, "shard"), 0, "tp")
    mkv_full = gather_in(jnp.concatenate([memory_key, memory_value], axis=1))
    mquery_full = gather_in(memory_query)
    mout_full = gather_out(memory_out)
    up_full = gather_in(up_weight)
    down_full = gather_out(down_weight)
    vectors = relative(
        jnp.stack(
            [
                out_bias,
                memory_obias,
                down_bias,
                gain_self,
                shift_self,
                gain_memory,
                shift_memory,
                gain_dense,
                shift_dense,
            ]
        ),
        1,
        "shard",
    )
    (
        out_bias,
        memory_obias,
        down_bias,
        gain_self,
        shift_self,
        gain_memory,
        shift_memory,
        gain_dense,
        shift_dense,
    ) = [vectors[i] for i in range(9)]
    upstream = wide(relative(cotangent[0], 1, "shard"))

    ends = jnp.cumsum(doc_lengths[0], dtype=jnp.int32)
    local = jnp.arange(rows, dtype=jnp.int32)
    place = base + (local // share_rows ^ tp_index) * share_rows + local % share_rows
    opens = jnp.max(jnp.where(place[:, None] >= ends[None, :], ends[None, :], 0), axis=1)
    lower = jnp.maximum(opens, place - (W - 1)) - base
    least = lower.reshape(-1, TILE)[:, 0] // TILE
    meta = jnp.concatenate([tp_index[None].astype(jnp.int32), least])
    lower = lower[None, :]

    zeros = jnp.zeros_like(query_bias)
    qkv = low(
        (matmul(inputs_rows, qkv_full) + jnp.concatenate([query_bias, zeros, value_bias]))
        * jnp.concatenate([zeros + 0.125, zeros + 1.0, zeros + 1.0])
    )
    old_kv = low(
        matmul(old_rows, qkv_full[:, width:]) + jnp.concatenate([zeros, value_bias])
    )
    self_mixed, self_mixed_t, self_lse = attend(
        meta, lower, (qkv, 0), (qkv, 1), (qkv, 2), width, (old_kv, None)
    )

    mkv_own = low(matmul(states, mkv_full) + jnp.concatenate([zeros, memory_vbias]))
    mkv = jnp.concatenate(gather_direct(mkv_own, "ctx"), axis=0)

    still = jnp.zeros((1,), jnp.int32)
    step_rows = share_rows // CHAINS
    chains = range(CHAINS)

    def chain_rows(array, c):
        if CHAINS == 1:
            return array
        split = array.reshape(tps, CHAINS, step_rows, array.shape[1])
        return split[:, c].reshape(tps * step_rows, array.shape[1])

    def own(array, c):
        return array[c * step_rows : (c + 1) * step_rows]

    count = tps * step_rows
    kept = []
    for c in chains:
        mixed = chain_rows(self_mixed, c)
        attn_share = scatter_rows(lambda s: matmul(mixed[s], out_full), count)
        first, normed_one, rstd_one = layer_norm(
            wide(own(share, c)) + attn_share + out_bias, gain_self, shift_self
        )
        first_rows = gather_rows(low(first))
        mquery = low((matmul(first_rows, mquery_full) + memory_qbias) * 0.125)
        cross_mixed, cross_mixed_t, cross_lse = attend(
            still, None, (mquery, 0), (mkv, 0), (mkv, 1), width
        )
        cross_share = scatter_rows(lambda s: matmul(cross_mixed[s], mout_full), count)
        second, normed_two, rstd_two = layer_norm(
            first + cross_share + memory_obias, gain_memory, shift_memory
        )
        second_rows = gather_rows(low(second))
        act, slope = gelu_and_slope(matmul(second_rows, up_full) + up_bias)
        act_low, slope_low = low(act), low(slope)
        dense_share = scatter_rows(lambda s: matmul(act_low[s], down_full), count)
        result, normed_three, rstd_three = layer_norm(
            second + dense_share + down_bias, gain_dense, shift_dense
        )
        grad_three, gain_dense_grad, shift_dense_grad = norm_back(
            own(upstream, c), normed_three, rstd_three, gain_dense
        )
        dense_low = low(grad_three)
        dense_rows = gather_rows(dense_low)
        hidden_low = low(contract("rd,fd->rf", dense_rows, down_full) * wide(slope_low))
        second_share = scatter_rows(
            lambda s: contract("rf,df->rd", hidden_low[s], up_full), count
        )
        grad_two, gain_memory_grad, shift_memory_grad = norm_back(
            grad_three + second_share, normed_two, rstd_two, gain_memory
        )
        cross_low = low(grad_two)
        cross_rows = gather_rows(cross_low)
        grad_cross_mixed = low(contract("rd,kd->rk", cross_rows, mout_full))
        mquery_back, mkeys_back, mvalues_back = attend_back(
            still,
            None,
            (mquery, 0),
            grad_cross_mixed,
            cross_mixed_t,
            cross_lse,
            (mkv, 0),
            (mkv, 1),
            width,
            "cross",
        )
        mquery_pre = mquery_back * 0.125
        first_share = scatter_rows(
            lambda s: contract("rk,dk->rd", mquery_pre[s], mquery_full), count
        )
        grad_one, gain_self_grad, shift_self_grad = norm_back(
            grad_two + first_share, normed_one, rstd_one, gain_self
        )
        self_low = low(grad_one)
        self_rows = gather_rows(self_low)
        grad_self = low(contract("rd,kd->rk", self_rows, out_full))
        kept.append(
            dict(
                result=low(result),
                grad_one=grad_one,
                grad_self=grad_self,
                mkeys=mkeys_back,
                mvalues=mvalues_back,
                out=contract("rk,rd->kd", mixed, self_rows),
                mquery=contract("rd,rk->dk", first_rows, mquery_pre),
                mout=contract("rk,rd->kd", cross_mixed, cross_rows),
                up=contract("rd,rf->df", second_rows, hidden_low),
                down=contract("rf,rd->fd", act_low, dense_rows),
                mquery_bias=column_sum(mquery_pre),
                up_bias=column_sum(hidden_low),
                early=jnp.stack(
                    [
                        column_sum(cross_low),
                        column_sum(dense_low),
                        gain_memory_grad,
                        shift_memory_grad,
                        gain_dense_grad,
                        shift_dense_grad,
                    ]
                ),
                late=jnp.stack([column_sum(self_low), gain_self_grad, shift_self_grad]),
            )
        )

    def total(name):
        value = kept[0][name]
        for other in kept[1:]:
            value = value + other[name]
        return value

    def joined(name):
        if CHAINS == 1:
            return kept[0][name]
        return jnp.concatenate([k[name] for k in kept], axis=0)

    def rows_joined(name):
        if CHAINS == 1:
            return kept[0][name]
        return jnp.stack([k[name].reshape(tps, step_rows, -1) for k in kept], axis=1).reshape(
            rows, -1
        )

    down_weight_grad = scatter_weight_t(total("down"))
    up_weight_grad = scatter_weight(total("up"))
    memory_out_grad = scatter_weight_t(total("mout"))
    memory_query_grad = scatter_weight(total("mquery"))

    own_states = states.shape[0]
    mkv_back = jnp.concatenate([total("mkeys"), total("mvalues")], axis=1)
    mkv_low = low(
        scatter_direct(
            [
                mkv_back[m * own_states : (m + 1) * own_states]
                for m in range(lax.axis_size("ctx"))
            ],
            "ctx",
        )
    )
    mkv_grad = scatter_weight(contract("ed,ek->dk", states, mkv_low))
    memory_vbias_grad = column_sum(mkv_low[:, width:])
    encoded_grad = scatter_rows(
        lambda s: contract("ek,dk->ed", mkv_low[s], mkv_full), own_states
    )

    out_weight_grad = scatter_weight_t(total("out"))
    grad_self = rows_joined("grad_self")
    query_start, old_keys, old_values = attend_back(
        meta,
        lower,
        (qkv, 0),
        grad_self,
        self_mixed_t,
        self_lse,
        (old_kv, 0),
        (old_kv, 1),
        width,
        "old",
    )
    old_back = jnp.concatenate([old_keys, old_values], axis=1)
    back = shift(old_back, "ctx", -1)
    query_back, keys_back, values_back = attend_back(
        meta,
        lower,
        (qkv, 0),
        grad_self,
        self_mixed_t,
        self_lse,
        (qkv, 1),
        (qkv, 2),
        width,
        "own",
        query_start,
    )
    query_pre = query_back * 0.125
    kv_back = jnp.concatenate([keys_back, values_back], axis=1)
    kv_grad = contract("rd,rk->dk", inputs_rows, kv_back) + contract(
        "rd,rk->dk", old_rows, old_back
    )
    kv_weight_grad = scatter_weight(kv_grad)
    query_weight_grad = scatter_weight(contract("rd,rk->dk", inputs_rows, query_pre))
    value_bias_grad = column_sum(values_back) + column_sum(old_values)
    kv_all = low(wide(kv_back) + wide(back))

    def inputs_term(s):
        term = contract("rk,dk->rd", query_pre[s], qkv_full[:, :width])
        return term + contract("rk,dk->rd", kv_all[s], qkv_full[:, width:])

    inputs_grad = joined("grad_one") + scatter_rows(inputs_term, rows)

    early = relative(total("early"), 1, "shard")
    late = relative(total("late"), 1, "shard")
    early = all_sum(early, ("tp", "ctx", "shard"))
    late = all_sum(late, ("tp", "ctx", "shard"))
    early_split = all_sum(
        jnp.concatenate([total("mquery_bias"), memory_vbias_grad, total("up_bias")])[None],
        ("ctx", "shard"),
    )[0]
    late_split = all_sum(
        jnp.concatenate([column_sum(query_pre), value_bias_grad])[None], ("ctx", "shard")
    )[0]
    return (
        relative(joined("result"), 1, "shard")[None],
        relative(inputs_grad, 1, "shard")[None],
        relative(encoded_grad, 1, "shard")[None],
        query_weight_grad,
        kv_weight_grad[:, :width],
        kv_weight_grad[:, width:],
        out_weight_grad,
        memory_query_grad,
        mkv_grad[:, :width],
        mkv_grad[:, width:],
        memory_out_grad,
        up_weight_grad,
        down_weight_grad,
        late_split[:width],
        late_split[width:],
        early_split[:width],
        early_split[width : 2 * width],
        early_split[2 * width :],
        late[0],
        early[0],
        early[1],
        late[1],
        late[2],
        early[2],
        early[3],
        early[4],
        early[5],
    )


def solution(mesh):
    placed = (
        P("shard", ("ctx", "tp"), None),
        P("shard", "ctx", None),
        P("shard", None),
        P("shard", ("ctx", "tp"), None),
        P("shard", "tp"),
        P("shard", "tp"),
        P("shard", "tp"),
        P("tp", "shard"),
        P("shard", "tp"),
        P("shard", "tp"),
        P("shard", "tp"),
        P("tp", "shard"),
        P("shard", "tp"),
        P("tp", "shard"),
        P("tp"),
        P("tp"),
        P("tp"),
        P("tp"),
        P("tp"),
        P(),
        P(),
        P(),
        P(),
        P(),
        P(),
        P(),
        P(),
        P(),
    )
    return jax.shard_map(
        per_device,
        mesh=mesh,
        in_specs=placed,
        out_specs=(
            P("shard", ("ctx", "tp"), None),
            P("shard", ("ctx", "tp"), None),
            P("shard", ("ctx", "tp"), None),
            P(("shard", "ctx"), "tp"),
            P(("shard", "ctx"), "tp"),
            P(("shard", "ctx"), "tp"),
            P("tp", ("shard", "ctx")),
            P(("shard", "ctx"), "tp"),
            P(("shard", "ctx"), "tp"),
            P(("shard", "ctx"), "tp"),
            P("tp", ("shard", "ctx")),
            P(("shard", "ctx"), "tp"),
            P("tp", ("shard", "ctx")),
            P("tp"),
            P("tp"),
            P("tp"),
            P("tp"),
            P("tp"),
            P(),
            P(),
            P(),
            P(),
            P(),
            P(),
            P(),
            P(),
            P(),
        ),
        check_vma=False,
    )
```

time: 1500 us -> 662 us (0.44)
  waiting for transfers between devices: 922 us -> 274 us
  blocking collectives: 193 us -> 0 us
  starting transfers between devices: 10.9 us -> 167 us
  matrix products: 215 us -> 76.6 us
  Pallas kernels: 0 us -> 68.7 us
  local copies, waits for them, and re-layouts: 60.4 us -> 22 us
  other arithmetic: 62.9 us -> 44.8 us
    reduce_scatter x19 -> x0, waiting for transfers between devices: 782 us -> none  [the longest x6 263 us: reduce_rows(): lax.psum_scatter(term(jnp.int32(0), share_rows * lax.axis_size('tp')), 't...]
    ppermute x4 -> x115, waiting for transfers between devices: 36.2 us -> 274 us  [the longest x113 270 us: swap(): lax.ppermute(array, axis, [(i, i ^ bit) for i in range(lax.axis_size(axis...]
    ppermute x4 -> x115, starting transfers between devices: 9.14 us -> 167 us  [the longest x113 162 us: swap(): lax.ppermute(array, axis, [(i, i ^ bit) for i in range(lax.axis_size(axis...]
    all_gather x8 -> x0, blocking collectives: 131 us -> none  [the longest x1 17.6 us: per_device(): lax.all_gather(query_weight, 'shard', axis=0, tiled=True)]
    all_gather x9 -> x0, waiting for transfers between devices: 101 us -> none  [the longest x6 68.6 us: gather_rows(): return lax.all_gather(piece, 'tp', axis=0, tiled=True)]
    dot_general x40 -> x22, matrix products: 128 us -> 38.9 us  [contract(): return jnp.einsum(form, left, right, preferred_element_type=jnp.float32)]
    pallas_call x0 -> x5, Pallas kernels: none -> 68.7 us  [the longest x3 41.9 us: attend_back(): pl.pallas_call(partial(attend_back_kernel, heads, masked, old), grid_spec...]
    psum x2 -> x0, blocking collectives: 62.7 us -> none  [the longest x1 40.5 us: per_device(): lax.psum((out_bias_grad, memory_obias_grad, down_bias_grad, gain_self_gra...]
  transfers between devices with their start and end apart: 32 -> 115, of which waited for: 24 -> 42; matrix products, arithmetic and copies ran while one was open for 12% -> 14% of each run, Pallas kernels for 0% -> 2%
where the time goes in v1:
time: 662 us; the launch traced here: 657 us
  waiting for transfers between devices  274 us (41%)
  starting transfers between devices  167 us (25%)
  matrix products  76.6 us (12%)
  Pallas kernels  68.7 us (10%)
  other arithmetic  44.8 us (7%)
  local copies, waits for them, and re-layouts  22 us (3%)
    ppermute x113, waiting for transfers between devices, swap(): lax.ppermute(array, axis, [(i, i ^ bit) for i in range(lax.axis_size(axis...  270 us
    ppermute x113, starting transfers between devices, swap(): lax.ppermute(array, axis, [(i, i ^ bit) for i in range(lax.axis_size(axis...  162 us
    pallas_call x3, Pallas kernels, attend_back(): pl.pallas_call(partial(attend_back_kernel, heads, masked, old), grid_spec...  41.9 us
    dot_general x22, matrix products, contract(): return jnp.einsum(form, left, right, preferred_element_type=jnp.float32)  38.9 us
    dot_general x11, matrix products, matmul(): return jnp.dot(left, right, preferred_element_type=jnp.float32)  37.7 us
    pallas_call x2, Pallas kernels, attend(): pl.pallas_call(partial(attend_kernel, heads, masked), grid_spec=pltpu.Pre...  26.8 us
  transfers between devices with their start and end apart: 115, of which 42 were waited for; matrix products, arithmetic and copies ran while one was open for 14% of the time, Pallas kernels for 2%

profile of v1, /device:TPU:0, one launch (start us, length us, event | category | flops | bytes accessed | tf_op | source)
XLA Modules:
  0.0 656.6 jit_solution(11954449581026702201)
XLA Ops:
  23.7 5.0 collective-permute-done.12
  37.8 15.8 %collective-permute-done.4 = bf16[256,768]{1,0:T(8,128)(2,1)S(1)} collective-permute-done((bf16[256,768]{1,0:T(8,128)(2,1)S(1)}, bf16[256,768]{1,0:T(8,128)(2,1)S(1)}, u32[]{:S(2)}, u32[]{:S(2)}) %collective-permute-start.4) | collective-permute-done | bytes 393248 | tf_op jit(solution)/shard_map/ppermute | solution.py:38
  55.0 6.9 %collective-permute-start.23 = (bf16[256,512]{1,0:T(8,128)(2,1)}, bf16[256,512]{1,0:T(8,128)(2,1)}, u32[]{:S(2)}, u32[]{:S(2)}) collective-permute-start(bf16[256,512]{1,0:T(8,128)(2,1)} %copy-done.94), channel_id=1, source_target_pairs={{0,16},{8,24},{16,0},{24,8},{1,17},{9,25},{17,1},{25,9},{2,18},{10... | collective-permute-start | bytes 786440 | tf_op jit(solution)/shard_map/ppermute | solution.py:38
  72.1 15.4 %shard_map.475 = (bf16[1024,256]{1,0:T(8,128)(2,1)}, f32[256,1024]{1,0:T(8,128)}, f32[4,1024]{1,0:T(4,128)}) custom-call(s32[5]{0:T(128)} %pad_add_fusion.meta, s32[1,1024]{1,0:T(1,128)} %fusion.82.refs_0_, bf16[1024,768]{1,0:T(8,128)(2,1)} %multiply_convert_fusion.2.refs_1_.refs_2_.refs_3_.refs_6_.refs_7_, ...), custom_call_target="tpu_custom_call" | custom-call | flops 2147483648 | bytes 2097152 | tf_op jit(solution)/shard_map/pallas_call | solution.py:269
  97.0 8.4 %collective-permute-done.15 = bf16[256,1024]{1,0:T(8,128)(2,1)} collective-permute-done((bf16[256,1024]{1,0:T(8,128)(2,1)S(1)}, bf16[256,1024]{1,0:T(8,128)(2,1)}, u32[]{:S(2)}, u32[]{:S(2)}) %collective-permute-start.15) | collective-permute-done | bytes 524320 | tf_op jit(solution)/shard_map/ppermute | solution.py:38
  115.0 7.1 %collective-permute-done.21 = bf16[256,256]{1,0:T(8,128)(2,1)S(1)} collective-permute-done((bf16[256,256]{1,0:T(8,128)(2,1)}, bf16[256,256]{1,0:T(8,128)(2,1)S(1)}, u32[]{:S(2)}, u32[]{:S(2)}) %collective-permute-start.21) | collective-permute-done | bytes 131104 | tf_op jit(solution)/shard_map/ppermute | solution.py:38
  122.1 7.9 %collective-permute-start.26 = (bf16[256,256]{1,0:T(8,128)(2,1)S(1)}, bf16[256,256]{1,0:T(8,128)(2,1)S(1)}, u32[]{:S(2)}, u32[]{:S(2)}) collective-permute-start(bf16[256,256]{1,0:T(8,128)(2,1)S(1)} %copy-done.87), channel_id=1, source_target_pairs={{0,8},{8,0},{16,24},{24,16},{1,9},{9,1},{17,25},{25,17},{2,10},{10... | collective-permute-start | bytes 393224 | tf_op jit(solution)/shard_map/ppermute | solution.py:38
  134.6 7.7 %collective-permute-start.25 = (bf16[256,512]{1,0:T(8,128)(2,1)S(1)}, bf16[256,512]{1,0:T(8,128)(2,1)S(1)}, u32[]{:S(2)}, u32[]{:S(2)}) collective-permute-start(bf16[256,512]{1,0:T(8,128)(2,1)S(1)} %fusion.10), channel_id=1, source_target_pairs={{0,4},{4,0},{1,5},{5,1},{2,6},{6,2},{3,7},{7,3},{8,12},{12,8},{9,1... | collective-permute-start | bytes 786440 | tf_op jit(solution)/shard_map/ppermute | solution.py:38
  142.4 6.6 %collective-permute-done.25 = bf16[256,512]{1,0:T(8,128)(2,1)S(1)} collective-permute-done((bf16[256,512]{1,0:T(8,128)(2,1)S(1)}, bf16[256,512]{1,0:T(8,128)(2,1)S(1)}, u32[]{:S(2)}, u32[]{:S(2)}) %collective-permute-start.25) | collective-permute-done | bytes 262176 | tf_op jit(solution)/shard_map/ppermute | solution.py:38
  151.4 11.4 %shard_map.476 = (bf16[1024,256]{1,0:T(8,128)(2,1)}, f32[256,1024]{1,0:T(8,128)}, f32[4,1024]{1,0:T(4,128)}) custom-call(s32[1]{0:T(128)} %constant.138.clone.1.meta, bf16[1024,256]{1,0:T(8,128)(2,1)} %fusion.9.refs_0_, bf16[512,512]{1,0:T(8,128)(2,1)} %pad_maximum_fusion.15.refs_1_.refs_2_.refs_4_.refs_5_, ...), custom_call_target="tpu_custom_call" | custom-call | flops 1073741824 | bytes 1572864 | tf_op jit(solution)/shard_map/pallas_call | solution.py:269
  171.5 9.0 %collective-permute-done.31 = bf16[256,1024]{1,0:T(8,128)(2,1)S(1)} collective-permute-done((bf16[256,1024]{1,0:T(8,128)(2,1)S(1)}, bf16[256,1024]{1,0:T(8,128)(2,1)S(1)}, u32[]{:S(2)}, u32[]{:S(2)}) %collective-permute-start.31) | collective-permute-done | bytes 524320 | tf_op jit(solution)/shard_map/ppermute | solution.py:38
  183.1 9.5 %collective-permute-done.35 = bf16[256,1024]{1,0:T(8,128)(2,1)S(1)} collective-permute-done((bf16[256,1024]{1,0:T(8,128)(2,1)S(1)}, bf16[256,1024]{1,0:T(8,128)(2,1)S(1)}, u32[]{:S(2)}, u32[]{:S(2)}) %collective-permute-start.35) | collective-permute-done | bytes 524320 | tf_op jit(solution)/shard_map/ppermute | solution.py:38
  192.6 13.5 %collective-permute-done.36 = bf16[256,1024]{1,0:T(8,128)(2,1)S(1)} collective-permute-done((bf16[256,1024]{1,0:T(8,128)(2,1)S(1)}, bf16[256,1024]{1,0:T(8,128)(2,1)S(1)}, u32[]{:S(2)}, u32[]{:S(2)}) %collective-permute-start.36) | collective-permute-done | bytes 524320 | tf_op jit(solution)/shard_map/ppermute | solution.py:38
  209.5 5.0 collective-permute-done.38
  214.5 36.5 %collective-permute-done.39 = bf16[1024,256]{1,0:T(8,128)(2,1)S(1)} collective-permute-done((bf16[1024,256]{1,0:T(8,128)(2,1)S(1)}, bf16[1024,256]{1,0:T(8,128)(2,1)S(1)}, u32[]{:S(2)}, u32[]{:S(2)}) %collective-permute-start.39) | collective-permute-done | bytes 524320 | tf_op jit(solution)/shard_map/ppermute | solution.py:38
  251.3 20.8 %multiply_convert_fusion.1 = (bf16[1024,1024]{1,0:T(8,128)(2,1)S(1)}, f32[1024,1024]{1,0:T(8,128)}) fusion(f32[1024]{0:T(1024)S(1)} %copy-done.135, bf16[1024,1024]{1,0:T(8,128)(2,1)S(1)} %constant_dynamic-update-slice_fusion.17, bf16[256,1024]{1,0:T(8,128)(2,1)S(1)} %collective-permute-done.34, bf16[256,1024]{1,0:T(8,128)(2,1)S(1)} %collective-permute-done.33, ...), kind=kOutput, calls=%fused_computation.8 | convolution fusion | flops 2162163712 | bytes 10489856 | tf_op jit(solution)/shard_map/dot_general | solution.py:22
  277.3 12.3 %collective-permute-done.43 = bf16[256,1024]{1,0:T(8,128)(2,1)S(1)} collective-permute-done((bf16[256,1024]{1,0:T(8,128)(2,1)S(1)}, bf16[256,1024]{1,0:T(8,128)(2,1)S(1)}, u32[]{:S(2)}, u32[]{:S(2)}) %collective-permute-start.43) | collective-permute-done | bytes 524320 | tf_op jit(solution)/shard_map/ppermute | solution.py:38
  294.9 11.9 %collective-permute-done.45 = bf16[256,1024]{1,0:T(8,128)(2,1)} collective-permute-done((bf16[256,1024]{1,0:T(8,128)(2,1)}, bf16[256,1024]{1,0:T(8,128)(2,1)}, u32[]{:S(2)}, u32[]{:S(2)}) %collective-permute-start.45) | collective-permute-done | bytes 524320 | tf_op jit(solution)/shard_map/ppermute | solution.py:38
  309.1 7.9 %convert_reduce_fusion = (f32[1024]{0:T(1024)}, bf16[1024,1024]{1,0:T(8,128)(2,1)S(1)}) fusion(f32[1024,1024]{1,0:T(8,128)} %get-tuple-element.220, f32[1024]{0:T(1024)} %param.46, bf16[1024,1024]{1,0:T(8,128)(2,1)} %copy-done.79, bf16[256,1024]{1,0:T(8,128)(2,1)} %collective-permute-done.46, bf16[256,1024]{1,0:T(8,128)(2,1)} %collective-permute-done.45, ...), kind=kOutput, calls=%fused_computation.6 | convolution fusion | flops 2171599872 | bytes 10493952 | tf_op jit(solution)/shard_map/rd,fd->rf/dot_general | solution.py:26
  332.4 16.8 %collective-permute-done.95 = bf16[4,1024,128]{2,1,0:T(8,128)(2,1)S(1)} collective-permute-done((bf16[4,1024,128]{2,1,0:T(8,128)(2,1)S(1)}, bf16[4,1024,128]{2,1,0:T(8,128)(2,1)S(1)}, u32[]{:S(2)}, u32[]{:S(2)}) %collective-permute-start.95) | collective-permute-done | bytes 1048608 | tf_op jit(solution)/shard_map/ppermute | solution.py:38
  357.0 10.4 %collective-permute-start.96 = (bf16[1024,128]{1,0:T(8,128)(2,1)S(1)}, bf16[1024,128]{1,0:T(8,128)(2,1)S(1)}, u32[]{:S(2)}, u32[]{:S(2)}) collective-permute-start(bf16[1024,128]{1,0:T(8,128)(2,1)S(1)} %get-tuple-element.105), channel_id=1, source_target_pairs={{0,8},{8,0},{16,24},{24,16},{1,9},{9,1},{17,25},{25,17},{2,10},{10... | collective-permute-start | bytes 786440 | tf_op jit(solution)/shard_map/ppermute | solution.py:38
  377.9 9.9 %collective-permute-start.113 = (f32[6,1024]{1,0:T(8,128)S(1)}, f32[6,1024]{1,0:T(8,128)S(1)}, u32[]{:S(2)}, u32[]{:S(2)}) collective-permute-start(f32[6,1024]{1,0:T(8,128)S(1)} %add.621), channel_id=1, source_target_pairs={{0,8},{8,0},{16,24},{24,16},{1,9},{9,1},{17,25},{25,17},{2,10},{10... | collective-permute-start | bytes 73736 | tf_op jit(solution)/shard_map/ppermute | solution.py:38
  407.0 10.4 %collective-permute-done.93 = bf16[128,1024]{1,0:T(8,128)(2,1)S(1)} collective-permute-done((bf16[128,1024]{1,0:T(8,128)(2,1)S(1)}, bf16[128,1024]{1,0:T(8,128)(2,1)S(1)}, u32[]{:S(2)}, u32[]{:S(2)}) %collective-permute-start.93) | collective-permute-done | bytes 262176 | tf_op jit(solution)/shard_map/ppermute | solution.py:38
  419.8 16.1 %shard_map.477 = (bf16[1024,256]{1,0:T(8,128)(2,1)}, f32[512,256]{1,0:T(8,128)}, f32[512,256]{1,0:T(8,128)}) custom-call(s32[1]{0:T(128)} %constant.138.clone.1.meta, bf16[1024,256]{1,0:T(8,128)(2,1)} %fusion.9.refs_0_, bf16[1024,256]{1,0:T(8,128)(2,1)} %convolution_convert_fusion.18.refs_1_, f32[256,1024]{1,0:T(8,128)} %get-tuple-element.44.refs_2_, ...), custom_call_target="tpu_custom_call" | custom-call | flops 2684354560 | bytes 3145728 | tf_op jit(solution)/shard_map/pallas_call | solution.py:311
  495.4 9.9 %collective-permute-done.55 = bf16[256,1024]{1,0:T(8,128)(2,1)S(1)} collective-permute-done((bf16[256,1024]{1,0:T(8,128)(2,1)S(1)}, bf16[256,1024]{1,0:T(8,128)(2,1)S(1)}, u32[]{:S(2)}, u32[]{:S(2)}) %collective-permute-start.55) | collective-permute-done | bytes 524320 | tf_op jit(solution)/shard_map/ppermute | solution.py:38
  513.1 11.7 %collective-permute-done.106 = f32[3,1024]{1,0:T(4,128)S(1)} collective-permute-done((f32[3,1024]{1,0:T(4,128)S(1)}, f32[3,1024]{1,0:T(4,128)S(1)}, u32[]{:S(2)}, u32[]{:S(2)}) %collective-permute-start.106) | collective-permute-done | bytes 12320 | tf_op jit(solution)/shard_map/ppermute | solution.py:38
  539.2 5.6 shard_map.478
  544.9 20.2 %shard_map.479 = (bf16[1024,256]{1,0:T(8,128)(2,1)}, bf16[1024,256]{1,0:T(8,128)(2,1)}, bf16[1024,256]{1,0:T(8,128)(2,1)}) custom-call(s32[5]{0:T(128)} %pad_add_fusion.meta, s32[1,1024]{1,0:T(1,128)} %fusion.82.refs_0_, f32[256,1024]{1,0:T(8,128)} %get-tuple-element.49.refs_1_, ...), custom_call_target="tpu_custom_call" | custom-call | flops 5368709120 | bytes 4194304 | tf_op jit(solution)/shard_map/pallas_call | solution.py:311
  568.9 4.9 collective-permute-start.99
  577.3 5.2 fusion.109
  602.0 18.4 %collective-permute-done.67 = bf16[4,128,256]{2,1,0:T(8,128)(2,1)S(1)} collective-permute-done((bf16[4,128,256]{2,1,0:T(8,128)(2,1)S(1)}, bf16[4,128,256]{2,1,0:T(8,128)(2,1)S(1)}, u32[]{:S(2)}, u32[]{:S(2)}) %collective-permute-start.67) | collective-permute-done | bytes 262176 | tf_op jit(solution)/shard_map/ppermute | solution.py:38
  642.9 6.6 %collective-permute-done.73 = bf16[128,512]{1,0:T(8,128)(2,1)S(1)} collective-permute-done((bf16[128,512]{1,0:T(8,128)(2,1)S(1)}, bf16[128,512]{1,0:T(8,128)(2,1)S(1)}, u32[]{:S(2)}, u32[]{:S(2)}) %collective-permute-start.73) | collective-permute-done | bytes 131104 | tf_op jit(solution)/shard_map/ppermute | solution.py:38
  (709 shorter events, 288.1 us)
Async XLA Ops:
  22.0 40.1 %collective-permute-start = (bf16[256,1024]{1,0:T(8,128)(2,1)S(1)}, bf16[256,1024]{1,0:T(8,128)(2,1)}, u32[]{:S(2)}, u32[]{:S(2)}) collective-permute-start(bf16[256,1024]{1,0:T(8,128)(2,1)S(1)} %pad_maximum_fusion.11), channel_id=1, source_target_pairs={{0,1},{1,0},{2,3},{3,2},{4,5},{5,4},{6,7},{7,6},{8,9},{9,8},{10,11... | collective-permute-start | bytes 1572872 | tf_op jit(solution)/shard_map/ppermute | solution.py:38
  22.0 31.6 %collective-permute-start.4 = (bf16[256,768]{1,0:T(8,128)(2,1)S(1)}, bf16[256,768]{1,0:T(8,128)(2,1)S(1)}, u32[]{:S(2)}, u32[]{:S(2)}) collective-permute-start(bf16[256,768]{1,0:T(8,128)(2,1)S(1)} %constant_dynamic-update-slice_fusion), channel_id=1, source_target_pairs={{0,16},{8,24},{16,0},{24,8},{1,17},{9,25},{17,1},{25,9},{2,18},{10... | collective-permute-start | bytes 1179656 | tf_op jit(solution)/shard_map/ppermute | solution.py:38
  28.7 26.3 %collective-permute-start.5 = (bf16[256,768]{1,0:T(8,128)(2,1)S(1)}, bf16[256,768]{1,0:T(8,128)(2,1)S(1)}, u32[]{:S(2)}, u32[]{:S(2)}) collective-permute-start(bf16[256,768]{1,0:T(8,128)(2,1)S(1)} %constant_dynamic-update-slice_fusion), channel_id=1, source_target_pairs={{0,24},{8,16},{16,8},{24,0},{1,25},{9,17},{17,9},{25,1},{2,26},{10... | collective-permute-start | bytes 1179656 | tf_op jit(solution)/shard_map/ppermute | solution.py:38
  28.7 33.7 %collective-permute-start.8 = (bf16[256,1024]{1,0:T(8,128)(2,1)}, bf16[256,1024]{1,0:T(8,128)(2,1)}, u32[]{:S(2)}, u32[]{:S(2)}) collective-permute-start(bf16[256,1024]{1,0:T(8,128)(2,1)} %pad_maximum_fusion.12), channel_id=1, source_target_pairs={{0,2},{1,3},{2,0},{3,1},{4,6},{5,7},{6,4},{7,5},{8,10},{9,11},{10,... | collective-permute-start | bytes 1572872 | tf_op jit(solution)/shard_map/ppermute | solution.py:38
  30.3 32.1 %collective-permute-start.2 = (bf16[256,1024]{1,0:T(8,128)(2,1)}, bf16[256,1024]{1,0:T(8,128)(2,1)}, u32[]{:S(2)}, u32[]{:S(2)}) collective-permute-start(bf16[256,1024]{1,0:T(8,128)(2,1)} %collective-permute-done.1), channel_id=1, source_target_pairs={{0,1},{1,0},{2,3},{3,2},{4,5},{5,4},{6,7},{7,6},{8,9},{9,8},{10,11... | collective-permute-start | bytes 1572872 | tf_op jit(solution)/shard_map/ppermute | solution.py:38
  53.6 76.5 %collective-permute-start.22 = (bf16[256,512]{1,0:T(8,128)(2,1)}, bf16[256,512]{1,0:T(8,128)(2,1)}, u32[]{:S(2)}, u32[]{:S(2)}) collective-permute-start(bf16[256,512]{1,0:T(8,128)(2,1)} %copy-done.94), channel_id=1, source_target_pairs={{0,8},{8,0},{16,24},{24,16},{1,9},{9,1},{17,25},{25,17},{2,10},{10... | collective-permute-start | bytes 786440 | tf_op jit(solution)/shard_map/ppermute | solution.py:38
  55.0 75.2 %collective-permute-start.23 = (bf16[256,512]{1,0:T(8,128)(2,1)}, bf16[256,512]{1,0:T(8,128)(2,1)}, u32[]{:S(2)}, u32[]{:S(2)}) collective-permute-start(bf16[256,512]{1,0:T(8,128)(2,1)} %copy-done.94), channel_id=1, source_target_pairs={{0,16},{8,24},{16,0},{24,8},{1,17},{9,25},{17,1},{25,9},{2,18},{10... | collective-permute-start | bytes 786440 | tf_op jit(solution)/shard_map/ppermute | solution.py:38
  62.0 48.2 %collective-permute-start.19 = (bf16[256,256]{1,0:T(8,128)(2,1)}, bf16[256,256]{1,0:T(8,128)(2,1)}, u32[]{:S(2)}, u32[]{:S(2)}) collective-permute-start(bf16[256,256]{1,0:T(8,128)(2,1)} %param.36), channel_id=1, source_target_pairs={{0,8},{8,0},{16,24},{24,16},{1,9},{9,1},{17,25},{25,17},{2,10},{10... | collective-permute-start | bytes 393224 | tf_op jit(solution)/shard_map/ppermute | solution.py:38
  107.6 24.9 %collective-permute-start.17 = (bf16[256,1024]{1,0:T(8,128)(2,1)S(1)}, bf16[256,1024]{1,0:T(8,128)(2,1)S(1)}, u32[]{:S(2)}, u32[]{:S(2)}) collective-permute-start(bf16[256,1024]{1,0:T(8,128)(2,1)S(1)} %fusion.19), channel_id=1, source_target_pairs={{0,2},{1,3},{2,0},{3,1},{4,6},{5,7},{6,4},{7,5},{8,10},{9,11},{10,... | collective-permute-start | bytes 1572872 | tf_op jit(solution)/shard_map/ppermute | solution.py:38
  167.1 25.5 %collective-permute-start.35 = (bf16[256,1024]{1,0:T(8,128)(2,1)S(1)}, bf16[256,1024]{1,0:T(8,128)(2,1)S(1)}, u32[]{:S(2)}, u32[]{:S(2)}) collective-permute-start(bf16[256,1024]{1,0:T(8,128)(2,1)S(1)} %copy-done.44), channel_id=1, source_target_pairs={{0,8},{8,0},{16,24},{24,16},{1,9},{9,1},{17,25},{25,17},{2,10},{10... | collective-permute-start | bytes 1572872 | tf_op jit(solution)/shard_map/ppermute | solution.py:38
  167.9 38.3 %collective-permute-start.36 = (bf16[256,1024]{1,0:T(8,128)(2,1)S(1)}, bf16[256,1024]{1,0:T(8,128)(2,1)S(1)}, u32[]{:S(2)}, u32[]{:S(2)}) collective-permute-start(bf16[256,1024]{1,0:T(8,128)(2,1)S(1)} %copy-done.44), channel_id=1, source_target_pairs={{0,16},{8,24},{16,0},{24,8},{1,17},{9,25},{17,1},{25,9},{2,18},{10... | collective-permute-start | bytes 1572872 | tf_op jit(solution)/shard_map/ppermute | solution.py:38
  169.9 38.9 %collective-permute-start.37 = (bf16[256,1024]{1,0:T(8,128)(2,1)S(1)}, bf16[256,1024]{1,0:T(8,128)(2,1)S(1)}, u32[]{:S(2)}, u32[]{:S(2)}) collective-permute-start(bf16[256,1024]{1,0:T(8,128)(2,1)S(1)} %copy-done.44), channel_id=1, source_target_pairs={{0,24},{8,16},{16,8},{24,0},{1,25},{9,17},{17,9},{25,1},{2,26},{10... | collective-permute-start | bytes 1572872 | tf_op jit(solution)/shard_map/ppermute | solution.py:38
  181.7 27.2 %collective-permute-start.33 = (bf16[256,1024]{1,0:T(8,128)(2,1)S(1)}, bf16[256,1024]{1,0:T(8,128)(2,1)S(1)}, u32[]{:S(2)}, u32[]{:S(2)}) collective-permute-start(bf16[256,1024]{1,0:T(8,128)(2,1)S(1)} %fusion.20), channel_id=1, source_target_pairs={{0,2},{1,3},{2,0},{3,1},{4,6},{5,7},{6,4},{7,5},{8,10},{9,11},{10,... | collective-permute-start | bytes 1572872 | tf_op jit(solution)/shard_map/ppermute | solution.py:38
  182.3 32.2 %collective-permute-start.38 = (bf16[1024,256]{1,0:T(8,128)(2,1)S(1)}, bf16[1024,256]{1,0:T(8,128)(2,1)S(1)}, u32[]{:S(2)}, u32[]{:S(2)}) collective-permute-start(bf16[1024,256]{1,0:T(8,128)(2,1)S(1)} %copy-done.45), channel_id=1, source_target_pairs={{0,8},{8,0},{16,24},{24,16},{1,9},{9,1},{17,25},{25,17},{2,10},{10... | collective-permute-start | bytes 1572872 | tf_op jit(solution)/shard_map/ppermute | solution.py:38
  192.5 58.5 %collective-permute-start.39 = (bf16[1024,256]{1,0:T(8,128)(2,1)S(1)}, bf16[1024,256]{1,0:T(8,128)(2,1)S(1)}, u32[]{:S(2)}, u32[]{:S(2)}) collective-permute-start(bf16[1024,256]{1,0:T(8,128)(2,1)S(1)} %copy-done.45), channel_id=1, source_target_pairs={{0,16},{8,24},{16,0},{24,8},{1,17},{9,25},{17,1},{25,9},{2,18},{10... | collective-permute-start | bytes 1572872 | tf_op jit(solution)/shard_map/ppermute | solution.py:38
  206.1 45.0 %collective-permute-start.40 = (bf16[1024,256]{1,0:T(8,128)(2,1)S(1)}, bf16[1024,256]{1,0:T(8,128)(2,1)S(1)}, u32[]{:S(2)}, u32[]{:S(2)}) collective-permute-start(bf16[1024,256]{1,0:T(8,128)(2,1)S(1)} %copy-done.45), channel_id=1, source_target_pairs={{0,24},{8,16},{16,8},{24,0},{1,25},{9,17},{17,9},{25,1},{2,26},{10... | collective-permute-start | bytes 1572872 | tf_op jit(solution)/shard_map/ppermute | solution.py:38
  208.8 42.4 %collective-permute-start.32 = (bf16[256,1024]{1,0:T(8,128)(2,1)S(1)}, bf16[256,1024]{1,0:T(8,128)(2,1)S(1)}, u32[]{:S(2)}, u32[]{:S(2)}) collective-permute-start(bf16[256,1024]{1,0:T(8,128)(2,1)S(1)} %fusion.20), channel_id=1, source_target_pairs={{0,1},{1,0},{2,3},{3,2},{4,5},{5,4},{6,7},{7,6},{8,9},{9,8},{10,11... | collective-permute-start | bytes 1572872 | tf_op jit(solution)/shard_map/ppermute | solution.py:38
  208.9 42.3 %collective-permute-start.34 = (bf16[256,1024]{1,0:T(8,128)(2,1)S(1)}, bf16[256,1024]{1,0:T(8,128)(2,1)S(1)}, u32[]{:S(2)}, u32[]{:S(2)}) collective-permute-start(bf16[256,1024]{1,0:T(8,128)(2,1)S(1)} %collective-permute-done.33), channel_id=1, source_target_pairs={{0,1},{1,0},{2,3},{3,2},{4,5},{5,4},{6,7},{7,6},{8,9},{9,8},{10,11... | collective-permute-start | bytes 1572872 | tf_op jit(solution)/shard_map/ppermute | solution.py:38
  322.9 26.2 %collective-permute-start.95 = (bf16[4,1024,128]{2,1,0:T(8,128)(2,1)S(1)}, bf16[4,1024,128]{2,1,0:T(8,128)(2,1)S(1)}, u32[]{:S(2)}, u32[]{:S(2)}) collective-permute-start(bf16[4,1024,128]{2,1,0:T(8,128)(2,1)S(1)} %pad_maximum_fusion.9), channel_id=1, source_target_pairs={{0,4},{4,0},{1,5},{5,1},{2,6},{6,2},{3,7},{7,3},{8,12},{12,8},{9,1... | collective-permute-start | bytes 3145736 | tf_op jit(solution)/shard_map/ppermute | solution.py:38
  326.6 24.7 %collective-permute-start.47 = (bf16[256,1024]{1,0:T(8,128)(2,1)S(1)}, bf16[256,1024]{1,0:T(8,128)(2,1)S(1)}, u32[]{:S(2)}, u32[]{:S(2)}) collective-permute-start(bf16[256,1024]{1,0:T(8,128)(2,1)S(1)} %slice.834), channel_id=1, source_target_pairs={{0,1},{1,0},{2,3},{3,2},{4,5},{5,4},{6,7},{7,6},{8,9},{9,8},{10,11... | collective-permute-start | bytes 1572872 | tf_op jit(solution)/shard_map/ppermute | solution.py:38
  326.9 24.4 %collective-permute-start.49 = (bf16[256,1024]{1,0:T(8,128)(2,1)S(1)}, bf16[256,1024]{1,0:T(8,128)(2,1)S(1)}, u32[]{:S(2)}, u32[]{:S(2)}) collective-permute-start(bf16[256,1024]{1,0:T(8,128)(2,1)S(1)} %add_convert_fusion.7), channel_id=1, source_target_pairs={{0,2},{1,3},{2,0},{3,1},{4,6},{5,7},{6,4},{7,5},{8,10},{9,11},{10,... | collective-permute-start | bytes 1572872 | tf_op jit(solution)/shard_map/ppermute | solution.py:38
  332.1 39.5 %collective-permute-start.91 = (bf16[4,128,1024]{2,1,0:T(8,128)(2,1)}, bf16[4,128,1024]{2,1,0:T(8,128)(2,1)}, u32[]{:S(2)}, u32[]{:S(2)}) collective-permute-start(bf16[4,128,1024]{2,1,0:T(8,128)(2,1)} %dynamic-slice_bitcast_fusion), channel_id=1, source_target_pairs={{0,4},{4,0},{1,5},{5,1},{2,6},{6,2},{3,7},{7,3},{8,12},{12,8},{9,1... | collective-permute-start | bytes 3145736 | tf_op jit(solution)/shard_map/ppermute | solution.py:38
  357.0 40.1 %collective-permute-start.96 = (bf16[1024,128]{1,0:T(8,128)(2,1)S(1)}, bf16[1024,128]{1,0:T(8,128)(2,1)S(1)}, u32[]{:S(2)}, u32[]{:S(2)}) collective-permute-start(bf16[1024,128]{1,0:T(8,128)(2,1)S(1)} %get-tuple-element.105), channel_id=1, source_target_pairs={{0,8},{8,0},{16,24},{24,16},{1,9},{9,1},{17,25},{25,17},{2,10},{10... | collective-permute-start | bytes 786440 | tf_op jit(solution)/shard_map/ppermute | solution.py:38
  367.4 31.0 %collective-permute-start.97 = (bf16[1024,128]{1,0:T(8,128)(2,1)S(1)}, bf16[1024,128]{1,0:T(8,128)(2,1)S(1)}, u32[]{:S(2)}, u32[]{:S(2)}) collective-permute-start(bf16[1024,128]{1,0:T(8,128)(2,1)S(1)} %get-tuple-element.107), channel_id=1, source_target_pairs={{0,16},{8,24},{16,0},{24,8},{1,17},{9,25},{17,1},{25,9},{2,18},{10... | collective-permute-start | bytes 786440 | tf_op jit(solution)/shard_map/ppermute | solution.py:38
  368.5 31.3 %collective-permute-start.98 = (bf16[1024,128]{1,0:T(8,128)(2,1)S(1)}, bf16[1024,128]{1,0:T(8,128)(2,1)S(1)}, u32[]{:S(2)}, u32[]{:S(2)}) collective-permute-start(bf16[1024,128]{1,0:T(8,128)(2,1)S(1)} %get-tuple-element.106), channel_id=1, source_target_pairs={{0,24},{8,16},{16,8},{24,0},{1,25},{9,17},{17,9},{25,1},{2,26},{10... | collective-permute-start | bytes 786440 | tf_op jit(solution)/shard_map/ppermute | solution.py:38
  438.1 57.3 %collective-permute-start.53 = (bf16[256,1024]{1,0:T(8,128)(2,1)S(1)}, bf16[256,1024]{1,0:T(8,128)(2,1)S(1)}, u32[]{:S(2)}, u32[]{:S(2)}) collective-permute-start(bf16[256,1024]{1,0:T(8,128)(2,1)S(1)} %slice.840), channel_id=1, source_target_pairs={{0,1},{1,0},{2,3},{3,2},{4,5},{5,4},{6,7},{7,6},{8,9},{9,8},{10,11... | collective-permute-start | bytes 1572872 | tf_op jit(solution)/shard_map/ppermute | solution.py:38
  438.2 44.1 %collective-permute-start.54 = (bf16[256,1024]{1,0:T(8,128)(2,1)S(1)}, bf16[256,1024]{1,0:T(8,128)(2,1)S(1)}, u32[]{:S(2)}, u32[]{:S(2)}) collective-permute-start(bf16[256,1024]{1,0:T(8,128)(2,1)S(1)} %slice.843), channel_id=1, source_target_pairs={{0,1},{1,0},{2,3},{3,2},{4,5},{5,4},{6,7},{7,6},{8,9},{9,8},{10,11... | collective-permute-start | bytes 1572872 | tf_op jit(solution)/shard_map/ppermute | solution.py:38
  575.8 56.0 %collective-permute-start.59 = (bf16[1024,512]{1,0:T(8,128)(2,1)S(1)}, bf16[1024,512]{1,0:T(8,128)(2,1)S(1)}, u32[]{:S(2)}, u32[]{:S(2)}) collective-permute-start(bf16[1024,512]{1,0:T(8,128)(2,1)S(1)} %constant_dynamic-update-slice_fusion.27), channel_id=1, source_target_pairs={{4,0},{5,1},{6,2},{7,3},{12,8},{13,9},{14,10},{15,11},{20,16},{21,... | collective-permute-start | bytes 3145736 | tf_op jit(solution)/shard_map/ppermute | solution.py:44
  585.3 46.1 %collective-permute-start.71 = (bf16[4,128,512]{2,1,0:T(8,128)(2,1)S(1)}, bf16[4,128,512]{2,1,0:T(8,128)(2,1)S(1)}, u32[]{:S(2)}, u32[]{:S(2)}) collective-permute-start(bf16[4,128,512]{2,1,0:T(8,128)(2,1)S(1)} %dynamic-slice_bitcast_fusion.2), channel_id=1, source_target_pairs={{0,4},{4,0},{1,5},{5,1},{2,6},{6,2},{3,7},{7,3},{8,12},{12,8},{9,1... | collective-permute-start | bytes 1572872 | tf_op jit(solution)/shard_map/ppermute | solution.py:38
  595.5 25.0 %collective-permute-start.67 = (bf16[4,128,256]{2,1,0:T(8,128)(2,1)S(1)}, bf16[4,128,256]{2,1,0:T(8,128)(2,1)S(1)}, u32[]{:S(2)}, u32[]{:S(2)}) collective-permute-start(bf16[4,128,256]{2,1,0:T(8,128)(2,1)S(1)} %dynamic-slice_bitcast_fusion.4), channel_id=1, source_target_pairs={{0,4},{4,0},{1,5},{5,1},{2,6},{6,2},{3,7},{7,3},{8,12},{12,8},{9,1... | collective-permute-start | bytes 786440 | tf_op jit(solution)/shard_map/ppermute | solution.py:38
  597.7 27.1 %collective-permute-start.76 = (bf16[256,128]{1,0:T(8,128)(2,1)S(1)}, bf16[256,128]{1,0:T(8,128)(2,1)S(1)}, u32[]{:S(2)}, u32[]{:S(2)}) collective-permute-start(bf16[256,128]{1,0:T(8,128)(2,1)S(1)} %get-tuple-element.174), channel_id=1, source_target_pairs={{0,8},{8,0},{16,24},{24,16},{1,9},{9,1},{17,25},{25,17},{2,10},{10... | collective-permute-start | bytes 196616 | tf_op jit(solution)/shard_map/ppermute | solution.py:38
  599.2 25.6 %collective-permute-start.77 = (bf16[256,128]{1,0:T(8,128)(2,1)S(1)}, bf16[256,128]{1,0:T(8,128)(2,1)S(1)}, u32[]{:S(2)}, u32[]{:S(2)}) collective-permute-start(bf16[256,128]{1,0:T(8,128)(2,1)S(1)} %get-tuple-element.176), channel_id=1, source_target_pairs={{0,16},{8,24},{16,0},{24,8},{1,17},{9,25},{17,1},{25,9},{2,18},{10... | collective-permute-start | bytes 196616 | tf_op jit(solution)/shard_map/ppermute | solution.py:38
  (223 other events, 3378.0 us)

commit v2 on v1

v2 whole, which is shorter than its diff:
```python
from functools import partial

import jax
import jax.numpy as jnp
from jax import lax
from jax.experimental import pallas as pl
from jax.experimental.pallas import tpu as pltpu
from jax.sharding import PartitionSpec as P

HDIM = 64
W = 1024
TILE = 256


EPSILON = 1e-05
NEGATIVE = -1e30
VMEM = 56 * 1024 * 1024


def matmul(left, right):
    return jnp.dot(left, right, preferred_element_type=jnp.float32)


def contract(form, left, right):
    return jnp.einsum(form, left, right, preferred_element_type=jnp.float32)


def low(value):
    return value.astype(jnp.bfloat16)


def wide(value):
    return value.astype(jnp.float32)


def swap(array, axis, bit):
    return lax.ppermute(array, axis, [(i, i ^ bit) for i in range(lax.axis_size(axis))])


def shift(array, axis, by):
    count = lax.axis_size(axis)
    pairs = [(i, i + by) for i in range(count) if 0 <= i + by < count]
    return lax.ppermute(array, axis, pairs)


def steps_of(*axes):
    steps = []
    for axis in axes:
        bit = lax.axis_size(axis) // 2
        while bit:
            steps.append((axis, bit))
            bit //= 2
    return steps


def after(value, *others):
    others = [other for other in others if other is not None]
    return lax.optimization_barrier((value, *others))[0] if others else value


def gather_tree(array, steps, start=None, used=None):
    for n, (axis, bit) in enumerate(steps):
        arrived = swap(after(array, start if n == 0 else None), axis, bit)
        array = jnp.concatenate([after(array, used if n == len(steps) - 1 else None), arrived])
    return array


def scatter_more(total, steps, start=None, used=None):
    for n, (axis, bit) in enumerate(reversed(steps)):
        half = total.shape[0] // 2
        arrived = swap(after(low(total[half:]), start if n == 0 else None), axis, bit)
        kept = after(total[:half], used if n == len(steps) - 1 else None)
        total = kept + wide(arrived)
    return total


def scatter_tree(make, size, steps, used=None):
    axis, bit = steps[-1]
    half = size // 2
    arrived = swap(low(make(slice(half, size))), axis, bit)
    total = after(make(slice(0, half)), used) + wide(arrived)
    return scatter_more(total, steps[:-1])


def all_sum(value, steps):
    for axis, bit in steps:
        value = value + swap(value, axis, bit)
    return value


def flat_bit(step, axes):
    axis, bit = step
    for other in axes[axes.index(axis) + 1 :]:
        bit = bit * lax.axis_size(other)
    return bit


def masks_of(axes, steps):
    masks = [0]
    for step in steps:
        masks = masks + [m | flat_bit(step, axes) for m in masks]
    return masks


def cross_over(blocks, axes):
    index = lax.axis_index(axes)
    bit = 1
    while bit < len(blocks):
        odd = (index & bit) != 0
        blocks = [jnp.where(odd, blocks[m ^ bit], blocks[m]) for m in range(len(blocks))]
        bit *= 2
    return blocks


def split(array, dim, count):
    size = array.shape[dim] // count
    return [lax.slice_in_dim(array, m * size, (m + 1) * size, axis=dim) for m in range(count)]


def to_tree(array, dim, axes, steps):
    masks = masks_of(axes, steps)
    blocks = cross_over(split(array, dim, len(masks)), axes)
    return jnp.concatenate([blocks[m] for m in masks], axis=dim)


def from_tree(array, dim, axes, steps):
    masks = masks_of(axes, steps)
    blocks = split(array, dim, len(masks))
    blocks = cross_over([blocks[masks.index(m)] for m in range(len(masks))], axes)
    return jnp.concatenate(blocks, axis=dim)


def in_tree(block, bits):
    return sum(((block >> k) & 1) << (bits - 1 - k) for k in range(bits))


def stack_heads(value, heads):
    lane = lax.broadcasted_iota(jnp.int32, value.shape, 1) // HDIM
    zero = jnp.zeros_like(value)
    return jnp.concatenate([jnp.where(lane == h, value, zero) for h in range(heads)], axis=0)


def scores_of(rows, stacked, head, count):
    part = stacked[head * count : (head + 1) * count, :]
    return lax.dot_general(rows, part, (((1,), (1,)), ((), ())), preferred_element_type=jnp.float32)


def allowed_in(lower, key_start, query_start, shape):
    key = key_start + lax.broadcasted_iota(jnp.int32, shape, 0)
    query = query_start + lax.broadcasted_iota(jnp.int32, (1, shape[1]), 1)
    return (key >= lower) & (key <= query)


def attend_kernel(heads, masked, bits, meta, *refs):
    if masked:
        lower_ref, query_ref, keys_ref, values_ref, old_keys_ref, old_values_ref = refs[:6]
        mixed_ref, mixed_t_ref, lse_ref, acc_ref = refs[6:]
        lower = lower_ref[...]
    else:
        query_ref, keys_ref, values_ref, mixed_ref, mixed_t_ref, lse_ref, acc_ref = refs
    step = pl.program_id(0)
    count = query_ref.shape[0]
    stacked = stack_heads(query_ref[...], heads)
    acc_ref[...] = jnp.zeros_like(acc_ref)
    tile = in_tree(step, bits) ^ meta[0]

    def add(carry, keys_from, values_from, place, key_tile, masking):
        rows = pl.ds(pl.multiple_of(place * count, count), count)
        keys, values_t = keys_from[rows, :], values_from[rows, :].T
        out = []
        for h in range(heads):
            top, total = carry[h]
            scores = scores_of(keys, stacked, h, count)
            if masking:
                ok = allowed_in(lower, key_tile * count, tile * count, scores.shape)
                scores = jnp.where(ok, scores, NEGATIVE)
            higher = jnp.maximum(top, jnp.max(scores, axis=0, keepdims=True))
            expo = jnp.exp(scores - higher)
            scale = jnp.exp(top - higher)
            part = slice(h * HDIM, (h + 1) * HDIM)
            acc_ref[part, :] = acc_ref[part, :] * scale + matmul(values_t[part, :], low(expo))
            out.append((higher, total * scale + jnp.sum(expo, axis=0, keepdims=True)))
        return tuple(out)

    first = jnp.full((1, count), NEGATIVE, jnp.float32)
    carry = tuple((first, jnp.zeros((1, count), jnp.float32)) for _ in range(heads))
    if masked:
        least = meta[1 + step]
        here = lambda n, c: add(
            c, keys_ref, values_ref, in_tree((tile - n) ^ meta[0], bits), tile - n, True
        )
        carry = lax.fori_loop(0, tile - jnp.maximum(least, 0) + 1, here, carry)
        tiles = old_keys_ref.shape[0] // count
        before = lambda n, c: add(
            c, old_keys_ref, old_values_ref, in_tree((n + tiles) ^ meta[0], bits), n, True
        )
        carry = lax.fori_loop(least, 0, before, carry)
    else:
        every = lambda n, c: add(c, keys_ref, values_ref, n, n, False)
        carry = lax.fori_loop(0, keys_ref.shape[0] // count, every, carry)
    for h in range(heads):
        top, total = carry[h]
        part = slice(h * HDIM, (h + 1) * HDIM)
        mixed_t_ref[part, :] = acc_ref[part, :] / total
        lse_ref[h : h + 1, :] = top + jnp.log(total)
    mixed_ref[...] = low(mixed_t_ref[...].T)


def attend_back_kernel(heads, masked, old, bits, meta, *refs):
    refs = list(refs)
    lower = refs.pop(0)[...] if masked else None
    start_ref = refs.pop(0) if masked and not old else None
    query_ref, grad_ref, mixed_t_ref, lse_ref, keys_ref, values_ref = refs[:6]
    grad_query_ref, grad_keys_ref, grad_values_ref, keys_acc, values_acc, query_acc = refs[6:]
    step = pl.program_id(0)
    count = query_ref.shape[0]

    @pl.when(step == 0)
    def _():
        keys_acc[...] = jnp.zeros_like(keys_acc)
        values_acc[...] = jnp.zeros_like(values_acc)

    tile = in_tree(step, bits) ^ meta[0]
    if start_ref is None:
        query_acc[...] = jnp.zeros_like(query_acc)
    else:
        query_acc[...] = start_ref[...]
    stacked = stack_heads(query_ref[...], heads)
    grad = grad_ref[...]
    stacked_grad = stack_heads(grad, heads)
    weighed = wide(grad.T) * mixed_t_ref[...]
    lse = lse_ref[...]
    inner = [
        jnp.sum(weighed[h * HDIM : (h + 1) * HDIM, :], axis=0, keepdims=True) for h in range(heads)
    ]

    def add(place, key_tile):
        rows = pl.ds(pl.multiple_of(place * count, count), count)
        keys, values = keys_ref[rows, :], values_ref[rows, :]
        keys_t = keys.T
        probs, slopes = [], []
        if masked:
            ok = allowed_in(lower, key_tile * count, tile * count, (count, count))
        for h in range(heads):
            expo = jnp.exp(scores_of(keys, stacked, h, count) - lse[h : h + 1, :])
            if masked:
                expo = jnp.where(ok, expo, 0.0)
            slope = low(expo * (scores_of(values, stacked_grad, h, count) - inner[h]))
            part = slice(h * HDIM, (h + 1) * HDIM)
            query_acc[part, :] += matmul(keys_t[part, :], slope)
            probs.append(low(expo))
            slopes.append(slope)
        values_acc[rows, :] += matmul(jnp.concatenate(probs, axis=1), stacked_grad)
        keys_acc[rows, :] += matmul(jnp.concatenate(slopes, axis=1), stacked)

    if not masked:
        pl.loop(0, keys_ref.shape[0] // count)(lambda n: add(n, n))
    elif old:
        tiles = keys_ref.shape[0] // count
        pl.loop(meta[1 + step], 0)(lambda n: add(in_tree((n + tiles) ^ meta[0], bits), n))
    else:
        pl.loop(jnp.maximum(meta[1 + step], 0), tile + 1)(
            lambda n: add(in_tree(n ^ meta[0], bits), n)
        )
    if old:
        grad_query_ref[...] = query_acc[...]
    else:
        grad_query_ref[...] = low(query_acc[...].T)

    @pl.when(step == pl.num_programs(0) - 1)
    def _():
        grad_keys_ref[...] = keys_acc[...].astype(grad_keys_ref.dtype)
        grad_values_ref[...] = values_acc[...].astype(grad_values_ref.dtype)


def tiled(width, column):
    return pl.BlockSpec((TILE, width), lambda t, meta: (t, column))


def tiled_t(height):
    return pl.BlockSpec((height, TILE), lambda t, meta: (0, t))


def entire(rows, width, column):
    return pl.BlockSpec((rows, width), lambda t, meta: (0, column))


def attend(meta, lower, query, keys, values, width, before=None):
    rows = query[0].shape[0]
    count = keys[0].shape[0]
    heads = width // HDIM
    masked = before is not None
    inputs = [query[0], keys[0], values[0]]
    specs = [
        tiled(width, query[1]),
        entire(count, width, keys[1]),
        entire(count, width, values[1]),
    ]
    if masked:
        inputs = [lower] + inputs + [before[0], before[0]]
        specs = [tiled_t(1)] + specs
        specs += [entire(before[0].shape[0], width, 0), entire(before[0].shape[0], width, 1)]
    pairs = rows * count * width
    return pl.pallas_call(
        partial(attend_kernel, heads, masked, (rows // TILE).bit_length() - 1),
        grid_spec=pltpu.PrefetchScalarGridSpec(
            num_scalar_prefetch=1,
            grid=(rows // TILE,),
            in_specs=specs,
            out_specs=[tiled(width, 0), tiled_t(width), tiled_t(heads)],
            scratch_shapes=[pltpu.VMEM((width, TILE), jnp.float32)],
        ),
        out_shape=[
            jax.ShapeDtypeStruct((rows, width), jnp.bfloat16),
            jax.ShapeDtypeStruct((width, rows), jnp.float32),
            jax.ShapeDtypeStruct((heads, rows), jnp.float32),
        ],
        compiler_params=pltpu.CompilerParams(vmem_limit_bytes=VMEM),
        cost_estimate=pl.CostEstimate(
            flops=64 * pairs, bytes_accessed=2 * (rows + count) * width * 2, transcendentals=0
        ),
    )(meta, *inputs)


def attend_back(meta, lower, query, grad, mixed_t, lse, keys, values, width, kind, start=None):
    rows = query[0].shape[0]
    count = keys[0].shape[0]
    heads = width // HDIM
    masked = kind != "cross"
    old = kind == "old"
    inputs = [query[0], grad, mixed_t, lse, keys[0], values[0]]
    specs = [
        tiled(width, query[1]),
        tiled(width, 0),
        tiled_t(width),
        tiled_t(heads),
        entire(count, width, keys[1]),
        entire(count, width, values[1]),
    ]
    if start is not None:
        inputs, specs = [start] + inputs, [tiled_t(width)] + specs
    if masked:
        inputs, specs = [lower] + inputs, [tiled_t(1)] + specs
    kept = jnp.bfloat16 if masked else jnp.float32
    pairs = rows * count * width
    return pl.pallas_call(
        partial(attend_back_kernel, heads, masked, old, (rows // TILE).bit_length() - 1),
        grid_spec=pltpu.PrefetchScalarGridSpec(
            num_scalar_prefetch=1,
            grid=(rows // TILE,),
            in_specs=specs,
            out_specs=[
                tiled_t(width) if old else tiled(width, 0),
                entire(count, width, 0),
                entire(count, width, 0),
            ],
            scratch_shapes=[
                pltpu.VMEM((count, width), jnp.float32),
                pltpu.VMEM((count, width), jnp.float32),
                pltpu.VMEM((width, TILE), jnp.float32),
            ],
        ),
        out_shape=[
            jax.ShapeDtypeStruct((width, rows), jnp.float32)
            if old
            else jax.ShapeDtypeStruct((rows, width), jnp.bfloat16),
            jax.ShapeDtypeStruct((count, width), kept),
            jax.ShapeDtypeStruct((count, width), kept),
        ],
        compiler_params=pltpu.CompilerParams(vmem_limit_bytes=VMEM),
        cost_estimate=pl.CostEstimate(
            flops=80 * pairs, bytes_accessed=4 * (rows + count) * width * 2, transcendentals=0
        ),
    )(meta, *inputs)


def layer_norm(value, gain, shift_by):
    centre = value - jnp.mean(value, axis=-1, keepdims=True)
    rstd = lax.rsqrt(jnp.mean(centre * centre, axis=-1, keepdims=True) + EPSILON)
    normed = centre * rstd
    return (normed * gain + shift_by, normed, rstd)


def norm_back(grad_out, normed, rstd, gain):
    scaled = grad_out * gain
    inner = scaled - jnp.mean(scaled, axis=-1, keepdims=True)
    inner = inner - normed * jnp.mean(scaled * normed, axis=-1, keepdims=True)
    return (rstd * inner, jnp.sum(grad_out * normed, axis=0), jnp.sum(grad_out, axis=0))


def gelu_and_slope(value):
    phi = 0.5 * (1.0 + lax.erf(value * 0.7071067811865476))
    bell = jnp.exp(-0.5 * value * value) * 0.3989422804014327
    return value * phi, phi + value * bell


def column_sum(value):
    return jnp.sum(wide(value), axis=0)


def per_device(
    inputs,
    encoded,
    doc_lengths,
    cotangent,
    query_weight,
    key_weight,
    value_weight,
    out_weight,
    memory_query,
    memory_key,
    memory_value,
    memory_out,
    up_weight,
    down_weight,
    query_bias,
    value_bias,
    memory_qbias,
    memory_vbias,
    up_bias,
    out_bias,
    memory_obias,
    down_bias,
    gain_self,
    shift_self,
    gain_memory,
    shift_memory,
    gain_dense,
    shift_dense,
):
    tp_index = lax.axis_index("tp")
    share_rows = inputs.shape[1]
    rows = share_rows * lax.axis_size("tp")
    width = query_weight.shape[1]
    base = lax.axis_index("ctx") * rows
    row_steps = steps_of("tp")
    weight_steps = steps_of("shard", "ctx")
    features = ("shard", "ctx")

    def turned(array, dim):
        return to_tree(array, dim, features, weight_steps)

    def turned_back(array, dim):
        return from_tree(array, dim, features, weight_steps)

    def gather_rows(piece):
        return gather_tree(piece, row_steps)

    def scatter_rows(make):
        return scatter_tree(make, rows, row_steps)

    def own_half(weight):
        part = weight.shape[0] // lax.axis_size("ctx")
        return lax.dynamic_slice_in_dim(weight, lax.axis_index("ctx") * part, part, 0)

    ctx_steps = steps_of("ctx")
    far_steps, near_steps = steps_of("shard")[:-1], steps_of("shard")[-1:]
    share = turned(inputs[0], 1)
    old_share = turned(shift(inputs[0], "ctx", 1), 1)
    inputs_rows = gather_rows(share)
    old_rows = gather_rows(old_share)
    qkv_own = own_half(jnp.concatenate([query_weight, key_weight, value_weight], axis=1))
    qkv_far = gather_tree(qkv_own, far_steps)
    qkv_near = gather_tree(qkv_far, near_steps)
    qkv_full = gather_tree(qkv_near, ctx_steps)
    out_far = gather_tree(own_half(out_weight.T), far_steps, qkv_far)
    out_near = gather_tree(out_far, near_steps, qkv_near)
    small_own = jnp.concatenate([memory_key, memory_value, memory_query, memory_out.T], axis=1)
    small_far = gather_tree(own_half(small_own), far_steps, qkv_near)
    small_near = gather_tree(small_far, near_steps)
    up_own = own_half(up_weight)
    down_own = own_half(down_weight.T)
    states = to_tree(turned(encoded[0], 1), 0, ("tp",), row_steps)
    vectors = turned(
        jnp.stack(
            [
                out_bias,
                memory_obias,
                down_bias,
                gain_self,
                shift_self,
                gain_memory,
                shift_memory,
                gain_dense,
                shift_dense,
            ]
        ),
        1,
    )
    (
        out_bias,
        memory_obias,
        down_bias,
        gain_self,
        shift_self,
        gain_memory,
        shift_memory,
        gain_dense,
        shift_dense,
    ) = [vectors[i] for i in range(9)]
    upstream = wide(turned(cotangent[0], 1))

    ends = jnp.cumsum(doc_lengths[0], dtype=jnp.int32)
    masks = jnp.asarray(masks_of(("tp",), row_steps), jnp.int32)
    starts = (masks ^ tp_index) * share_rows
    place = base + (starts[:, None] + jnp.arange(share_rows, dtype=jnp.int32)).reshape(-1)
    opens = jnp.max(jnp.where(place[:, None] >= ends[None, :], ends[None, :], 0), axis=1)
    lower = jnp.maximum(opens, place - (W - 1)) - base
    least = lower.reshape(-1, TILE)[:, 0] // TILE
    meta = jnp.concatenate([tp_index[None].astype(jnp.int32), least])
    lower = lower[None, :]

    zeros = jnp.zeros_like(query_bias)
    qkv = low(
        (matmul(inputs_rows, qkv_full) + jnp.concatenate([query_bias, zeros, value_bias]))
        * jnp.concatenate([zeros + 0.125, zeros + 1.0, zeros + 1.0])
    )
    old_kv = low(matmul(old_rows, qkv_full[:, width:]) + jnp.concatenate([zeros, value_bias]))
    qkv = after(qkv, out_near, small_near)
    mixed, mixed_t, self_lse = attend(
        meta, lower, (qkv, 0), (qkv, 1), (qkv, 2), width, (old_kv, None)
    )
    out_full = gather_tree(out_near, ctx_steps, qkv_full, mixed)
    mkv_full = gather_tree(small_near[:, : 2 * width], ctx_steps, old_kv, mixed)
    up_far = gather_tree(up_own, far_steps, small_near, mixed)
    mixed = after(mixed, mkv_full)
    attn_part = scatter_tree(
        lambda s: contract("rk,dk->rd", mixed[s], out_full), rows, row_steps[-1:]
    )

    mkv_own = low(
        matmul(states, after(mkv_full, attn_part)) + jnp.concatenate([zeros, memory_vbias])
    )

    def weight_terms(*pairs):
        def make(s):
            return jnp.concatenate(
                [contract("rd,rk->dk", left[:, s], right) for left, right in pairs], axis=1
            )

        return make

    model = share.shape[1]

    still = jnp.zeros((1,), jnp.int32)
    attn_share = scatter_more(attn_part, row_steps[:-1])
    first, normed_one, rstd_one = layer_norm(
        wide(share) + attn_share + out_bias, gain_self, shift_self
    )
    first_low = after(low(first), up_far)
    mkv = gather_tree(mkv_own, ctx_steps, None, first_low)
    up_near = gather_tree(up_far, near_steps, attn_part, first_low)
    down_far = gather_tree(down_own, far_steps, attn_part, first_low)
    small_full = gather_tree(small_near[:, 2 * width :], ctx_steps, attn_part, first_low)
    mquery_full, mout_full = small_full[:, :width], small_full[:, width:]
    first_rows = after(gather_rows(first_low), up_near, down_far)
    mquery = low((matmul(first_rows, mquery_full) + memory_qbias) * 0.125)
    cross_mixed, cross_mixed_t, cross_lse = attend(
        still, None, (mquery, 0), (mkv, 0), (mkv, 1), width
    )
    up_full = gather_tree(up_near, ctx_steps, mkv, cross_mixed)
    down_near = gather_tree(down_far, near_steps, mkv, cross_mixed)
    cross_mixed = after(cross_mixed, up_full, down_near)
    cross_share = scatter_rows(lambda s: contract("rk,dk->rd", cross_mixed[s], mout_full))
    second, normed_two, rstd_two = layer_norm(
        first + cross_share + memory_obias, gain_memory, shift_memory
    )
    second_low = low(second)
    down_full = gather_tree(down_near, ctx_steps, cross_mixed, second_low)
    second_rows = gather_rows(second_low)
    act, slope = gelu_and_slope(matmul(second_rows, up_full) + up_bias)
    act_low, slope_low = low(act), low(slope)
    dense_share = scatter_rows(lambda s: contract("rf,df->rd", act_low[s], down_full))
    result, normed_three, rstd_three = layer_norm(
        second + dense_share + down_bias, gain_dense, shift_dense
    )
    grad_three, gain_dense_grad, shift_dense_grad = norm_back(
        upstream, normed_three, rstd_three, gain_dense
    )
    dense_low = low(grad_three)
    dense_rows = gather_rows(dense_low)
    hidden_low = low(matmul(dense_rows, down_full) * wide(slope_low))
    second_share = scatter_rows(lambda s: contract("rf,df->rd", hidden_low[s], up_full))
    grad_two, gain_memory_grad, shift_memory_grad = norm_back(
        grad_three + second_share, normed_two, rstd_two, gain_memory
    )

    cross_low = low(grad_two)
    down_part = scatter_tree(weight_terms((dense_rows, act_low)), model, ctx_steps, cross_low)
    cross_rows = gather_rows(cross_low)
    down_near_grad = scatter_more(down_part, near_steps, None, cross_rows)
    grad_cross_mixed = low(matmul(cross_rows, mout_full))
    mquery_back, mkeys_back, mvalues_back = attend_back(
        still,
        None,
        (mquery, 0),
        grad_cross_mixed,
        cross_mixed_t,
        cross_lse,
        (mkv, 0),
        (mkv, 1),
        width,
        "cross",
    )
    mquery_pre = mquery_back * 0.125
    down_grads = scatter_more(down_near_grad, far_steps, None, mquery_pre)
    up_part = scatter_tree(weight_terms((second_rows, hidden_low)), model, ctx_steps, mquery_pre)
    first_part = scatter_tree(
        lambda s: contract("rk,dk->rd", mquery_pre[s], mquery_full), rows, row_steps[-1:]
    )
    first_share = scatter_more(first_part, row_steps[:-1])
    grad_one, gain_self_grad, shift_self_grad = norm_back(
        grad_two + first_share, normed_one, rstd_one, gain_self
    )
    self_low = low(grad_one)
    self_rows = gather_rows(self_low)
    up_near_grad = scatter_more(up_part, near_steps, first_part, self_low)
    up_grads = scatter_more(up_near_grad, far_steps, None, self_rows)
    mkv_back = after(jnp.concatenate([mkeys_back, mvalues_back], axis=1), first_part)
    mkv_low = low(scatter_tree(lambda s: mkv_back[s], mkv_back.shape[0], ctx_steps))
    encoded_grad = scatter_tree(
        lambda s: contract("ek,dk->ed", mkv_low[s], mkv_full), states.shape[0], row_steps
    )
    small_part = scatter_tree(
        weight_terms((states, mkv_low), (first_rows, mquery_pre), (cross_rows, cross_mixed)),
        model,
        ctx_steps,
        self_rows,
    )
    grad_self = after(low(matmul(self_rows, out_full)), small_part)

    query_start, old_keys, old_values = attend_back(
        meta,
        lower,
        (qkv, 0),
        grad_self,
        mixed_t,
        self_lse,
        (old_kv, 0),
        (old_kv, 1),
        width,
        "old",
    )
    old_back = jnp.concatenate([old_keys, old_values], axis=1)
    back = shift(old_back, "ctx", -1)
    small_near_grads = scatter_more(small_part, near_steps, None, old_back)
    grad_self_later = after(grad_self, small_near_grads, query_start)
    query_back, keys_back, values_back = attend_back(
        meta,
        lower,
        (qkv, 0),
        grad_self_later,
        mixed_t,
        self_lse,
        (qkv, 1),
        (qkv, 2),
        width,
        "own",
        query_start,
    )
    query_pre = query_back * 0.125
    small_grads = scatter_more(small_near_grads, far_steps, None, query_pre)
    out_part = scatter_tree(weight_terms((self_rows, mixed)), model, ctx_steps, query_pre)
    own_back = jnp.concatenate([query_pre, keys_back, values_back], axis=1)

    def qkv_terms(s):
        own = contract("rd,rk->dk", inputs_rows[:, s], own_back)
        old = contract("rd,rk->dk", old_rows[:, s], old_back)
        return own + jnp.pad(old, ((0, 0), (width, 0)))

    kv_all = low(wide(own_back[:, width:]) + wide(back))

    def inputs_term(s):
        term = contract("rk,dk->rd", query_pre[s], qkv_full[:, :width])
        return term + contract("rk,dk->rd", kv_all[s], qkv_full[:, width:])

    inputs_part = scatter_tree(inputs_term, rows, row_steps[-1:])
    inputs_grad = grad_one + scatter_more(inputs_part, row_steps[:-1])
    qkv_grads = scatter_more(
        scatter_tree(qkv_terms, model, ctx_steps, inputs_part), weight_steps[: -len(ctx_steps)]
    )
    out_grads = scatter_more(out_part, steps_of("shard"), inputs_part)

    everywhere = jnp.stack(
        [
            column_sum(self_low),
            column_sum(cross_low),
            column_sum(dense_low),
            gain_self_grad,
            shift_self_grad,
            gain_memory_grad,
            shift_memory_grad,
            gain_dense_grad,
            shift_dense_grad,
        ]
    )
    everywhere = all_sum(turned_back(everywhere, 1), row_steps)
    by_heads = jnp.concatenate(
        [
            column_sum(query_pre),
            column_sum(values_back) + column_sum(old_values),
            column_sum(mquery_pre),
            column_sum(mkv_low[:, width:]),
            column_sum(hidden_low),
        ]
    )
    lanes = 128
    sums = all_sum(
        after(
            jnp.concatenate([everywhere.reshape(-1, lanes), by_heads.reshape(-1, lanes)], axis=0),
            inputs_part,
        ),
        weight_steps,
    )
    cut = everywhere.size // lanes
    totals = sums[:cut].reshape(everywhere.shape)
    head_totals = sums[cut:].reshape(-1)
    return (
        turned_back(low(result), 1)[None],
        turned_back(inputs_grad, 1)[None],
        turned_back(encoded_grad, 1)[None],
        qkv_grads[:, :width],
        qkv_grads[:, width : 2 * width],
        qkv_grads[:, 2 * width :],
        out_grads.T,
        small_grads[:, 2 * width : 3 * width],
        small_grads[:, :width],
        small_grads[:, width : 2 * width],
        small_grads[:, 3 * width :].T,
        up_grads,
        down_grads.T,
        head_totals[:width],
        head_totals[width : 2 * width],
        head_totals[2 * width : 3 * width],
        head_totals[3 * width : 4 * width],
        head_totals[4 * width :],
        totals[0],
        totals[1],
        totals[2],
        totals[3],
        totals[4],
        totals[5],
        totals[6],
        totals[7],
        totals[8],
    )


def solution(mesh):
    placed = (
        P("shard", ("ctx", "tp"), None),
        P("shard", "ctx", None),
        P("shard", None),
        P("shard", ("ctx", "tp"), None),
        P("shard", "tp"),
        P("shard", "tp"),
        P("shard", "tp"),
        P("tp", "shard"),
        P("shard", "tp"),
        P("shard", "tp"),
        P("shard", "tp"),
        P("tp", "shard"),
        P("shard", "tp"),
        P("tp", "shard"),
        P("tp"),
        P("tp"),
        P("tp"),
        P("tp"),
        P("tp"),
        P(),
        P(),
        P(),
        P(),
        P(),
        P(),
        P(),
        P(),
        P(),
    )
    return jax.shard_map(
        per_device,
        mesh=mesh,
        in_specs=placed,
        out_specs=(
            P("shard", ("ctx", "tp"), None),
            P("shard", ("ctx", "tp"), None),
            P("shard", ("ctx", "tp"), None),
            P(("shard", "ctx"), "tp"),
            P(("shard", "ctx"), "tp"),
            P(("shard", "ctx"), "tp"),
            P("tp", ("shard", "ctx")),
            P(("shard", "ctx"), "tp"),
            P(("shard", "ctx"), "tp"),
            P(("shard", "ctx"), "tp"),
            P("tp", ("shard", "ctx")),
            P(("shard", "ctx"), "tp"),
            P("tp", ("shard", "ctx")),
            P("tp"),
            P("tp"),
            P("tp"),
            P("tp"),
            P("tp"),
            P(),
            P(),
            P(),
            P(),
            P(),
            P(),
            P(),
            P(),
            P(),
        ),
        check_vma=False,
    )
```

time: 662 us -> 517 us (0.78)
  waiting for transfers between devices: 274 us -> 194 us
  starting transfers between devices: 167 us -> 90.9 us
  matrix products: 76.6 us -> 58.8 us
  local copies, waits for them, and re-layouts: 22 us -> 38.9 us
  other arithmetic: 44.8 us -> 61.3 us
    ppermute x113 -> x66, starting transfers between devices: 162 us -> 84.4 us  [swap(): lax.ppermute(array, axis, [(i, i ^ bit) for i in range(lax.axis_size(axis...]
    ppermute x113 -> x66, waiting for transfers between devices: 270 us -> 194 us  [swap(): lax.ppermute(array, axis, [(i, i ^ bit) for i in range(lax.axis_size(axis...]
    concatenate x10 -> x37, other arithmetic: 4.57 us -> 19 us  [the longest x21 11.7 us: gather_tree(): jnp.concatenate([after(array, used if n == len(steps) - 1 else None), arr...]
    dot_general x11 -> x8, matrix products: 37.7 us -> 23.7 us  [matmul(): return jnp.dot(left, right, preferred_element_type=jnp.float32)]
    unnamed x301 -> x320, local copies, waits for them, and re-layouts: 9.64 us -> 19.5 us
    unnamed x0 -> x65, other arithmetic: none -> 9.12 us
    add x12 -> x16, other arithmetic: 6.15 us -> 13.8 us  [the longest x9 6.76 us: scatter_more(): total = kept + wide(arrived)]
    slice x22 -> x34, local copies, waits for them, and re-layouts: 4.89 us -> 12.3 us  [the longest x17 7.7 us: scatter_more(): total[half:]]
  transfers between devices with their start and end apart: 115 -> 68, of which waited for: 42 -> 34; matrix products, arithmetic and copies ran while one was open for 14% -> 24% of each run, Pallas kernels for 2% -> 12%
where the time goes in v2:
time: 517 us; the launch traced here: 511 us
  waiting for transfers between devices  194 us (38%)
  starting transfers between devices  90.9 us (18%)
  Pallas kernels  62.9 us (12%)
  other arithmetic  61.3 us (12%)
  matrix products  58.8 us (11%)
  local copies, waits for them, and re-layouts  38.9 us (8%)
    ppermute x66, waiting for transfers between devices, swap(): lax.ppermute(array, axis, [(i, i ^ bit) for i in range(lax.axis_size(axis...  194 us
    ppermute x66, starting transfers between devices, swap(): lax.ppermute(array, axis, [(i, i ^ bit) for i in range(lax.axis_size(axis...  84.4 us
    pallas_call x3, Pallas kernels, attend_back(): pl.pallas_call(partial(attend_back_kernel, heads, masked, old, (rows // T...  38.6 us
    dot_general x32, matrix products, contract(): return jnp.einsum(form, left, right, preferred_element_type=jnp.float32)  35.1 us
    pallas_call x2, Pallas kernels, attend(): pl.pallas_call(partial(attend_kernel, heads, masked, (rows // TILE).bit_l...  24.4 us
    dot_general x8, matrix products, matmul(): return jnp.dot(left, right, preferred_element_type=jnp.float32)  23.7 us
    unnamed x320, local copies, waits for them, and re-layouts  19.5 us
    concatenate x21, other arithmetic, gather_tree(): jnp.concatenate([after(array, used if n == len(steps) - 1 else None), arr...  11.7 us
  transfers between devices with their start and end apart: 68, of which 34 were waited for; matrix products, arithmetic and copies ran while one was open for 24% of the time, Pallas kernels for 12%

profile of v2, /device:TPU:0, one launch (start us, length us, event | category | flops | bytes accessed | tf_op | source)
XLA Modules:
  0.0 510.9 jit_solution(13509394096813699669)
XLA Ops:
  0.7 5.0 collective-permute-start.9
  32.7 6.5 %collective-permute-done.3 = bf16[256,768]{1,0:T(8,128)(2,1)S(1)} collective-permute-done((bf16[256,768]{1,0:T(8,128)(2,1)S(1)}, bf16[256,768]{1,0:T(8,128)(2,1)S(1)}, u32[]{:S(2)}, u32[]{:S(2)}) %collective-permute-start.3) | collective-permute-done | bytes 393248 | tf_op jit(solution)/shard_map/ppermute | solution.py:37
  43.8 9.1 %collective-permute-done.7 = bf16[128,1024]{0,1:T(8,128)(2,1)S(1)} collective-permute-done((bf16[128,1024]{0,1:T(8,128)(2,1)S(1)}, bf16[128,1024]{0,1:T(8,128)(2,1)S(1)}, u32[]{:S(2)}, u32[]{:S(2)}) %collective-permute-start.7) | collective-permute-done | bytes 262176 | tf_op jit(solution)/shard_map/ppermute | solution.py:37
  58.0 8.8 %collective-permute-done.8 = bf16[256,1024]{0,1:T(8,128)(2,1)S(1)} collective-permute-done((bf16[256,1024]{0,1:T(8,128)(2,1)S(1)}, bf16[256,1024]{0,1:T(8,128)(2,1)S(1)}, u32[]{:S(2)}, u32[]{:S(2)}) %collective-permute-start.8) | collective-permute-done | bytes 524320 | tf_op jit(solution)/shard_map/ppermute | solution.py:37
  74.8 13.0 %shard_map.484 = (bf16[1024,256]{1,0:T(8,128)(2,1)}, f32[256,1024]{1,0:T(8,128)}, f32[4,1024]{1,0:T(4,128)}) custom-call(s32[5]{0:T(128)} %pad_add_fusion.1.meta, s32[1,1024]{1,0:T(1,128)} %maximum_subtract_fusion.refs_0_, bf16[1024,768]{1,0:T(8,128)(2,1)} %multiply_convert_fusion.2.refs_1_.refs_2_.refs_3_.refs_6_.refs_7_, ...), custom_call_target="tpu_custom_call" | custom-call | flops 17179869184 | bytes 2097152 | tf_op jit(solution)/shard_map/pallas_call | solution.py:304
  95.4 12.5 %collective-permute-done.16 = bf16[128,1024]{1,0:T(8,128)(2,1)S(1)} collective-permute-done((bf16[128,1024]{1,0:T(8,128)(2,1)S(1)}, bf16[128,1024]{1,0:T(8,128)(2,1)S(1)}, u32[]{:S(2)}, u32[]{:S(2)}) %collective-permute-start.16) | collective-permute-done | bytes 262176 | tf_op jit(solution)/shard_map/ppermute | solution.py:37
  113.9 7.1 %collective-permute-start.22 = (bf16[256,512]{1,0:T(8,128)(2,1)S(1)}, bf16[256,512]{1,0:T(8,128)(2,1)S(1)}, u32[]{:S(2)}, u32[]{:S(2)}) collective-permute-start(bf16[256,512]{1,0:T(8,128)(2,1)S(1)} %fusion.10), channel_id=1, source_target_pairs={{0,4},{4,0},{1,5},{5,1},{2,6},{6,2},{3,7},{7,3},{8,12},{12,8},{9,1... | collective-permute-start | bytes 786440 | tf_op jit(solution)/shard_map/ppermute | solution.py:37
  127.9 7.1 %collective-permute-start.21 = (bf16[512,512]{0,1:T(8,128)(2,1)S(1)}, bf16[512,512]{0,1:T(8,128)(2,1)S(1)}, u32[]{:S(2)}, u32[]{:S(2)}) collective-permute-start(bf16[512,512]{0,1:T(8,128)(2,1)S(1)} %copy-done.46), channel_id=1, source_target_pairs={{0,4},{4,0},{1,5},{5,1},{2,6},{6,2},{3,7},{7,3},{8,12},{12,8},{9,1... | collective-permute-start | bytes 1572872 | tf_op jit(solution)/shard_map/ppermute | solution.py:37
  135.1 4.9 collective-permute-done.20
  140.2 6.0 %collective-permute-done.19 = bf16[256,1024]{1,0:T(8,128)(2,1)S(1)} collective-permute-done((bf16[256,1024]{1,0:T(8,128)(2,1)S(1)}, bf16[256,1024]{1,0:T(8,128)(2,1)S(1)}, u32[]{:S(2)}, u32[]{:S(2)}) %collective-permute-start.19) | collective-permute-done | bytes 524320 | tf_op jit(solution)/shard_map/ppermute | solution.py:37
  146.2 7.1 %collective-permute-start.23 = (bf16[512,1024]{1,0:T(8,128)(2,1)S(1)}, bf16[512,1024]{1,0:T(8,128)(2,1)S(1)}, u32[]{:S(2)}, u32[]{:S(2)}) collective-permute-start(bf16[512,1024]{1,0:T(8,128)(2,1)S(1)} %constant_dynamic-update-slice_fusion.30), channel_id=1, source_target_pairs={{0,4},{4,0},{1,5},{5,1},{2,6},{6,2},{3,7},{7,3},{8,12},{12,8},{9,1... | collective-permute-start | bytes 3145736 | tf_op jit(solution)/shard_map/ppermute | solution.py:37
  156.8 11.3 %shard_map.485 = (bf16[1024,256]{1,0:T(8,128)(2,1)}, f32[256,1024]{1,0:T(8,128)}, f32[4,1024]{1,0:T(4,128)}) custom-call(s32[1]{0:T(128)} %constant.81.clone.1.meta, bf16[1024,256]{1,0:T(8,128)(2,1)} %fusion.9.refs_0_, bf16[512,512]{1,0:T(8,128)(2,1)} %copy-done.100, bf16[512,512]{1,0:T(8,128)(2,1)} %copy-done.100), custom_call_target="tpu_custom_call" | custom-call | flops 8589934592 | bytes 1572864 | tf_op jit(solution)/shard_map/pallas_call | solution.py:304
  168.3 7.7 %collective-permute-done.23 = bf16[512,1024]{1,0:T(8,128)(2,1)S(1)} collective-permute-done((bf16[512,1024]{1,0:T(8,128)(2,1)S(1)}, bf16[512,1024]{1,0:T(8,128)(2,1)S(1)}, u32[]{:S(2)}, u32[]{:S(2)}) %collective-permute-start.23) | collective-permute-done | bytes 1048608 | tf_op jit(solution)/shard_map/ppermute | solution.py:37
  181.4 12.5 %collective-permute-done.26 = bf16[256,1024]{1,0:T(8,128)(2,1)S(1)} collective-permute-done((bf16[256,1024]{1,0:T(8,128)(2,1)S(1)}, bf16[256,1024]{1,0:T(8,128)(2,1)S(1)}, u32[]{:S(2)}, u32[]{:S(2)}) %collective-permute-start.26) | collective-permute-done | bytes 524320 | tf_op jit(solution)/shard_map/ppermute | solution.py:37
  198.3 9.9 %collective-permute-done.27 = bf16[256,1024]{1,0:T(8,128)(2,1)S(1)} collective-permute-done((bf16[256,1024]{1,0:T(8,128)(2,1)S(1)}, bf16[256,1024]{1,0:T(8,128)(2,1)S(1)}, u32[]{:S(2)}, u32[]{:S(2)}) %collective-permute-start.27) | collective-permute-done | bytes 524320 | tf_op jit(solution)/shard_map/ppermute | solution.py:37
  208.5 12.1 %collective-permute-done.29 = bf16[512,1024]{0,1:T(8,128)(2,1)S(1)} collective-permute-done((bf16[512,1024]{0,1:T(8,128)(2,1)S(1)}, bf16[512,1024]{0,1:T(8,128)(2,1)S(1)}, u32[]{:S(2)}, u32[]{:S(2)}) %collective-permute-start.29) | collective-permute-done | bytes 1048608 | tf_op jit(solution)/shard_map/ppermute | solution.py:37
  220.8 6.5 %multiply_convert_fusion.1 = (bf16[1024,1024]{1,0:T(8,128)(2,1)S(1)}, f32[1024,1024]{1,0:T(8,128)}) fusion(f32[1024]{0:T(1024)S(1)} %copy-done.143, bf16[1024,1024]{1,0:T(8,128)(2,1)S(1)} %constant_dynamic-update-slice_fusion.46, bf16[512,1024]{1,0:T(8,128)(2,1)S(1)} %collective-permute-done.28, bf16[256,1024]{1,0:T(8,128)(2,1)S(1)} %collective-permute-done.27, ...), kind=kOutput, calls=%fused_computation.8 | convolution fusion | flops 2160066560 | bytes 10489856 | tf_op jit(solution)/shard_map/dot_general | solution.py:21
  233.5 13.3 %collective-permute-done.31 = bf16[256,1024]{1,0:T(8,128)(2,1)S(1)} collective-permute-done((bf16[256,1024]{1,0:T(8,128)(2,1)S(1)}, bf16[256,1024]{1,0:T(8,128)(2,1)S(1)}, u32[]{:S(2)}, u32[]{:S(2)}) %collective-permute-start.31) | collective-permute-done | bytes 524320 | tf_op jit(solution)/shard_map/ppermute | solution.py:37
  250.2 12.6 %collective-permute-done.32 = bf16[256,1024]{1,0:T(8,128)(2,1)S(1)} collective-permute-done((bf16[256,1024]{1,0:T(8,128)(2,1)S(1)}, bf16[256,1024]{1,0:T(8,128)(2,1)S(1)}, u32[]{:S(2)}, u32[]{:S(2)}) %collective-permute-start.32) | collective-permute-done | bytes 524320 | tf_op jit(solution)/shard_map/ppermute | solution.py:37
  271.8 6.8 %convert_reduce_fusion = (f32[1024]{0:T(1024)S(1)}, bf16[1024,1024]{1,0:T(8,128)(2,1)S(1)}) fusion(f32[1024,1024]{1,0:T(8,128)} %get-tuple-element.414, f32[1024]{0:T(1024)S(1)} %copy-done.144, bf16[1024,1024]{0,1:T(8,128)(2,1)S(1)} %copy-done.82, bf16[512,1024]{1,0:T(8,128)(2,1)} %collective-permute-done.33, bf16[256,1024]{1,0:T(8,128)(2,1)S(1)} %copy-done.54, ...), kind=kOutput, calls=%fused_computation.6 | convolution fusion | flops 2169502720 | bytes 10493952 | tf_op jit(solution)/shard_map/dot_general | solution.py:21
  293.0 9.1 %collective-permute-done.35 = bf16[256,1024]{1,0:T(8,128)(2,1)S(1)} collective-permute-done((bf16[256,1024]{1,0:T(8,128)(2,1)S(1)}, bf16[256,1024]{1,0:T(8,128)(2,1)S(1)}, u32[]{:S(2)}, u32[]{:S(2)}) %collective-permute-start.35) | collective-permute-done | bytes 524320 | tf_op jit(solution)/shard_map/ppermute | solution.py:37
  304.4 5.6 %collective-permute-done.60 = bf16[512,1024]{1,0:T(8,128)(2,1)S(1)} collective-permute-done((bf16[512,1024]{1,0:T(8,128)(2,1)S(1)}, bf16[512,1024]{1,0:T(8,128)(2,1)S(1)}, u32[]{:S(2)}, u32[]{:S(2)}) %collective-permute-start.60) | collective-permute-done | bytes 1048608 | tf_op jit(solution)/shard_map/ppermute | solution.py:37
  311.9 4.8 collective-permute-done.36
  321.0 15.8 %shard_map.486 = (bf16[1024,256]{1,0:T(8,128)(2,1)}, f32[512,256]{1,0:T(8,128)}, f32[512,256]{1,0:T(8,128)}) custom-call(s32[1]{0:T(128)} %constant.81.clone.1.meta, bf16[1024,256]{1,0:T(8,128)(2,1)} %fusion.9.refs_0_, bf16[1024,256]{1,0:T(8,128)(2,1)} %convolution_convert_fusion.9.refs_1_, f32[256,1024]{1,0:T(8,128)} %get-tuple-element.117.refs_2_, ...), custom_call_target="tpu_custom_call" | custom-call | flops 10737418240 | bytes 3145728 | tf_op jit(solution)/shard_map/pallas_call | solution.py:346
  353.1 3.6 collective-permute-done.62
  367.6 7.3 %collective-permute-done.39 = bf16[256,1024]{1,0:T(8,128)(2,1)S(1)} collective-permute-done((bf16[256,1024]{1,0:T(8,128)(2,1)S(1)}, bf16[256,1024]{1,0:T(8,128)(2,1)S(1)}, u32[]{:S(2)}, u32[]{:S(2)}) %collective-permute-start.39) | collective-permute-done | bytes 524320 | tf_op jit(solution)/shard_map/ppermute | solution.py:37
  384.4 10.1 %collective-permute-done.49 = bf16[64,1024]{1,0:T(8,128)(2,1)S(1)} collective-permute-done((bf16[64,1024]{1,0:T(8,128)(2,1)}, bf16[64,1024]{1,0:T(8,128)(2,1)S(1)}, u32[]{:S(2)}, u32[]{:S(2)}) %collective-permute-start.49) | collective-permute-done | bytes 131104 | tf_op jit(solution)/shard_map/ppermute | solution.py:37
  403.9 5.7 %shard_map.487 = (f32[256,1024]{1,0:T(8,128)}, bf16[1024,256]{1,0:T(8,128)(2,1)}, bf16[1024,256]{1,0:T(8,128)(2,1)}) custom-call(s32[5]{0:T(128)} %pad_add_fusion.1.meta, s32[1,1024]{1,0:T(1,128)} %maximum_subtract_fusion.refs_0_, bf16[1024,768]{1,0:T(8,128)(2,1)} %multiply_convert_fusion.2.refs_1_.refs_2_.refs_3_.refs_6_.refs_7_, ...), custom_call_target="tpu_custom_call" | custom-call | flops 21474836480 | bytes 4194304 | tf_op jit(solution)/shard_map/pallas_call | solution.py:346
  416.3 9.3 %collective-permute-start.53 = (bf16[512,256]{1,0:T(8,128)(2,1)S(1)}, bf16[512,256]{1,0:T(8,128)(2,1)S(1)}, u32[]{:S(2)}, u32[]{:S(2)}) collective-permute-start(bf16[512,256]{1,0:T(8,128)(2,1)S(1)} %convolution_convert_fusion.10), channel_id=1, source_target_pairs={{0,4},{4,0},{1,5},{5,1},{2,6},{6,2},{3,7},{7,3},{8,12},{12,8},{9,1... | collective-permute-start | bytes 786440 | tf_op jit(solution)/shard_map/ppermute | solution.py:37
  432.7 17.0 %shard_map.488 = (bf16[1024,256]{1,0:T(8,128)(2,1)}, bf16[1024,256]{1,0:T(8,128)(2,1)}, bf16[1024,256]{1,0:T(8,128)(2,1)}) custom-call(s32[5]{0:T(128)} %pad_add_fusion.1.meta, s32[1,1024]{1,0:T(1,128)} %maximum_subtract_fusion.refs_0_, f32[256,1024]{1,0:T(8,128)} %get-tuple-element.127.refs_1_, ...), custom_call_target="tpu_custom_call" | custom-call | flops 21474836480 | bytes 4194304 | tf_op jit(solution)/shard_map/pallas_call | solution.py:346
  457.2 7.1 %collective-permute-start.50 = (bf16[512,768]{1,0:T(8,128)(2,1)}, bf16[512,768]{1,0:T(8,128)(2,1)S(1)}, u32[]{:S(2)}, u32[]{:S(2)}) collective-permute-start(bf16[512,768]{1,0:T(8,128)(2,1)} %add_convert_fusion.3), channel_id=1, source_target_pairs={{0,4},{4,0},{1,5},{5,1},{2,6},{6,2},{3,7},{7,3},{8,12},{12,8},{9,1... | collective-permute-start | bytes 2359304 | tf_op jit(solution)/shard_map/ppermute | solution.py:37
  502.8 6.8 %collective-permute-done.52 = bf16[128,768]{1,0:T(8,128)(2,1)S(1)} collective-permute-done((bf16[128,768]{1,0:T(8,128)(2,1)S(1)}, bf16[128,768]{1,0:T(8,128)(2,1)S(1)}, u32[]{:S(2)}, u32[]{:S(2)}) %collective-permute-start.52) | collective-permute-done | bytes 196640 | tf_op jit(solution)/shard_map/ppermute | solution.py:37
  (696 shorter events, 224.5 us)
Async XLA Ops:
  0.7 31.5 %collective-permute-start.9 = (bf16[256,1024]{1,0:T(8,128)(2,1)}, bf16[256,1024]{1,0:T(8,128)(2,1)S(1)}, u32[]{:S(2)}, u32[]{:S(2)}) collective-permute-start(bf16[256,1024]{1,0:T(8,128)(2,1)} %bitcast.111), channel_id=1, source_target_pairs={{0,4},{1,5},{2,6},{3,7},{8,12},{9,13},{10,14},{11,15},{16,20},{17,... | collective-permute-start | bytes 1572872 | tf_op jit(solution)/shard_map/ppermute | solution.py:43
  6.7 20.1 %collective-permute-start.2 = (bf16[128,768]{1,0:T(8,128)(2,1)S(1)}, bf16[128,768]{1,0:T(8,128)(2,1)S(1)}, u32[]{:S(2)}, u32[]{:S(2)}) collective-permute-start(bf16[128,768]{1,0:T(8,128)(2,1)S(1)} %fusion.82), channel_id=1, source_target_pairs={{0,16},{8,24},{16,0},{24,8},{1,17},{9,25},{17,1},{25,9},{2,18},{10... | collective-permute-start | bytes 589832 | tf_op jit(solution)/shard_map/ppermute | solution.py:37
  11.0 31.1 %collective-permute-start = (bf16[256,1024]{1,0:T(8,128)(2,1)S(1)}, bf16[256,1024]{1,0:T(8,128)(2,1)S(1)}, u32[]{:S(2)}, u32[]{:S(2)}) collective-permute-start(bf16[256,1024]{1,0:T(8,128)(2,1)S(1)} %constant_dynamic-update-slice_fusion), channel_id=1, source_target_pairs={{0,2},{1,3},{2,0},{3,1},{4,6},{5,7},{6,4},{7,5},{8,10},{9,11},{10,... | collective-permute-start | bytes 1572872 | tf_op jit(solution)/shard_map/ppermute | solution.py:37
  39.3 18.2 %collective-permute-start.4 = (bf16[512,768]{1,0:T(8,128)(2,1)S(1)}, bf16[512,768]{1,0:T(8,128)(2,1)S(1)}, u32[]{:S(2)}, u32[]{:S(2)}) collective-permute-start(bf16[512,768]{1,0:T(8,128)(2,1)S(1)} %pad_maximum_fusion.20), channel_id=1, source_target_pairs={{0,4},{4,0},{1,5},{5,1},{2,6},{6,2},{3,7},{7,3},{8,12},{12,8},{9,1... | collective-permute-start | bytes 2359304 | tf_op jit(solution)/shard_map/ppermute | solution.py:37
  42.2 25.6 %collective-permute-start.1 = (bf16[512,1024]{1,0:T(8,128)(2,1)S(1)}, bf16[512,1024]{1,0:T(8,128)(2,1)S(1)}, u32[]{:S(2)}, u32[]{:S(2)}) collective-permute-start(bf16[512,1024]{1,0:T(8,128)(2,1)S(1)} %pad_maximum_fusion.10), channel_id=1, source_target_pairs={{0,1},{1,0},{2,3},{3,2},{4,5},{5,4},{6,7},{7,6},{8,9},{9,8},{10,11... | collective-permute-start | bytes 3145736 | tf_op jit(solution)/shard_map/ppermute | solution.py:37
  53.9 17.0 %collective-permute-start.11 = (bf16[512,1024]{1,0:T(8,128)(2,1)S(1)}, bf16[512,1024]{1,0:T(8,128)(2,1)S(1)}, u32[]{:S(2)}, u32[]{:S(2)}) collective-permute-start(bf16[512,1024]{1,0:T(8,128)(2,1)S(1)} %pad_maximum_fusion.12), channel_id=1, source_target_pairs={{0,1},{1,0},{2,3},{3,2},{4,5},{5,4},{6,7},{7,6},{8,9},{9,8},{10,11... | collective-permute-start | bytes 3145736 | tf_op jit(solution)/shard_map/ppermute | solution.py:37
  57.7 30.2 %collective-permute-start.13 = (bf16[512,256]{0,1:T(8,128)(2,1)S(1)}, bf16[512,256]{0,1:T(8,128)(2,1)}, u32[]{:S(2)}, u32[]{:S(2)}) collective-permute-start(bf16[512,256]{0,1:T(8,128)(2,1)S(1)} %pad_maximum_fusion.26), channel_id=1, source_target_pairs={{0,4},{4,0},{1,5},{5,1},{2,6},{6,2},{3,7},{7,3},{8,12},{12,8},{9,1... | collective-permute-start | bytes 786440 | tf_op jit(solution)/shard_map/ppermute | solution.py:37
  73.1 15.9 %collective-permute-start.12 = (bf16[512,512]{0,1:T(8,128)(2,1)S(1)}, bf16[512,512]{0,1:T(8,128)(2,1)S(1)}, u32[]{:S(2)}, u32[]{:S(2)}) collective-permute-start(bf16[512,512]{0,1:T(8,128)(2,1)S(1)} %get-tuple-element.93), channel_id=1, source_target_pairs={{0,4},{4,0},{1,5},{5,1},{2,6},{6,2},{3,7},{7,3},{8,12},{12,8},{9,1... | collective-permute-start | bytes 1572872 | tf_op jit(solution)/shard_map/ppermute | solution.py:37
  92.8 15.1 %collective-permute-start.15 = (bf16[256,1024]{1,0:T(8,128)(2,1)S(1)}, bf16[256,1024]{1,0:T(8,128)(2,1)S(1)}, u32[]{:S(2)}, u32[]{:S(2)}) collective-permute-start(bf16[256,1024]{1,0:T(8,128)(2,1)S(1)} %slice.1322), channel_id=1, source_target_pairs={{0,2},{1,3},{2,0},{3,1},{4,6},{5,7},{6,4},{7,5},{8,10},{9,11},{10,... | collective-permute-start | bytes 1572872 | tf_op jit(solution)/shard_map/ppermute | solution.py:37
  93.4 14.5 %collective-permute-start.16 = (bf16[128,1024]{1,0:T(8,128)(2,1)S(1)}, bf16[128,1024]{1,0:T(8,128)(2,1)S(1)}, u32[]{:S(2)}, u32[]{:S(2)}) collective-permute-start(bf16[128,1024]{1,0:T(8,128)(2,1)S(1)} %constant_dynamic-slice_fusion), channel_id=1, source_target_pairs={{0,16},{8,24},{16,0},{24,8},{1,17},{9,25},{17,1},{25,9},{2,18},{10... | collective-permute-start | bytes 786440 | tf_op jit(solution)/shard_map/ppermute | solution.py:37
  113.9 21.2 %collective-permute-start.22 = (bf16[256,512]{1,0:T(8,128)(2,1)S(1)}, bf16[256,512]{1,0:T(8,128)(2,1)S(1)}, u32[]{:S(2)}, u32[]{:S(2)}) collective-permute-start(bf16[256,512]{1,0:T(8,128)(2,1)S(1)} %fusion.10), channel_id=1, source_target_pairs={{0,4},{4,0},{1,5},{5,1},{2,6},{6,2},{3,7},{7,3},{8,12},{12,8},{9,1... | collective-permute-start | bytes 786440 | tf_op jit(solution)/shard_map/ppermute | solution.py:37
  124.8 28.7 %collective-permute-start.18 = (bf16[512,1024]{1,0:T(8,128)(2,1)S(1)}, bf16[512,1024]{1,0:T(8,128)(2,1)S(1)}, u32[]{:S(2)}, u32[]{:S(2)}) collective-permute-start(bf16[512,1024]{1,0:T(8,128)(2,1)S(1)} %pad_maximum_fusion.13), channel_id=1, source_target_pairs={{0,1},{1,0},{2,3},{3,2},{4,5},{5,4},{6,7},{7,6},{8,9},{9,8},{10,11... | collective-permute-start | bytes 3145736 | tf_op jit(solution)/shard_map/ppermute | solution.py:37
  124.9 15.1 %collective-permute-start.20 = (bf16[128,1024]{0,1:T(8,128)(2,1)S(1)}, bf16[128,1024]{0,1:T(8,128)(2,1)S(1)}, u32[]{:S(2)}, u32[]{:S(2)}) collective-permute-start(bf16[128,1024]{0,1:T(8,128)(2,1)S(1)} %dynamic-slice_bitcast_fusion), channel_id=1, source_target_pairs={{0,16},{8,24},{16,0},{24,8},{1,17},{9,25},{17,1},{25,9},{2,18},{10... | collective-permute-start | bytes 786440 | tf_op jit(solution)/shard_map/ppermute | solution.py:37
  125.0 21.2 %collective-permute-start.19 = (bf16[256,1024]{1,0:T(8,128)(2,1)S(1)}, bf16[256,1024]{1,0:T(8,128)(2,1)S(1)}, u32[]{:S(2)}, u32[]{:S(2)}) collective-permute-start(bf16[256,1024]{1,0:T(8,128)(2,1)S(1)} %copy-done.59), channel_id=1, source_target_pairs={{0,8},{8,0},{16,24},{24,16},{1,9},{9,1},{17,25},{25,17},{2,10},{10... | collective-permute-start | bytes 1572872 | tf_op jit(solution)/shard_map/ppermute | solution.py:37
  127.9 25.5 %collective-permute-start.21 = (bf16[512,512]{0,1:T(8,128)(2,1)S(1)}, bf16[512,512]{0,1:T(8,128)(2,1)S(1)}, u32[]{:S(2)}, u32[]{:S(2)}) collective-permute-start(bf16[512,512]{0,1:T(8,128)(2,1)S(1)} %copy-done.46), channel_id=1, source_target_pairs={{0,4},{4,0},{1,5},{5,1},{2,6},{6,2},{3,7},{7,3},{8,12},{12,8},{9,1... | collective-permute-start | bytes 1572872 | tf_op jit(solution)/shard_map/ppermute | solution.py:37
  140.1 28.1 %collective-permute-start.24 = (bf16[256,1024]{0,1:T(8,128)(2,1)S(1)}, bf16[256,1024]{0,1:T(8,128)(2,1)S(1)}, u32[]{:S(2)}, u32[]{:S(2)}) collective-permute-start(bf16[256,1024]{0,1:T(8,128)(2,1)S(1)} %constant_dynamic-update-slice_fusion.32), channel_id=1, source_target_pairs={{0,8},{8,0},{16,24},{24,16},{1,9},{9,1},{17,25},{25,17},{2,10},{10... | collective-permute-start | bytes 1572872 | tf_op jit(solution)/shard_map/ppermute | solution.py:37
  146.2 29.8 %collective-permute-start.23 = (bf16[512,1024]{1,0:T(8,128)(2,1)S(1)}, bf16[512,1024]{1,0:T(8,128)(2,1)S(1)}, u32[]{:S(2)}, u32[]{:S(2)}) collective-permute-start(bf16[512,1024]{1,0:T(8,128)(2,1)S(1)} %constant_dynamic-update-slice_fusion.30), channel_id=1, source_target_pairs={{0,4},{4,0},{1,5},{5,1},{2,6},{6,2},{3,7},{7,3},{8,12},{12,8},{9,1... | collective-permute-start | bytes 3145736 | tf_op jit(solution)/shard_map/ppermute | solution.py:37
  196.5 24.1 %collective-permute-start.29 = (bf16[512,1024]{0,1:T(8,128)(2,1)S(1)}, bf16[512,1024]{0,1:T(8,128)(2,1)S(1)}, u32[]{:S(2)}, u32[]{:S(2)}) collective-permute-start(bf16[512,1024]{0,1:T(8,128)(2,1)S(1)} %constant_dynamic-update-slice_fusion.48), channel_id=1, source_target_pairs={{0,4},{4,0},{1,5},{5,1},{2,6},{6,2},{3,7},{7,3},{8,12},{12,8},{9,1... | collective-permute-start | bytes 3145736 | tf_op jit(solution)/shard_map/ppermute | solution.py:37
  232.7 14.0 %collective-permute-start.31 = (bf16[256,1024]{1,0:T(8,128)(2,1)S(1)}, bf16[256,1024]{1,0:T(8,128)(2,1)S(1)}, u32[]{:S(2)}, u32[]{:S(2)}) collective-permute-start(bf16[256,1024]{1,0:T(8,128)(2,1)S(1)} %slice.1320), channel_id=1, source_target_pairs={{0,2},{1,3},{2,0},{3,1},{4,6},{5,7},{6,4},{7,5},{8,10},{9,11},{10,... | collective-permute-start | bytes 1572872 | tf_op jit(solution)/shard_map/ppermute | solution.py:37
  283.9 26.1 %collective-permute-start.60 = (bf16[512,1024]{1,0:T(8,128)(2,1)S(1)}, bf16[512,1024]{1,0:T(8,128)(2,1)S(1)}, u32[]{:S(2)}, u32[]{:S(2)}) collective-permute-start(bf16[512,1024]{1,0:T(8,128)(2,1)S(1)} %convolution_convert_fusion), channel_id=1, source_target_pairs={{0,4},{4,0},{1,5},{5,1},{2,6},{6,2},{3,7},{7,3},{8,12},{12,8},{9,1... | collective-permute-start | bytes 3145736 | tf_op jit(solution)/shard_map/ppermute | solution.py:37
  291.3 55.9 %collective-permute-start.57 = (bf16[512,1024]{1,0:T(8,128)(2,1)}, bf16[512,1024]{1,0:T(8,128)(2,1)}, u32[]{:S(2)}, u32[]{:S(2)}) collective-permute-start(bf16[512,1024]{1,0:T(8,128)(2,1)} %convolution_convert_fusion.1), channel_id=1, source_target_pairs={{0,4},{4,0},{1,5},{5,1},{2,6},{6,2},{3,7},{7,3},{8,12},{12,8},{9,1... | collective-permute-start | bytes 3145736 | tf_op jit(solution)/shard_map/ppermute | solution.py:37
  311.3 30.1 %collective-permute-start.61 = (bf16[256,1024]{1,0:T(8,128)(2,1)}, bf16[256,1024]{1,0:T(8,128)(2,1)}, u32[]{:S(2)}, u32[]{:S(2)}) collective-permute-start(bf16[256,1024]{1,0:T(8,128)(2,1)} %slice.1314), channel_id=1, source_target_pairs={{0,8},{8,0},{16,24},{24,16},{1,9},{9,1},{17,25},{25,17},{2,10},{10... | collective-permute-start | bytes 1572872 | tf_op jit(solution)/shard_map/ppermute | solution.py:37
  361.6 20.8 %collective-permute-start.58 = (bf16[256,1024]{1,0:T(8,128)(2,1)}, bf16[256,1024]{1,0:T(8,128)(2,1)}, u32[]{:S(2)}, u32[]{:S(2)}) collective-permute-start(bf16[256,1024]{1,0:T(8,128)(2,1)} %slice.1315), channel_id=1, source_target_pairs={{0,8},{8,0},{16,24},{24,16},{1,9},{9,1},{17,25},{25,17},{2,10},{10... | collective-permute-start | bytes 1572872 | tf_op jit(solution)/shard_map/ppermute | solution.py:37
  365.2 33.5 %collective-permute-start.43 = (bf16[512,1024]{0,1:T(8,128)(2,1)}, bf16[512,1024]{0,1:T(8,128)(2,1)}, u32[]{:S(2)}, u32[]{:S(2)}) collective-permute-start(bf16[512,1024]{0,1:T(8,128)(2,1)} %pad_maximum_fusion.19), channel_id=1, source_target_pairs={{0,4},{4,0},{1,5},{5,1},{2,6},{6,2},{3,7},{7,3},{8,12},{12,8},{9,1... | collective-permute-start | bytes 3145736 | tf_op jit(solution)/shard_map/ppermute | solution.py:37
  377.8 17.8 %collective-permute-start.40 = (bf16[256,1024]{1,0:T(8,128)(2,1)S(1)}, bf16[256,1024]{1,0:T(8,128)(2,1)S(1)}, u32[]{:S(2)}, u32[]{:S(2)}) collective-permute-start(bf16[256,1024]{1,0:T(8,128)(2,1)S(1)} %get-tuple-element.283), channel_id=1, source_target_pairs={{0,2},{1,3},{2,0},{3,1},{4,6},{5,7},{6,4},{7,5},{8,10},{9,11},{10,... | collective-permute-start | bytes 1572872 | tf_op jit(solution)/shard_map/ppermute | solution.py:37
  384.4 43.7 %collective-permute-start.59 = (bf16[128,1024]{1,0:T(8,128)(2,1)}, bf16[128,1024]{1,0:T(8,128)(2,1)}, u32[]{:S(2)}, u32[]{:S(2)}) collective-permute-start(bf16[128,1024]{1,0:T(8,128)(2,1)} %slice.1325), channel_id=1, source_target_pairs={{0,16},{8,24},{16,0},{24,8},{1,17},{9,25},{17,1},{25,9},{2,18},{10... | collective-permute-start | bytes 786440 | tf_op jit(solution)/shard_map/ppermute | solution.py:37
  414.7 52.0 %collective-permute-start.45 = (bf16[1024,512]{1,0:T(8,128)(2,1)}, bf16[1024,512]{1,0:T(8,128)(2,1)S(1)}, u32[]{:S(2)}, u32[]{:S(2)}) collective-permute-start(bf16[1024,512]{1,0:T(8,128)(2,1)} %constant_dynamic-update-slice_fusion.68), channel_id=1, source_target_pairs={{4,0},{5,1},{6,2},{7,3},{12,8},{13,9},{14,10},{15,11},{20,16},{21,... | collective-permute-start | bytes 3145736 | tf_op jit(solution)/shard_map/ppermute | solution.py:43
  416.2 16.3 %collective-permute-start.44 = (bf16[256,1024]{0,1:T(8,128)(2,1)S(1)}, bf16[256,1024]{0,1:T(8,128)(2,1)S(1)}, u32[]{:S(2)}, u32[]{:S(2)}) collective-permute-start(bf16[256,1024]{0,1:T(8,128)(2,1)S(1)} %slice.1317), channel_id=1, source_target_pairs={{0,8},{8,0},{16,24},{24,16},{1,9},{9,1},{17,25},{25,17},{2,10},{10... | collective-permute-start | bytes 1572872 | tf_op jit(solution)/shard_map/ppermute | solution.py:37
  416.3 38.1 %collective-permute-start.53 = (bf16[512,256]{1,0:T(8,128)(2,1)S(1)}, bf16[512,256]{1,0:T(8,128)(2,1)S(1)}, u32[]{:S(2)}, u32[]{:S(2)}) collective-permute-start(bf16[512,256]{1,0:T(8,128)(2,1)S(1)} %convolution_convert_fusion.10), channel_id=1, source_target_pairs={{0,4},{4,0},{1,5},{5,1},{2,6},{6,2},{3,7},{7,3},{8,12},{12,8},{9,1... | collective-permute-start | bytes 786440 | tf_op jit(solution)/shard_map/ppermute | solution.py:37
  450.9 19.0 %collective-permute-start.56 = (bf16[128,1024]{0,1:T(8,128)(2,1)S(1)}, bf16[128,1024]{0,1:T(8,128)(2,1)S(1)}, u32[]{:S(2)}, u32[]{:S(2)}) collective-permute-start(bf16[128,1024]{0,1:T(8,128)(2,1)S(1)} %slice.1326), channel_id=1, source_target_pairs={{0,16},{8,24},{16,0},{24,8},{1,17},{9,25},{17,1},{25,9},{2,18},{10... | collective-permute-start | bytes 786440 | tf_op jit(solution)/shard_map/ppermute | solution.py:37
  457.2 24.9 %collective-permute-start.50 = (bf16[512,768]{1,0:T(8,128)(2,1)}, bf16[512,768]{1,0:T(8,128)(2,1)S(1)}, u32[]{:S(2)}, u32[]{:S(2)}) collective-permute-start(bf16[512,768]{1,0:T(8,128)(2,1)} %add_convert_fusion.3), channel_id=1, source_target_pairs={{0,4},{4,0},{1,5},{5,1},{2,6},{6,2},{3,7},{7,3},{8,12},{12,8},{9,1... | collective-permute-start | bytes 2359304 | tf_op jit(solution)/shard_map/ppermute | solution.py:37
  486.3 14.8 %collective-permute-start.47 = (bf16[256,1024]{1,0:T(8,128)(2,1)}, bf16[256,1024]{1,0:T(8,128)(2,1)}, u32[]{:S(2)}, u32[]{:S(2)}) collective-permute-start(bf16[256,1024]{1,0:T(8,128)(2,1)} %slice.1316), channel_id=1, source_target_pairs={{0,2},{1,3},{2,0},{3,1},{4,6},{5,7},{6,4},{7,5},{8,10},{9,11},{10,... | collective-permute-start | bytes 1572872 | tf_op jit(solution)/shard_map/ppermute | solution.py:37
  (190 other events, 1616.8 us)

commit v3 on v2

v3 whole, which is shorter than its diff:
```python
from functools import partial

import jax
import jax.numpy as jnp
from jax import lax
from jax.experimental import pallas as pl
from jax.experimental.pallas import tpu as pltpu
from jax.sharding import PartitionSpec as P

HDIM = 64
W = 1024
TILE = 256


EPSILON = 1e-05
NEGATIVE = -1e30
VMEM = 32 * 1024 * 1024


def matmul(left, right):
    return jnp.dot(left, right, preferred_element_type=jnp.float32)


def contract(form, left, right):
    return jnp.einsum(form, left, right, preferred_element_type=jnp.float32)


def low(value):
    return value.astype(jnp.bfloat16)


def wide(value):
    return value.astype(jnp.float32)


def swap(array, axis, bit):
    return lax.ppermute(array, axis, [(i, i ^ bit) for i in range(lax.axis_size(axis))])


def shift(array, axis, by):
    count = lax.axis_size(axis)
    pairs = [(i, i + by) for i in range(count) if 0 <= i + by < count]
    return lax.ppermute(array, axis, pairs)


def steps_of(*axes):
    steps = []
    for axis in axes:
        bit = lax.axis_size(axis) // 2
        while bit:
            steps.append((axis, bit))
            bit //= 2
    return steps


def after(value, *others):
    others = [other for other in others if other is not None]
    return lax.optimization_barrier((value, *others))[0] if others else value


def gather_tree(array, steps, start=None, used=None):
    for n, (axis, bit) in enumerate(steps):
        arrived = swap(after(array, start if n == 0 else None), axis, bit)
        array = jnp.concatenate([after(array, used if n == len(steps) - 1 else None), arrived])
    return array


def scatter_more(total, steps, start=None, used=None):
    for n, (axis, bit) in enumerate(reversed(steps)):
        half = total.shape[0] // 2
        arrived = swap(after(low(total[half:]), start if n == 0 else None), axis, bit)
        kept = after(total[:half], used if n == len(steps) - 1 else None)
        total = kept + wide(arrived)
    return total


def scatter_tree(make, size, steps, used=None):
    axis, bit = steps[-1]
    half = size // 2
    arrived = swap(low(make(slice(half, size))), axis, bit)
    total = after(make(slice(0, half)), used) + wide(arrived)
    return scatter_more(total, steps[:-1])


def all_sum(value, steps):
    for axis, bit in steps:
        value = value + swap(value, axis, bit)
    return value


def flat_bit(step, axes):
    axis, bit = step
    for other in axes[axes.index(axis) + 1 :]:
        bit = bit * lax.axis_size(other)
    return bit


def masks_of(axes, steps):
    masks = [0]
    for step in steps:
        masks = masks + [m | flat_bit(step, axes) for m in masks]
    return masks


def cross_over(blocks, axes):
    index = lax.axis_index(axes)
    bit = 1
    while bit < len(blocks):
        odd = (index & bit) != 0
        blocks = [jnp.where(odd, blocks[m ^ bit], blocks[m]) for m in range(len(blocks))]
        bit *= 2
    return blocks


def split(array, dim, count):
    size = array.shape[dim] // count
    return [lax.slice_in_dim(array, m * size, (m + 1) * size, axis=dim) for m in range(count)]


def to_tree(array, dim, axes, steps):
    masks = masks_of(axes, steps)
    blocks = cross_over(split(array, dim, len(masks)), axes)
    return jnp.concatenate([blocks[m] for m in masks], axis=dim)


def from_tree(array, dim, axes, steps):
    masks = masks_of(axes, steps)
    blocks = split(array, dim, len(masks))
    blocks = cross_over([blocks[masks.index(m)] for m in range(len(masks))], axes)
    return jnp.concatenate(blocks, axis=dim)


def in_tree(block, bits):
    return sum(((block >> k) & 1) << (bits - 1 - k) for k in range(bits))


def stack_heads(value, heads, turned):
    feature = lax.broadcasted_iota(jnp.int32, value.shape, 0 if turned else 1) // HDIM
    zero = jnp.zeros_like(value)
    parts = [jnp.where(feature == h, value, zero) for h in range(heads)]
    return jnp.concatenate(parts, axis=1 if turned else 0)


def allowed_in(lower, query, key_start, count):
    key = key_start + lax.broadcasted_iota(jnp.int32, (count, lower.shape[1]), 0)
    return (key >= lower) & (key <= query)


def along_heads(row, heads):
    return jnp.concatenate([row] * heads, axis=1)


def tile_of(ref, index, count, columns=None):
    rows = pl.ds(pl.multiple_of(index * count, count), count)
    return ref[rows, :] if columns is None else ref[rows, columns]


def lanes_of(index, count):
    return pl.ds(pl.multiple_of(index * count, count), count)


def attend_kernel(width, masked, *refs):
    if masked:
        meta, lower_ref, source_ref, old_ref, mixed_ref, mixed_t_ref, lse_ref, acc_ref = refs
        query_ref, first = source_ref, width
    else:
        query_ref, source_ref, mixed_ref, mixed_t_ref, lse_ref, acc_ref = refs
        first = 0
    heads, count = width // HDIM, TILE
    steps = mixed_ref.shape[0] // count
    bits = steps.bit_length() - 1

    @pl.loop(0, steps)
    def _(step):
        stacked = stack_heads(tile_of(query_ref, step, count, slice(0, width)).T, heads, True)
        acc_ref[...] = jnp.zeros_like(acc_ref)
        if masked:
            tile = in_tree(step, bits) ^ meta[0]
            lower = along_heads(lower_ref[:, lanes_of(step, count)], heads)
            place_of = tile * count + lax.broadcasted_iota(jnp.int32, (1, count), 1)
            place_of = along_heads(place_of, heads)

        def add(carry, ref, column, place, key_tile, masking, size=count):
            keys = tile_of(ref, place, size, slice(column, column + width))
            values_t = tile_of(ref, place, size, slice(column + width, column + 2 * width)).T
            top, total = carry
            scores = matmul(keys, stacked)
            if masking:
                ok = allowed_in(lower, place_of, key_tile * count, count)
                scores = jnp.where(ok, scores, NEGATIVE)
            higher = jnp.maximum(top, jnp.max(scores, axis=0, keepdims=True))
            expo = jnp.exp(scores - higher)
            scale = jnp.exp(top - higher)
            total = total * scale + jnp.sum(expo, axis=0, keepdims=True)
            expo = low(expo)
            for h in range(heads):
                part, lanes = slice(h * HDIM, (h + 1) * HDIM), slice(h * count, (h + 1) * count)
                acc_ref[part, :] = acc_ref[part, :] * scale[:, lanes] + matmul(
                    values_t[part, :], expo[:, lanes]
                )
            return higher, total

        carry = (
            jnp.full((1, heads * count), NEGATIVE, jnp.float32),
            jnp.zeros((1, heads * count), jnp.float32),
        )
        if masked:
            least = meta[1 + step]
            here = lambda n, c: add(
                c, source_ref, first, in_tree((tile - n) ^ meta[0], bits), tile - n, True
            )
            carry = lax.fori_loop(0, tile - jnp.maximum(least, 0) + 1, here, carry)
            before = lambda n, c: add(
                c, old_ref, 0, in_tree((n + steps) ^ meta[0], bits), n, True
            )
            carry = lax.fori_loop(least, 0, before, carry)
        else:
            every = lambda n, c: add(c, source_ref, first, n, n, False, 2 * count)
            carry = lax.fori_loop(0, source_ref.shape[0] // (2 * count), every, carry)
        top, total = carry
        lse = top + jnp.log(total)
        whole = lanes_of(step, count)
        for h in range(heads):
            part, lanes = slice(h * HDIM, (h + 1) * HDIM), slice(h * count, (h + 1) * count)
            acc_ref[part, :] = acc_ref[part, :] / total[:, lanes]
            lse_ref[h : h + 1, whole] = lse[:, lanes]
        mixed_t_ref[:, whole] = acc_ref[...]
        mixed_ref[whole, :] = low(acc_ref[...].T)


def attend_back_kernel(width, kind, *refs):
    refs = list(refs)
    masked, old = kind != "cross", kind == "old"
    if masked:
        meta, lower_ref = refs.pop(0), refs.pop(0)
    start_ref = refs.pop(0) if kind == "own" else None
    query_ref = refs.pop(0)
    grad_ref, mixed_t_ref, lse_ref = refs[:3]
    refs = refs[3:]
    source_ref = query_ref if kind == "own" else refs.pop(0)
    first = width if kind == "own" else 0
    grad_query_ref, grad_kv_ref, keys_acc, values_acc, query_acc = refs
    heads, count = width // HDIM, TILE
    steps = grad_ref.shape[0] // count
    bits = steps.bit_length() - 1
    keys_acc[...] = jnp.zeros_like(keys_acc)
    values_acc[...] = jnp.zeros_like(values_acc)

    def of_queries(step):
        whole = lanes_of(step, count)
        query = tile_of(query_ref, step, count, slice(0, width))
        grad = tile_of(grad_ref, step, count)
        grad_t = grad.T
        stacked = stack_heads(query, heads, False)
        stacked_t = stack_heads(query.T, heads, True)
        stacked_grad = stack_heads(grad, heads, False)
        stacked_grad_t = stack_heads(grad_t, heads, True)
        weighed = wide(grad_t) * mixed_t_ref[:, whole]
        lse = jnp.concatenate([lse_ref[h : h + 1, whole] for h in range(heads)], axis=1)
        inner = jnp.concatenate(
            [
                jnp.sum(weighed[h * HDIM : (h + 1) * HDIM, :], axis=0, keepdims=True)
                for h in range(heads)
            ],
            axis=1,
        )
        if masked:
            tile = in_tree(step, bits) ^ meta[0]
            lower = along_heads(lower_ref[:, whole], heads)
            place_of = tile * count + lax.broadcasted_iota(jnp.int32, (1, count), 1)
            place_of = along_heads(place_of, heads)

        def add(place, key_tile, size=count):
            rows = pl.ds(pl.multiple_of(place * size, size), size)
            keys = source_ref[rows, first : first + width]
            values = source_ref[rows, first + width : first + 2 * width]
            keys_t = keys.T
            probs = jnp.exp(matmul(keys, stacked_t) - lse)
            if masked:
                ok = allowed_in(lower, place_of, key_tile * count, count)
                probs = jnp.where(ok, probs, 0.0)
            slopes = low(probs * (matmul(values, stacked_grad_t) - inner))
            values_acc[rows, :] += matmul(low(probs), stacked_grad)
            keys_acc[rows, :] += matmul(slopes, stacked)
            for h in range(heads):
                part, lanes = slice(h * HDIM, (h + 1) * HDIM), slice(h * count, (h + 1) * count)
                query_acc[part, :] += matmul(keys_t[part, :], slopes[:, lanes])

        if not masked:
            pl.loop(0, source_ref.shape[0] // (2 * count))(lambda n: add(n, n, 2 * count))
        elif old:
            pl.loop(meta[1 + step], 0)(lambda n: add(in_tree((n + steps) ^ meta[0], bits), n))
        else:
            pl.loop(jnp.maximum(meta[1 + step], 0), tile + 1)(
                lambda n: add(in_tree(n ^ meta[0], bits), n)
            )

    @pl.loop(0, steps)
    def _(step):
        whole = lanes_of(step, count)
        if start_ref is None:
            query_acc[...] = jnp.zeros_like(query_acc)
        else:
            query_acc[...] = start_ref[:, whole]
        if old:
            pl.when(meta[1 + step] < 0)(lambda: of_queries(step))
            grad_query_ref[:, whole] = query_acc[...]
        else:
            of_queries(step)
            grad_query_ref[whole, :] = low(query_acc[...].T)

    grad_kv_ref[:, :width] = keys_acc[...].astype(grad_kv_ref.dtype)
    grad_kv_ref[:, width:] = values_acc[...].astype(grad_kv_ref.dtype)


IN_VMEM = pl.BlockSpec(memory_space=pltpu.VMEM)
IN_SMEM = pl.BlockSpec(memory_space=pltpu.SMEM)


def attend(width, query, source, meta=None, lower=None, old=None):
    rows = query.shape[0]
    heads = width // HDIM
    masked = old is not None
    inputs = [meta, lower, source, old] if masked else [query, source]
    specs = [IN_SMEM if masked else IN_VMEM] + [IN_VMEM] * (len(inputs) - 1)
    pairs = rows * source.shape[0] * width
    return pl.pallas_call(
        partial(attend_kernel, width, masked),
        in_specs=specs,
        out_specs=[IN_VMEM] * 3,
        out_shape=[
            jax.ShapeDtypeStruct((rows, width), jnp.bfloat16),
            jax.ShapeDtypeStruct((width, rows), jnp.float32),
            jax.ShapeDtypeStruct((heads, rows), jnp.float32),
        ],
        scratch_shapes=[pltpu.VMEM((width, TILE), jnp.float32)],
        compiler_params=pltpu.CompilerParams(vmem_limit_bytes=VMEM),
        cost_estimate=pl.CostEstimate(
            flops=48 * pairs, bytes_accessed=8 * rows * width, transcendentals=0
        ),
    )(*inputs)


def attend_back(width, kind, query, grad, mixed_t, lse, source=None, meta=None, lower=None, start=None):
    rows = grad.shape[0]
    inputs = [] if kind == "cross" else [meta, lower]
    inputs += [start] if kind == "own" else []
    inputs += [query, grad, mixed_t, lse] + ([] if kind == "own" else [source])
    specs = [IN_VMEM] * len(inputs)
    if kind != "cross":
        specs[0] = IN_SMEM
    count = (query if kind == "own" else source).shape[0]
    pairs = rows * count * width
    return pl.pallas_call(
        partial(attend_back_kernel, width, kind),
        in_specs=specs,
        out_specs=[IN_VMEM] * 2,
        out_shape=[
            jax.ShapeDtypeStruct((width, rows), jnp.float32)
            if kind == "old"
            else jax.ShapeDtypeStruct((rows, width), jnp.bfloat16),
            jax.ShapeDtypeStruct(
                (count, 2 * width), jnp.float32 if kind == "cross" else jnp.bfloat16
            ),
        ],
        scratch_shapes=[
            pltpu.VMEM((count, width), jnp.float32),
            pltpu.VMEM((count, width), jnp.float32),
            pltpu.VMEM((width, TILE), jnp.float32),
        ],
        compiler_params=pltpu.CompilerParams(vmem_limit_bytes=VMEM),
        cost_estimate=pl.CostEstimate(
            flops=64 * pairs, bytes_accessed=16 * rows * width, transcendentals=0
        ),
    )(*inputs)


def layer_norm(value, gain, shift_by):
    centre = value - jnp.mean(value, axis=-1, keepdims=True)
    rstd = lax.rsqrt(jnp.mean(centre * centre, axis=-1, keepdims=True) + EPSILON)
    normed = centre * rstd
    return (normed * gain + shift_by, normed, rstd)


def norm_back(grad_out, normed, rstd, gain):
    scaled = grad_out * gain
    inner = scaled - jnp.mean(scaled, axis=-1, keepdims=True)
    inner = inner - normed * jnp.mean(scaled * normed, axis=-1, keepdims=True)
    return (rstd * inner, jnp.sum(grad_out * normed, axis=0), jnp.sum(grad_out, axis=0))


def gelu_and_slope(value):
    phi = 0.5 * (1.0 + lax.erf(value * 0.7071067811865476))
    bell = jnp.exp(-0.5 * value * value) * 0.3989422804014327
    return value * phi, phi + value * bell


def column_sum(value):
    return jnp.sum(wide(value), axis=0)


def per_device(
    inputs,
    encoded,
    doc_lengths,
    cotangent,
    query_weight,
    key_weight,
    value_weight,
    out_weight,
    memory_query,
    memory_key,
    memory_value,
    memory_out,
    up_weight,
    down_weight,
    query_bias,
    value_bias,
    memory_qbias,
    memory_vbias,
    up_bias,
    out_bias,
    memory_obias,
    down_bias,
    gain_self,
    shift_self,
    gain_memory,
    shift_memory,
    gain_dense,
    shift_dense,
):
    tp_index = lax.axis_index("tp")
    share_rows = inputs.shape[1]
    rows = share_rows * lax.axis_size("tp")
    width = query_weight.shape[1]
    base = lax.axis_index("ctx") * rows
    row_steps = steps_of("tp")
    weight_steps = steps_of("shard", "ctx")
    features = ("shard", "ctx")

    def turned(array, dim):
        return to_tree(array, dim, features, weight_steps)

    def turned_back(array, dim):
        return from_tree(array, dim, features, weight_steps)

    def gather_rows(piece):
        return gather_tree(piece, row_steps)

    def scatter_rows(make):
        return scatter_tree(make, rows, row_steps)

    def own_half(weight):
        part = weight.shape[0] // lax.axis_size("ctx")
        return lax.dynamic_slice_in_dim(weight, lax.axis_index("ctx") * part, part, 0)

    ctx_steps = steps_of("ctx")
    far_steps, near_steps = steps_of("shard")[:-1], steps_of("shard")[-1:]
    share = turned(inputs[0], 1)
    old_share = turned(shift(inputs[0], "ctx", 1), 1)
    inputs_rows = gather_rows(share)
    old_rows = gather_rows(old_share)
    qkv_own = own_half(jnp.concatenate([query_weight, key_weight, value_weight], axis=1))
    qkv_far = gather_tree(qkv_own, far_steps)
    qkv_near = gather_tree(qkv_far, near_steps)
    qkv_full = gather_tree(qkv_near, ctx_steps)
    out_far = gather_tree(own_half(out_weight.T), far_steps, qkv_far)
    out_near = gather_tree(out_far, near_steps, qkv_near)
    small_own = jnp.concatenate([memory_key, memory_value, memory_query, memory_out.T], axis=1)
    small_far = gather_tree(own_half(small_own), far_steps, qkv_near)
    up_own = own_half(up_weight)
    down_own = own_half(down_weight.T)
    states = to_tree(turned(encoded[0], 1), 0, ("tp",), row_steps)
    vectors = turned(
        jnp.stack(
            [
                out_bias,
                memory_obias,
                down_bias,
                gain_self,
                shift_self,
                gain_memory,
                shift_memory,
                gain_dense,
                shift_dense,
            ]
        ),
        1,
    )
    (
        out_bias,
        memory_obias,
        down_bias,
        gain_self,
        shift_self,
        gain_memory,
        shift_memory,
        gain_dense,
        shift_dense,
    ) = [vectors[i] for i in range(9)]
    upstream = wide(turned(cotangent[0], 1))

    ends = jnp.cumsum(doc_lengths[0], dtype=jnp.int32)
    masks = jnp.asarray(masks_of(("tp",), row_steps), jnp.int32)
    starts = (masks ^ tp_index) * share_rows
    place = base + (starts[:, None] + jnp.arange(share_rows, dtype=jnp.int32)).reshape(-1)
    opens = jnp.max(jnp.where(place[:, None] >= ends[None, :], ends[None, :], 0), axis=1)
    lower = jnp.maximum(opens, place - (W - 1)) - base
    least = lower.reshape(-1, TILE)[:, 0] // TILE
    meta = jnp.concatenate([tp_index[None].astype(jnp.int32), least])
    lower = lower[None, :]

    zeros = jnp.zeros_like(query_bias)
    qkv = low(
        (matmul(inputs_rows, qkv_full) + jnp.concatenate([query_bias, zeros, value_bias]))
        * jnp.concatenate([zeros + 0.125, zeros + 1.0, zeros + 1.0])
    )
    old_kv = low(matmul(old_rows, qkv_full[:, width:]) + jnp.concatenate([zeros, value_bias]))
    small_near = gather_tree(small_far, near_steps, None, qkv)
    qkv = after(qkv, out_near, small_near)
    mixed, mixed_t, self_lse = attend(width, qkv, qkv, meta, lower, old_kv)
    out_full = gather_tree(out_near, ctx_steps, qkv_full, mixed)
    mkv_full = gather_tree(small_near[:, : 2 * width], ctx_steps, None, mixed)
    up_far = gather_tree(up_own, far_steps, small_near, mixed)
    mixed = after(mixed, mkv_full, up_far)
    attn_part = scatter_tree(
        lambda s: contract("rk,dk->rd", mixed[s], out_full), rows, row_steps[-1:]
    )

    mkv_own = low(
        matmul(states, after(mkv_full, attn_part)) + jnp.concatenate([zeros, memory_vbias])
    )

    def weight_terms(*pairs):
        def make(s):
            return jnp.concatenate(
                [contract("rd,rk->dk", left[:, s], right) for left, right in pairs], axis=1
            )

        return make

    model = share.shape[1]

    attn_share = scatter_more(attn_part, row_steps[:-1])
    first, normed_one, rstd_one = layer_norm(
        wide(share) + attn_share + out_bias, gain_self, shift_self
    )
    up_near = gather_tree(up_far, near_steps, mixed, attn_part)
    down_far = gather_tree(down_own, far_steps, mixed, attn_part)
    mkv = gather_tree(mkv_own, ctx_steps)
    small_full = gather_tree(small_near[:, 2 * width :], ctx_steps, mixed, attn_part)
    first_low = after(low(first), up_near, down_far, mkv, small_full)
    mquery_full, mout_full = small_full[:, :width], small_full[:, width:]
    first_rows = gather_rows(first_low)
    down_near = gather_tree(down_far, near_steps, first_low, first_rows)
    mquery = low((matmul(first_rows, mquery_full) + memory_qbias) * 0.125)
    mquery = after(mquery, down_near)
    cross_mixed, cross_mixed_t, cross_lse = attend(width, mquery, mkv)
    up_full = gather_tree(up_near, ctx_steps, first_low, cross_mixed)
    cross_part = scatter_tree(
        lambda s: contract("rk,dk->rd", cross_mixed[s], mout_full), rows, row_steps[-1:]
    )
    cross_part = after(cross_part, up_full)
    cross_share = scatter_more(cross_part, row_steps[:-1])
    second, normed_two, rstd_two = layer_norm(
        first + cross_share + memory_obias, gain_memory, shift_memory
    )
    second_low = low(second)
    down_full = gather_tree(down_near, ctx_steps, cross_part, second_low)
    second_rows = after(gather_rows(second_low), down_full)
    act, slope = gelu_and_slope(matmul(second_rows, up_full) + up_bias)
    act_low, slope_low = low(act), low(slope)
    dense_share = scatter_rows(lambda s: contract("rf,df->rd", act_low[s], down_full))
    result, normed_three, rstd_three = layer_norm(
        second + dense_share + down_bias, gain_dense, shift_dense
    )
    grad_three, gain_dense_grad, shift_dense_grad = norm_back(
        upstream, normed_three, rstd_three, gain_dense
    )
    dense_low = low(grad_three)
    dense_rows = gather_rows(dense_low)
    hidden_low = low(matmul(dense_rows, down_full) * wide(slope_low))
    second_share = scatter_rows(lambda s: contract("rf,df->rd", hidden_low[s], up_full))
    grad_two, gain_memory_grad, shift_memory_grad = norm_back(
        grad_three + second_share, normed_two, rstd_two, gain_memory
    )

    cross_low = low(grad_two)
    cross_rows = gather_rows(cross_low)
    down_part = scatter_tree(weight_terms((dense_rows, act_low)), model, ctx_steps, cross_rows)
    grad_cross_mixed = low(matmul(cross_rows, mout_full))
    mquery_back, mkv_sum = attend_back(
        width, "cross", mquery, grad_cross_mixed, cross_mixed_t, cross_lse, mkv
    )
    mquery_pre = mquery_back * 0.125
    down_near_grad = scatter_more(down_part, near_steps, None, mquery_pre)
    up_part = scatter_tree(weight_terms((second_rows, hidden_low)), model, ctx_steps, mquery_pre)
    first_part = scatter_tree(
        lambda s: contract("rk,dk->rd", mquery_pre[s], mquery_full), rows, row_steps[-1:]
    )
    first_share = scatter_more(first_part, row_steps[:-1])
    grad_one, gain_self_grad, shift_self_grad = norm_back(
        grad_two + first_share, normed_one, rstd_one, gain_self
    )
    self_low = low(grad_one)
    self_rows = gather_rows(self_low)
    down_grads = scatter_more(down_near_grad, far_steps, first_part, self_low)
    up_near_grad = scatter_more(up_part, near_steps, first_part, self_low)
    up_grads = scatter_more(up_near_grad, far_steps, None, self_rows)
    mkv_back = after(mkv_sum, first_part)
    mkv_low = low(scatter_tree(lambda s: mkv_back[s], mkv_back.shape[0], ctx_steps))
    encoded_grad = scatter_tree(
        lambda s: contract("ek,dk->ed", mkv_low[s], mkv_full), states.shape[0], row_steps
    )
    small_part = scatter_tree(
        weight_terms((states, mkv_low), (first_rows, mquery_pre), (cross_rows, cross_mixed)),
        model,
        ctx_steps,
        self_rows,
    )
    grad_self = after(low(matmul(self_rows, out_full)), small_part)

    query_start, old_back = attend_back(
        width, "old", qkv, grad_self, mixed_t, self_lse, old_kv, meta, lower
    )
    back = shift(old_back, "ctx", -1)
    small_near_grads = scatter_more(small_part, near_steps, None, old_back)
    grad_self_later = after(grad_self, small_near_grads, query_start)
    query_back, kv_back = attend_back(
        width, "own", qkv, grad_self_later, mixed_t, self_lse, None, meta, lower, query_start
    )
    query_pre = query_back * 0.125
    small_grads = scatter_more(small_near_grads, far_steps, None, query_pre)
    own_back = jnp.concatenate([query_pre, kv_back], axis=1)

    def qkv_terms(s):
        own = contract("rd,rk->dk", inputs_rows[:, s], own_back)
        old = contract("rd,rk->dk", old_rows[:, s], old_back)
        return own + jnp.pad(old, ((0, 0), (width, 0)))

    kv_all = low(wide(kv_back) + wide(back))

    def inputs_term(s):
        term = contract("rk,dk->rd", query_pre[s], qkv_full[:, :width])
        return term + contract("rk,dk->rd", kv_all[s], qkv_full[:, width:])

    inputs_part = scatter_tree(inputs_term, rows, row_steps[-1:])
    inputs_grad = grad_one + scatter_more(inputs_part, row_steps[:-1])
    sent = low(inputs_part[inputs_part.shape[0] // 2 :])
    qkv_grads = scatter_more(
        scatter_tree(qkv_terms, model, ctx_steps, sent), weight_steps[: -len(ctx_steps)]
    )
    out_part = scatter_tree(weight_terms((self_rows, mixed)), model, ctx_steps, sent)
    out_grads = scatter_more(out_part, steps_of("shard"))

    everywhere = jnp.stack(
        [
            column_sum(self_low),
            column_sum(cross_low),
            column_sum(dense_low),
            gain_self_grad,
            shift_self_grad,
            gain_memory_grad,
            shift_memory_grad,
            gain_dense_grad,
            shift_dense_grad,
        ]
    )
    everywhere = all_sum(turned_back(everywhere, 1), row_steps)
    by_heads = jnp.concatenate(
        [
            column_sum(query_pre),
            column_sum(kv_back[:, width:]) + column_sum(old_back[:, width:]),
            column_sum(mquery_pre),
            column_sum(mkv_low[:, width:]),
            column_sum(hidden_low),
        ]
    )
    lanes = 128
    sums = all_sum(
        after(
            jnp.concatenate([everywhere.reshape(-1, lanes), by_heads.reshape(-1, lanes)], axis=0),
            sent,
        ),
        weight_steps,
    )
    cut = everywhere.size // lanes
    totals = sums[:cut].reshape(everywhere.shape)
    head_totals = sums[cut:].reshape(-1)
    return (
        turned_back(low(result), 1)[None],
        turned_back(inputs_grad, 1)[None],
        turned_back(encoded_grad, 1)[None],
        qkv_grads[:, :width],
        qkv_grads[:, width : 2 * width],
        qkv_grads[:, 2 * width :],
        out_grads.T,
        small_grads[:, 2 * width : 3 * width],
        small_grads[:, :width],
        small_grads[:, width : 2 * width],
        small_grads[:, 3 * width :].T,
        up_grads,
        down_grads.T,
        head_totals[:width],
        head_totals[width : 2 * width],
        head_totals[2 * width : 3 * width],
        head_totals[3 * width : 4 * width],
        head_totals[4 * width :],
        totals[0],
        totals[1],
        totals[2],
        totals[3],
        totals[4],
        totals[5],
        totals[6],
        totals[7],
        totals[8],
    )


def solution(mesh):
    placed = (
        P("shard", ("ctx", "tp"), None),
        P("shard", "ctx", None),
        P("shard", None),
        P("shard", ("ctx", "tp"), None),
        P("shard", "tp"),
        P("shard", "tp"),
        P("shard", "tp"),
        P("tp", "shard"),
        P("shard", "tp"),
        P("shard", "tp"),
        P("shard", "tp"),
        P("tp", "shard"),
        P("shard", "tp"),
        P("tp", "shard"),
        P("tp"),
        P("tp"),
        P("tp"),
        P("tp"),
        P("tp"),
        P(),
        P(),
        P(),
        P(),
        P(),
        P(),
        P(),
        P(),
        P(),
    )
    return jax.shard_map(
        per_device,
        mesh=mesh,
        in_specs=placed,
        out_specs=(
            P("shard", ("ctx", "tp"), None),
            P("shard", ("ctx", "tp"), None),
            P("shard", ("ctx", "tp"), None),
            P(("shard", "ctx"), "tp"),
            P(("shard", "ctx"), "tp"),
            P(("shard", "ctx"), "tp"),
            P("tp", ("shard", "ctx")),
            P(("shard", "ctx"), "tp"),
            P(("shard", "ctx"), "tp"),
            P(("shard", "ctx"), "tp"),
            P("tp", ("shard", "ctx")),
            P(("shard", "ctx"), "tp"),
            P("tp", ("shard", "ctx")),
            P("tp"),
            P("tp"),
            P("tp"),
            P("tp"),
            P("tp"),
            P(),
            P(),
            P(),
            P(),
            P(),
            P(),
            P(),
            P(),
            P(),
        ),
        check_vma=False,
    )
```

time: 517 us -> 444 us (0.86)
  Pallas kernels: 62.9 us -> 30.5 us
  starting transfers between devices: 90.9 us -> 72.9 us
  other arithmetic: 61.3 us -> 52.9 us
  matrix products: 58.8 us -> 51.4 us
  local copies, waits for them, and re-layouts: 38.9 us -> 32.9 us
    pallas_call x5, Pallas kernels: 62.9 us -> 30.5 us  [the longest x3 17.9 us: attend_back(): pl.pallas_call(partial(attend_back_kernel, width, kind), in_specs=specs,...]
    ppermute x66, starting transfers between devices: 84.4 us -> 66.3 us  [swap(): lax.ppermute(array, axis, [(i, i ^ bit) for i in range(lax.axis_size(axis...]
    concatenate x21 -> x20, other arithmetic: 11.7 us -> 18.3 us  [gather_tree(): jnp.concatenate([after(array, used if n == len(steps) - 1 else None), arr...]
    unnamed x320 -> x239, local copies, waits for them, and re-layouts: 19.5 us -> 20 us
  transfers between devices with their start and end apart: 68 -> 68, of which waited for: 34 -> 35; matrix products, arithmetic and copies ran while one was open for 24% -> 24% of each run, Pallas kernels for 12% -> 7%
where the time goes in v3:
time: 444 us; the launch traced here: 436 us
  waiting for transfers between devices  191 us (43%)
  starting transfers between devices  72.9 us (16%)
  other arithmetic  52.9 us (12%)
  matrix products  51.4 us (12%)
  local copies, waits for them, and re-layouts  32.9 us (7%)
  Pallas kernels  30.5 us (7%)
    ppermute x66, waiting for transfers between devices, swap(): lax.ppermute(array, axis, [(i, i ^ bit) for i in range(lax.axis_size(axis...  191 us
    ppermute x66, starting transfers between devices, swap(): lax.ppermute(array, axis, [(i, i ^ bit) for i in range(lax.axis_size(axis...  66.3 us
    dot_general x32, matrix products, contract(): return jnp.einsum(form, left, right, preferred_element_type=jnp.float32)  31.2 us
    dot_general x8, matrix products, matmul(): return jnp.dot(left, right, preferred_element_type=jnp.float32)  20.3 us
    unnamed x239, local copies, waits for them, and re-layouts  20 us
    concatenate x20, other arithmetic, gather_tree(): jnp.concatenate([after(array, used if n == len(steps) - 1 else None), arr...  18.3 us
    pallas_call x3, Pallas kernels, attend_back(): pl.pallas_call(partial(attend_back_kernel, width, kind), in_specs=specs,...  17.9 us
    pallas_call x2, Pallas kernels, attend(): pl.pallas_call(partial(attend_kernel, width, masked), in_specs=specs, out...  12.5 us
  transfers between devices with their start and end apart: 68, of which 35 were waited for; matrix products, arithmetic and copies ran while one was open for 24% of the time, Pallas kernels for 7%

profile of v3, /device:TPU:0, one launch (start us, length us, event | category | flops | bytes accessed | tf_op | source)
XLA Modules:
  0.0 435.6 jit_solution(17331199809383389355)
XLA Ops:
  0.7 5.0 %collective-permute-start.9 = (bf16[256,1024]{1,0:T(8,128)(2,1)}, bf16[256,1024]{1,0:T(8,128)(2,1)S(1)}, u32[]{:S(2)}, u32[]{:S(2)}) collective-permute-start(bf16[256,1024]{1,0:T(8,128)(2,1)} %bitcast.112), channel_id=1, source_target_pairs={{0,4},{1,5},{2,6},{3,7},{8,12},{9,13},{10,14},{11,15},{16,20},{17,... | collective-permute-start | bytes 1572872 | tf_op jit(solution)/shard_map/ppermute | solution.py:43
  30.0 6.9 %collective-permute-done.3 = bf16[256,768]{1,0:T(8,128)(2,1)S(1)} collective-permute-done((bf16[256,768]{1,0:T(8,128)(2,1)S(1)}, bf16[256,768]{1,0:T(8,128)(2,1)S(1)}, u32[]{:S(2)}, u32[]{:S(2)}) %collective-permute-start.3) | collective-permute-done | bytes 393248 | tf_op jit(solution)/shard_map/ppermute | solution.py:37
  42.2 5.4 %collective-permute-done.6 = bf16[256,256]{0,1:T(8,128)(2,1)} collective-permute-done((bf16[256,256]{0,1:T(8,128)(2,1)}, bf16[256,256]{0,1:T(8,128)(2,1)}, u32[]{:S(2)}, u32[]{:S(2)}) %collective-permute-start.6) | collective-permute-done | bytes 131104 | tf_op jit(solution)/shard_map/ppermute | solution.py:37
  48.5 3.9 collective-permute-done.7
  57.4 3.6 multiply_convert_fusion.2.refs_2_.refs_3_
  61.1 5.6 %collective-permute-done.8 = bf16[256,1024]{0,1:T(8,128)(2,1)S(1)} collective-permute-done((bf16[256,1024]{0,1:T(8,128)(2,1)S(1)}, bf16[256,1024]{0,1:T(8,128)(2,1)S(1)}, u32[]{:S(2)}, u32[]{:S(2)}) %collective-permute-start.8) | collective-permute-done | bytes 524320 | tf_op jit(solution)/shard_map/ppermute | solution.py:37
  71.5 8.1 %shard_map.484 = (bf16[1024,256]{1,0:T(8,128)(2,1)S(1)}, f32[256,1024]{1,0:T(8,128)S(1)}, f32[4,1024]{1,0:T(4,128)S(1)}) custom-call(s32[5]{0:T(128)S(1)} %pad_add_fusion.1.refs_0_, s32[1,1024]{1,0:T(1,128)S(1)} %maximum_subtract_fusion.refs_1_, bf16[1024,768]{1,0:T(8,128)(2,1)S(1)} %multiply_convert_fusion.2.refs_2_.refs_3_, ...), custom_call_target="tpu_custom_call" | custom-call | flops 12884901888 | bytes 2097152 | tf_op jit(solution)/shard_map/pallas_call | solution.py:327
  90.6 7.6 %collective-permute-done.18 = bf16[128,1024]{0,1:T(8,128)(2,1)S(1)} collective-permute-done((bf16[128,1024]{0,1:T(8,128)(2,1)S(1)}, bf16[128,1024]{0,1:T(8,128)(2,1)S(1)}, u32[]{:S(2)}, u32[]{:S(2)}) %collective-permute-start.18) | collective-permute-done | bytes 262176 | tf_op jit(solution)/shard_map/ppermute | solution.py:37
  98.2 5.4 %collective-permute-done.17 = bf16[256,1024]{1,0:T(8,128)(2,1)S(1)} collective-permute-done((bf16[256,1024]{1,0:T(8,128)(2,1)S(1)}, bf16[256,1024]{1,0:T(8,128)(2,1)S(1)}, u32[]{:S(2)}, u32[]{:S(2)}) %collective-permute-start.17) | collective-permute-done | bytes 524320 | tf_op jit(solution)/shard_map/ppermute | solution.py:37
  107.6 11.2 %collective-permute-done.21 = bf16[256,1024]{1,0:T(8,128)(2,1)S(1)} collective-permute-done((bf16[256,1024]{1,0:T(8,128)(2,1)S(1)}, bf16[256,1024]{1,0:T(8,128)(2,1)S(1)}, u32[]{:S(2)}, u32[]{:S(2)}) %collective-permute-start.21) | collective-permute-done | bytes 524320 | tf_op jit(solution)/shard_map/ppermute | solution.py:37
  123.5 11.0 %collective-permute-done.23 = bf16[256,1024]{0,1:T(8,128)(2,1)S(1)} collective-permute-done((bf16[256,1024]{0,1:T(8,128)(2,1)S(1)}, bf16[256,1024]{0,1:T(8,128)(2,1)S(1)}, u32[]{:S(2)}, u32[]{:S(2)}) %collective-permute-start.23) | collective-permute-done | bytes 524320 | tf_op jit(solution)/shard_map/ppermute | solution.py:37
  134.5 4.4 %shard_map.485 = (bf16[1024,256]{1,0:T(8,128)(2,1)S(1)}, f32[256,1024]{1,0:T(8,128)S(1)}, f32[4,1024]{1,0:T(4,128)S(1)}) custom-call(bf16[1024,256]{1,0:T(8,128)(2,1)S(1)} %fusion.9.refs_0_, bf16[512,512]{1,0:T(8,128)(2,1)S(1)} %pad_maximum_fusion.22.refs_1_.refs_4_), custom_call_target="tpu_custom_call" | custom-call | flops 6442450944 | bytes 2097152 | tf_op jit(solution)/shard_map/pallas_call | solution.py:327
  139.6 4.9 %collective-permute-done.25 = bf16[512,1024]{1,0:T(8,128)(2,1)S(1)} collective-permute-done((bf16[512,1024]{1,0:T(8,128)(2,1)S(1)}, bf16[512,1024]{1,0:T(8,128)(2,1)S(1)}, u32[]{:S(2)}, u32[]{:S(2)}) %collective-permute-start.25) | collective-permute-done | bytes 1048608 | tf_op jit(solution)/shard_map/ppermute | solution.py:37
  146.9 11.8 %collective-permute-done.26 = bf16[256,1024]{1,0:T(8,128)(2,1)S(1)} collective-permute-done((bf16[256,1024]{1,0:T(8,128)(2,1)S(1)}, bf16[256,1024]{1,0:T(8,128)(2,1)S(1)}, u32[]{:S(2)}, u32[]{:S(2)}) %collective-permute-start.26) | collective-permute-done | bytes 524320 | tf_op jit(solution)/shard_map/ppermute | solution.py:37
  162.9 9.5 %collective-permute-done.27 = bf16[256,1024]{1,0:T(8,128)(2,1)S(1)} collective-permute-done((bf16[256,1024]{1,0:T(8,128)(2,1)S(1)}, bf16[256,1024]{1,0:T(8,128)(2,1)S(1)}, u32[]{:S(2)}, u32[]{:S(2)}) %collective-permute-start.27) | collective-permute-done | bytes 524320 | tf_op jit(solution)/shard_map/ppermute | solution.py:37
  172.7 12.3 %collective-permute-done.29 = bf16[512,1024]{0,1:T(8,128)(2,1)S(1)} collective-permute-done((bf16[512,1024]{0,1:T(8,128)(2,1)S(1)}, bf16[512,1024]{0,1:T(8,128)(2,1)S(1)}, u32[]{:S(2)}, u32[]{:S(2)}) %collective-permute-start.29) | collective-permute-done | bytes 1048608 | tf_op jit(solution)/shard_map/ppermute | solution.py:37
  185.9 4.5 %multiply_convert_fusion.1 = (bf16[1024,1024]{1,0:T(8,128)(2,1)S(1)}, f32[1024,1024]{1,0:T(8,128)}) fusion(f32[1024]{0:T(1024)S(1)} %copy-done.103, bf16[1024,1024]{1,0:T(8,128)(2,1)S(1)} %pad_maximum_fusion.2, bf16[1024,1024]{1,0:T(8,128)(2,1)S(1)} %constant_dynamic-update-slice_fusion.51), kind=kOutput, calls=%fused_computation.8 | convolution fusion | flops 2153775104 | bytes 10489856 | tf_op jit(solution)/shard_map/dot_general | solution.py:21
  196.4 13.5 %collective-permute-done.31 = bf16[256,1024]{1,0:T(8,128)(2,1)S(1)} collective-permute-done((bf16[256,1024]{1,0:T(8,128)(2,1)S(1)}, bf16[256,1024]{1,0:T(8,128)(2,1)S(1)}, u32[]{:S(2)}, u32[]{:S(2)}) %collective-permute-start.31) | collective-permute-done | bytes 524320 | tf_op jit(solution)/shard_map/ppermute | solution.py:37
  212.1 12.8 %collective-permute-done.32 = bf16[256,1024]{1,0:T(8,128)(2,1)S(1)} collective-permute-done((bf16[256,1024]{1,0:T(8,128)(2,1)S(1)}, bf16[256,1024]{1,0:T(8,128)(2,1)S(1)}, u32[]{:S(2)}, u32[]{:S(2)}) %collective-permute-start.32) | collective-permute-done | bytes 524320 | tf_op jit(solution)/shard_map/ppermute | solution.py:37
  230.3 7.1 %convert_reduce_fusion = (f32[1024]{0:T(1024)S(1)}, bf16[1024,1024]{1,0:T(8,128)(2,1)S(1)}) fusion(f32[1024,1024]{1,0:T(8,128)} %get-tuple-element.408, f32[1024]{0:T(1024)S(1)} %copy-done.103, bf16[1024,1024]{0,1:T(8,128)(2,1)S(1)} %copy-done.77, bf16[512,1024]{1,0:T(8,128)(2,1)} %collective-permute-done.33, bf16[256,1024]{1,0:T(8,128)(2,1)S(1)} %copy-done.55, ...), kind=kOutput, calls=%fused_computation.6 | convolution fusion | flops 2169502720 | bytes 10493952 | tf_op jit(solution)/shard_map/dot_general | solution.py:21
  251.9 8.9 %collective-permute-done.35 = bf16[256,1024]{1,0:T(8,128)(2,1)S(1)} collective-permute-done((bf16[256,1024]{1,0:T(8,128)(2,1)S(1)}, bf16[256,1024]{1,0:T(8,128)(2,1)S(1)}, u32[]{:S(2)}, u32[]{:S(2)}) %collective-permute-start.35) | collective-permute-done | bytes 524320 | tf_op jit(solution)/shard_map/ppermute | solution.py:37
  263.1 12.5 %collective-permute-done.36 = bf16[256,1024]{1,0:T(8,128)(2,1)S(1)} collective-permute-done((bf16[256,1024]{1,0:T(8,128)(2,1)S(1)}, bf16[256,1024]{1,0:T(8,128)(2,1)S(1)}, u32[]{:S(2)}, u32[]{:S(2)}) %collective-permute-start.36) | collective-permute-done | bytes 524320 | tf_op jit(solution)/shard_map/ppermute | solution.py:37
  279.2 6.6 %shard_map.486 = (bf16[1024,256]{1,0:T(8,128)(2,1)S(1)}, f32[512,512]{1,0:T(8,128)S(1)}) custom-call(bf16[1024,256]{1,0:T(8,128)(2,1)S(1)} %fusion.9.refs_0_, bf16[1024,256]{1,0:T(8,128)(2,1)S(1)} %convolution_convert_fusion.9.refs_1_, f32[256,1024]{1,0:T(8,128)S(1)} %copy-done.5, f32[4,1024]{1,0:T(4,128)S(1)} %get-tuple-element.115.refs_3_, ...), custom_call_target="tpu_custom_call" | custom-call | flops 8589934592 | bytes 4194304 | tf_op jit(solution)/shard_map/pallas_call | solution.py:354
  290.4 5.6 %collective-permute-done.57 = bf16[512,1024]{1,0:T(8,128)(2,1)S(1)} collective-permute-done((bf16[512,1024]{1,0:T(8,128)(2,1)S(1)}, bf16[512,1024]{1,0:T(8,128)(2,1)S(1)}, u32[]{:S(2)}, u32[]{:S(2)}) %collective-permute-start.57) | collective-permute-done | bytes 1048608 | tf_op jit(solution)/shard_map/ppermute | solution.py:37
  325.1 8.3 %collective-permute-done.63 = f32[9,1024]{1,0:T(8,128)S(1)} collective-permute-done((f32[9,1024]{1,0:T(8,128)S(1)}, f32[9,1024]{1,0:T(8,128)S(1)}, u32[]{:S(2)}, u32[]{:S(2)}) %collective-permute-start.63) | collective-permute-done | bytes 36896 | tf_op jit(solution)/shard_map/ppermute | solution.py:37
  352.7 5.1 %collective-permute-start.53 = (bf16[512,256]{1,0:T(8,128)(2,1)}, bf16[512,256]{1,0:T(8,128)(2,1)}, u32[]{:S(2)}, u32[]{:S(2)}) collective-permute-start(bf16[512,256]{1,0:T(8,128)(2,1)} %convolution_convert_fusion.10), channel_id=1, source_target_pairs={{0,4},{4,0},{1,5},{5,1},{2,6},{6,2},{3,7},{7,3},{8,12},{12,8},{9,1... | collective-permute-start | bytes 786440 | tf_op jit(solution)/shard_map/ppermute | solution.py:37
  361.5 3.5 collective-permute-done.44
  365.1 10.4 %shard_map.488 = (bf16[1024,256]{1,0:T(8,128)(2,1)S(1)}, bf16[1024,512]{1,0:T(8,128)(2,1)S(1)}) custom-call(s32[5]{0:T(128)S(1)} %pad_add_fusion.1.refs_0_, s32[1,1024]{1,0:T(1,128)S(1)} %maximum_subtract_fusion.refs_1_, f32[256,1024]{1,0:T(8,128)S(1)} %get-tuple-element.123.refs_2_, bf16[1024,768]{1,0:T(8,128)(2,1)S(1)} %copy-done.3, ...), custom_call_target="tpu_custom_call" | custom-call | flops 17179869184 | bytes 4194304 | tf_op jit(solution)/shard_map/pallas_call | solution.py:354
  379.2 7.0 %collective-permute-start.50 = (bf16[512,768]{1,0:T(8,128)(2,1)}, bf16[512,768]{1,0:T(8,128)(2,1)S(1)}, u32[]{:S(2)}, u32[]{:S(2)}) collective-permute-start(bf16[512,768]{1,0:T(8,128)(2,1)} %add_convert_fusion.3), channel_id=1, source_target_pairs={{0,4},{4,0},{1,5},{5,1},{2,6},{6,2},{3,7},{7,3},{8,12},{12,8},{9,1... | collective-permute-start | bytes 2359304 | tf_op jit(solution)/shard_map/ppermute | solution.py:37
  418.6 3.6 collective-permute-done.55
  424.4 3.4 collective-permute-start.52
  429.4 5.2 %collective-permute-done.52 = bf16[128,768]{1,0:T(8,128)(2,1)S(1)} collective-permute-done((bf16[128,768]{1,0:T(8,128)(2,1)S(1)}, bf16[128,768]{1,0:T(8,128)(2,1)S(1)}, u32[]{:S(2)}, u32[]{:S(2)}) %collective-permute-start.52) | collective-permute-done | bytes 196640 | tf_op jit(solution)/shard_map/ppermute | solution.py:37
  (612 shorter events, 197.6 us)
Async XLA Ops:
  0.7 26.7 %collective-permute-start.9 = (bf16[256,1024]{1,0:T(8,128)(2,1)}, bf16[256,1024]{1,0:T(8,128)(2,1)S(1)}, u32[]{:S(2)}, u32[]{:S(2)}) collective-permute-start(bf16[256,1024]{1,0:T(8,128)(2,1)} %bitcast.112), channel_id=1, source_target_pairs={{0,4},{1,5},{2,6},{3,7},{8,12},{9,13},{10,14},{11,15},{16,20},{17,... | collective-permute-start | bytes 1572872 | tf_op jit(solution)/shard_map/ppermute | solution.py:43
  6.7 18.7 %collective-permute-start.2 = (bf16[128,768]{1,0:T(8,128)(2,1)S(1)}, bf16[128,768]{1,0:T(8,128)(2,1)S(1)}, u32[]{:S(2)}, u32[]{:S(2)}) collective-permute-start(bf16[128,768]{1,0:T(8,128)(2,1)S(1)} %fusion.80), channel_id=1, source_target_pairs={{0,16},{8,24},{16,0},{24,8},{1,17},{9,25},{17,1},{25,9},{2,18},{10... | collective-permute-start | bytes 589832 | tf_op jit(solution)/shard_map/ppermute | solution.py:37
  11.0 16.7 %collective-permute-start = (bf16[256,1024]{1,0:T(8,128)(2,1)S(1)}, bf16[256,1024]{1,0:T(8,128)(2,1)}, u32[]{:S(2)}, u32[]{:S(2)}) collective-permute-start(bf16[256,1024]{1,0:T(8,128)(2,1)S(1)} %constant_dynamic-update-slice_fusion), channel_id=1, source_target_pairs={{0,2},{1,3},{2,0},{3,1},{4,6},{5,7},{6,4},{7,5},{8,10},{9,11},{10,... | collective-permute-start | bytes 1572872 | tf_op jit(solution)/shard_map/ppermute | solution.py:37
  29.8 27.6 %collective-permute-start.1 = (bf16[512,1024]{1,0:T(8,128)(2,1)}, bf16[512,1024]{1,0:T(8,128)(2,1)}, u32[]{:S(2)}, u32[]{:S(2)}) collective-permute-start(bf16[512,1024]{1,0:T(8,128)(2,1)} %pad_maximum_fusion.9), channel_id=1, source_target_pairs={{0,1},{1,0},{2,3},{3,2},{4,5},{5,4},{6,7},{7,6},{8,9},{9,8},{10,11... | collective-permute-start | bytes 3145736 | tf_op jit(solution)/shard_map/ppermute | solution.py:37
  37.9 17.8 %collective-permute-start.4 = (bf16[512,768]{1,0:T(8,128)(2,1)}, bf16[512,768]{1,0:T(8,128)(2,1)}, u32[]{:S(2)}, u32[]{:S(2)}) collective-permute-start(bf16[512,768]{1,0:T(8,128)(2,1)} %pad_maximum_fusion.19), channel_id=1, source_target_pairs={{0,4},{4,0},{1,5},{5,1},{2,6},{6,2},{3,7},{7,3},{8,12},{12,8},{9,1... | collective-permute-start | bytes 2359304 | tf_op jit(solution)/shard_map/ppermute | solution.py:37
  38.0 15.6 %collective-permute-start.10 = (bf16[256,1024]{1,0:T(8,128)(2,1)S(1)}, bf16[256,1024]{1,0:T(8,128)(2,1)S(1)}, u32[]{:S(2)}, u32[]{:S(2)}) collective-permute-start(bf16[256,1024]{1,0:T(8,128)(2,1)S(1)} %constant_dynamic-update-slice_fusion.10), channel_id=1, source_target_pairs={{0,2},{1,3},{2,0},{3,1},{4,6},{5,7},{6,4},{7,5},{8,10},{9,11},{10,... | collective-permute-start | bytes 1572872 | tf_op jit(solution)/shard_map/ppermute | solution.py:37
  53.7 15.5 %collective-permute-start.11 = (bf16[512,1024]{1,0:T(8,128)(2,1)S(1)}, bf16[512,1024]{1,0:T(8,128)(2,1)S(1)}, u32[]{:S(2)}, u32[]{:S(2)}) collective-permute-start(bf16[512,1024]{1,0:T(8,128)(2,1)S(1)} %pad_maximum_fusion.10), channel_id=1, source_target_pairs={{0,1},{1,0},{2,3},{3,2},{4,5},{5,4},{6,7},{7,6},{8,9},{9,8},{10,11... | collective-permute-start | bytes 3145736 | tf_op jit(solution)/shard_map/ppermute | solution.py:37
  57.0 24.7 %collective-permute-start.14 = (bf16[512,256]{0,1:T(8,128)(2,1)S(1)}, bf16[512,256]{0,1:T(8,128)(2,1)S(1)}, u32[]{:S(2)}, u32[]{:S(2)}) collective-permute-start(bf16[512,256]{0,1:T(8,128)(2,1)S(1)} %pad_maximum_fusion.24), channel_id=1, source_target_pairs={{0,4},{4,0},{1,5},{5,1},{2,6},{6,2},{3,7},{7,3},{8,12},{12,8},{9,1... | collective-permute-start | bytes 786440 | tf_op jit(solution)/shard_map/ppermute | solution.py:37
  83.6 14.5 %collective-permute-start.18 = (bf16[128,1024]{0,1:T(8,128)(2,1)S(1)}, bf16[128,1024]{0,1:T(8,128)(2,1)S(1)}, u32[]{:S(2)}, u32[]{:S(2)}) collective-permute-start(bf16[128,1024]{0,1:T(8,128)(2,1)S(1)} %dynamic-slice_bitcast_fusion), channel_id=1, source_target_pairs={{0,16},{8,24},{16,0},{24,8},{1,17},{9,25},{17,1},{25,9},{2,18},{10... | collective-permute-start | bytes 786440 | tf_op jit(solution)/shard_map/ppermute | solution.py:37
  84.0 19.7 %collective-permute-start.17 = (bf16[256,1024]{1,0:T(8,128)(2,1)S(1)}, bf16[256,1024]{1,0:T(8,128)(2,1)S(1)}, u32[]{:S(2)}, u32[]{:S(2)}) collective-permute-start(bf16[256,1024]{1,0:T(8,128)(2,1)S(1)} %constant_dynamic-update-slice_fusion.20), channel_id=1, source_target_pairs={{0,8},{8,0},{16,24},{24,16},{1,9},{9,1},{17,25},{25,17},{2,10},{10... | collective-permute-start | bytes 1572872 | tf_op jit(solution)/shard_map/ppermute | solution.py:37
  86.4 17.3 %collective-permute-start.20 = (bf16[512,512]{0,1:T(8,128)(2,1)S(1)}, bf16[512,512]{0,1:T(8,128)(2,1)S(1)}, u32[]{:S(2)}, u32[]{:S(2)}) collective-permute-start(bf16[512,512]{0,1:T(8,128)(2,1)S(1)} %get-tuple-element.102), channel_id=1, source_target_pairs={{0,4},{4,0},{1,5},{5,1},{2,6},{6,2},{3,7},{7,3},{8,12},{12,8},{9,1... | collective-permute-start | bytes 1572872 | tf_op jit(solution)/shard_map/ppermute | solution.py:37
  88.7 16.6 %collective-permute-start.19 = (bf16[256,512]{1,0:T(8,128)(2,1)S(1)}, bf16[256,512]{1,0:T(8,128)(2,1)S(1)}, u32[]{:S(2)}, u32[]{:S(2)}) collective-permute-start(bf16[256,512]{1,0:T(8,128)(2,1)S(1)} %fusion.10), channel_id=1, source_target_pairs={{0,4},{4,0},{1,5},{5,1},{2,6},{6,2},{3,7},{7,3},{8,12},{12,8},{9,1... | collective-permute-start | bytes 786440 | tf_op jit(solution)/shard_map/ppermute | solution.py:37
  89.6 15.7 %collective-permute-start.16 = (bf16[256,1024]{1,0:T(8,128)(2,1)S(1)}, bf16[256,1024]{1,0:T(8,128)(2,1)S(1)}, u32[]{:S(2)}, u32[]{:S(2)}) collective-permute-start(bf16[256,1024]{1,0:T(8,128)(2,1)S(1)} %slice.1326), channel_id=1, source_target_pairs={{0,2},{1,3},{2,0},{3,1},{4,6},{5,7},{6,4},{7,5},{8,10},{9,11},{10,... | collective-permute-start | bytes 1572872 | tf_op jit(solution)/shard_map/ppermute | solution.py:37
  118.9 25.6 %collective-permute-start.25 = (bf16[512,1024]{1,0:T(8,128)(2,1)S(1)}, bf16[512,1024]{1,0:T(8,128)(2,1)S(1)}, u32[]{:S(2)}, u32[]{:S(2)}) collective-permute-start(bf16[512,1024]{1,0:T(8,128)(2,1)S(1)} %constant_dynamic-update-slice_fusion.32), channel_id=1, source_target_pairs={{0,4},{4,0},{1,5},{5,1},{2,6},{6,2},{3,7},{7,3},{8,12},{12,8},{9,1... | collective-permute-start | bytes 3145736 | tf_op jit(solution)/shard_map/ppermute | solution.py:37
  161.5 23.5 %collective-permute-start.29 = (bf16[512,1024]{0,1:T(8,128)(2,1)S(1)}, bf16[512,1024]{0,1:T(8,128)(2,1)S(1)}, u32[]{:S(2)}, u32[]{:S(2)}) collective-permute-start(bf16[512,1024]{0,1:T(8,128)(2,1)S(1)} %constant_dynamic-update-slice_fusion.49), channel_id=1, source_target_pairs={{0,4},{4,0},{1,5},{5,1},{2,6},{6,2},{3,7},{7,3},{8,12},{12,8},{9,1... | collective-permute-start | bytes 3145736 | tf_op jit(solution)/shard_map/ppermute | solution.py:37
  195.8 14.0 %collective-permute-start.31 = (bf16[256,1024]{1,0:T(8,128)(2,1)S(1)}, bf16[256,1024]{1,0:T(8,128)(2,1)S(1)}, u32[]{:S(2)}, u32[]{:S(2)}) collective-permute-start(bf16[256,1024]{1,0:T(8,128)(2,1)S(1)} %slice.1324), channel_id=1, source_target_pairs={{0,2},{1,3},{2,0},{3,1},{4,6},{5,7},{6,4},{7,5},{8,10},{9,11},{10,... | collective-permute-start | bytes 1572872 | tf_op jit(solution)/shard_map/ppermute | solution.py:37
  246.7 14.1 %collective-permute-start.35 = (bf16[256,1024]{1,0:T(8,128)(2,1)S(1)}, bf16[256,1024]{1,0:T(8,128)(2,1)S(1)}, u32[]{:S(2)}, u32[]{:S(2)}) collective-permute-start(bf16[256,1024]{1,0:T(8,128)(2,1)S(1)} %slice.1323), channel_id=1, source_target_pairs={{0,2},{1,3},{2,0},{3,1},{4,6},{5,7},{6,4},{7,5},{8,10},{9,11},{10,... | collective-permute-start | bytes 1572872 | tf_op jit(solution)/shard_map/ppermute | solution.py:37
  248.5 38.1 %collective-permute-start.60 = (bf16[512,1024]{1,0:T(8,128)(2,1)S(1)}, bf16[512,1024]{1,0:T(8,128)(2,1)S(1)}, u32[]{:S(2)}, u32[]{:S(2)}) collective-permute-start(bf16[512,1024]{1,0:T(8,128)(2,1)S(1)} %convolution_convert_fusion), channel_id=1, source_target_pairs={{0,4},{4,0},{1,5},{5,1},{2,6},{6,2},{3,7},{7,3},{8,12},{12,8},{9,1... | collective-permute-start | bytes 3145736 | tf_op jit(solution)/shard_map/ppermute | solution.py:37
  250.1 45.9 %collective-permute-start.57 = (bf16[512,1024]{1,0:T(8,128)(2,1)S(1)}, bf16[512,1024]{1,0:T(8,128)(2,1)S(1)}, u32[]{:S(2)}, u32[]{:S(2)}) collective-permute-start(bf16[512,1024]{1,0:T(8,128)(2,1)S(1)} %convolution_convert_fusion.1), channel_id=1, source_target_pairs={{0,4},{4,0},{1,5},{5,1},{2,6},{6,2},{3,7},{7,3},{8,12},{12,8},{9,1... | collective-permute-start | bytes 3145736 | tf_op jit(solution)/shard_map/ppermute | solution.py:37
  287.0 14.3 %collective-permute-start.61 = (bf16[256,1024]{1,0:T(8,128)(2,1)S(1)}, bf16[256,1024]{1,0:T(8,128)(2,1)S(1)}, u32[]{:S(2)}, u32[]{:S(2)}) collective-permute-start(bf16[256,1024]{1,0:T(8,128)(2,1)S(1)} %slice.1318), channel_id=1, source_target_pairs={{0,8},{8,0},{16,24},{24,16},{1,9},{9,1},{17,25},{25,17},{2,10},{10... | collective-permute-start | bytes 1572872 | tf_op jit(solution)/shard_map/ppermute | solution.py:37
  303.7 29.8 %collective-permute-start.62 = (bf16[128,1024]{1,0:T(8,128)(2,1)}, bf16[128,1024]{1,0:T(8,128)(2,1)S(1)}, u32[]{:S(2)}, u32[]{:S(2)}) collective-permute-start(bf16[128,1024]{1,0:T(8,128)(2,1)} %slice.1328), channel_id=1, source_target_pairs={{0,16},{8,24},{16,0},{24,8},{1,17},{9,25},{17,1},{25,9},{2,18},{10... | collective-permute-start | bytes 786440 | tf_op jit(solution)/shard_map/ppermute | solution.py:37
  304.3 18.5 %collective-permute-start.58 = (bf16[256,1024]{1,0:T(8,128)(2,1)}, bf16[256,1024]{1,0:T(8,128)(2,1)}, u32[]{:S(2)}, u32[]{:S(2)}) collective-permute-start(bf16[256,1024]{1,0:T(8,128)(2,1)} %slice.1319), channel_id=1, source_target_pairs={{0,8},{8,0},{16,24},{24,16},{1,9},{9,1},{17,25},{25,17},{2,10},{10... | collective-permute-start | bytes 1572872 | tf_op jit(solution)/shard_map/ppermute | solution.py:37
  309.4 32.5 %collective-permute-start.43 = (bf16[512,1024]{0,1:T(8,128)(2,1)}, bf16[512,1024]{0,1:T(8,128)(2,1)}, u32[]{:S(2)}, u32[]{:S(2)}) collective-permute-start(bf16[512,1024]{0,1:T(8,128)(2,1)} %pad_maximum_fusion.16), channel_id=1, source_target_pairs={{0,4},{4,0},{1,5},{5,1},{2,6},{6,2},{3,7},{7,3},{8,12},{12,8},{9,1... | collective-permute-start | bytes 3145736 | tf_op jit(solution)/shard_map/ppermute | solution.py:37
  317.9 18.9 %collective-permute-start.40 = (bf16[256,1024]{1,0:T(8,128)(2,1)S(1)}, bf16[256,1024]{1,0:T(8,128)(2,1)}, u32[]{:S(2)}, u32[]{:S(2)}) collective-permute-start(bf16[256,1024]{1,0:T(8,128)(2,1)S(1)} %get-tuple-element.277), channel_id=1, source_target_pairs={{0,2},{1,3},{2,0},{3,1},{4,6},{5,7},{6,4},{7,5},{8,10},{9,11},{10,... | collective-permute-start | bytes 1572872 | tf_op jit(solution)/shard_map/ppermute | solution.py:37
  318.5 14.9 %collective-permute-start.63 = (f32[9,1024]{1,0:T(8,128)S(1)}, f32[9,1024]{1,0:T(8,128)S(1)}, u32[]{:S(2)}, u32[]{:S(2)}) collective-permute-start(f32[9,1024]{1,0:T(8,128)S(1)} %constant_dynamic-update-slice_fusion.87), channel_id=1, source_target_pairs={{0,2},{1,3},{2,0},{3,1},{4,6},{5,7},{6,4},{7,5},{8,10},{9,11},{10,... | collective-permute-start | bytes 110600 | tf_op jit(solution)/shard_map/ppermute | solution.py:37
  334.6 25.2 %collective-permute-start.59 = (bf16[128,1024]{1,0:T(8,128)(2,1)S(1)}, bf16[128,1024]{1,0:T(8,128)(2,1)S(1)}, u32[]{:S(2)}, u32[]{:S(2)}) collective-permute-start(bf16[128,1024]{1,0:T(8,128)(2,1)S(1)} %slice.1329), channel_id=1, source_target_pairs={{0,16},{8,24},{16,0},{24,8},{1,17},{9,25},{17,1},{25,9},{2,18},{10... | collective-permute-start | bytes 786440 | tf_op jit(solution)/shard_map/ppermute | solution.py:37
  348.0 41.1 %collective-permute-start.45 = (bf16[1024,512]{1,0:T(8,128)(2,1)S(1)}, bf16[1024,512]{1,0:T(8,128)(2,1)S(1)}, u32[]{:S(2)}, u32[]{:S(2)}) collective-permute-start(bf16[1024,512]{1,0:T(8,128)(2,1)S(1)} %get-tuple-element.124), channel_id=1, source_target_pairs={{4,0},{5,1},{6,2},{7,3},{12,8},{13,9},{14,10},{15,11},{20,16},{21,... | collective-permute-start | bytes 3145736 | tf_op jit(solution)/shard_map/ppermute | solution.py:43
  350.8 14.2 %collective-permute-start.44 = (bf16[256,1024]{0,1:T(8,128)(2,1)S(1)}, bf16[256,1024]{0,1:T(8,128)(2,1)S(1)}, u32[]{:S(2)}, u32[]{:S(2)}) collective-permute-start(bf16[256,1024]{0,1:T(8,128)(2,1)S(1)} %slice.1321), channel_id=1, source_target_pairs={{0,8},{8,0},{16,24},{24,16},{1,9},{9,1},{17,25},{25,17},{2,10},{10... | collective-permute-start | bytes 1572872 | tf_op jit(solution)/shard_map/ppermute | solution.py:37
  352.7 52.4 %collective-permute-start.53 = (bf16[512,256]{1,0:T(8,128)(2,1)}, bf16[512,256]{1,0:T(8,128)(2,1)}, u32[]{:S(2)}, u32[]{:S(2)}) collective-permute-start(bf16[512,256]{1,0:T(8,128)(2,1)} %convolution_convert_fusion.10), channel_id=1, source_target_pairs={{0,4},{4,0},{1,5},{5,1},{2,6},{6,2},{3,7},{7,3},{8,12},{12,8},{9,1... | collective-permute-start | bytes 786440 | tf_op jit(solution)/shard_map/ppermute | solution.py:37
  376.0 18.5 %collective-permute-start.56 = (bf16[128,1024]{0,1:T(8,128)(2,1)S(1)}, bf16[128,1024]{0,1:T(8,128)(2,1)S(1)}, u32[]{:S(2)}, u32[]{:S(2)}) collective-permute-start(bf16[128,1024]{0,1:T(8,128)(2,1)S(1)} %slice.1330), channel_id=1, source_target_pairs={{0,16},{8,24},{16,0},{24,8},{1,17},{9,25},{17,1},{25,9},{2,18},{10... | collective-permute-start | bytes 786440 | tf_op jit(solution)/shard_map/ppermute | solution.py:37
  379.2 29.9 %collective-permute-start.50 = (bf16[512,768]{1,0:T(8,128)(2,1)}, bf16[512,768]{1,0:T(8,128)(2,1)S(1)}, u32[]{:S(2)}, u32[]{:S(2)}) collective-permute-start(bf16[512,768]{1,0:T(8,128)(2,1)} %add_convert_fusion.3), channel_id=1, source_target_pairs={{0,4},{4,0},{1,5},{5,1},{2,6},{6,2},{3,7},{7,3},{8,12},{12,8},{9,1... | collective-permute-start | bytes 2359304 | tf_op jit(solution)/shard_map/ppermute | solution.py:37
  403.7 24.1 %collective-permute-start.47 = (bf16[256,1024]{1,0:T(8,128)(2,1)}, bf16[256,1024]{1,0:T(8,128)(2,1)}, u32[]{:S(2)}, u32[]{:S(2)}) collective-permute-start(bf16[256,1024]{1,0:T(8,128)(2,1)} %slice.1320), channel_id=1, source_target_pairs={{0,2},{1,3},{2,0},{3,1},{4,6},{5,7},{6,4},{7,5},{8,10},{9,11},{10,... | collective-permute-start | bytes 1572872 | tf_op jit(solution)/shard_map/ppermute | solution.py:37
  (148 other events, 1272.4 us)

commit v4 on v3

--- a/solution.py
+++ b/solution.py
@@ -74,10 +74,10 @@
     return total
 
 
-def scatter_tree(make, size, steps, used=None):
+def scatter_tree(make, size, steps, used=None, start=None):
     axis, bit = steps[-1]
     half = size // 2
-    arrived = swap(low(make(slice(half, size))), axis, bit)
+    arrived = swap(after(low(make(slice(half, size))), start), axis, bit)
     total = after(make(slice(0, half)), used) + wide(arrived)
     return scatter_more(total, steps[:-1])
 
@@ -458,8 +458,8 @@
     far_steps, near_steps = steps_of("shard")[:-1], steps_of("shard")[-1:]
     share = turned(inputs[0], 1)
     old_share = turned(shift(inputs[0], "ctx", 1), 1)
-    inputs_rows = gather_rows(share)
-    old_rows = gather_rows(old_share)
+    inputs_rows = lax.optimization_barrier(gather_rows(share))
+    old_rows = lax.optimization_barrier(gather_rows(old_share))
     qkv_own = own_half(jnp.concatenate([query_weight, key_weight, value_weight], axis=1))
     qkv_far = gather_tree(qkv_own, far_steps)
     qkv_near = gather_tree(qkv_far, near_steps)
@@ -551,26 +551,51 @@
     small_full = gather_tree(small_near[:, 2 * width :], ctx_steps, mixed, attn_part)
     first_low = after(low(first), up_near, down_far, mkv, small_full)
     mquery_full, mout_full = small_full[:, :width], small_full[:, width:]
-    first_rows = gather_rows(first_low)
-    down_near = gather_tree(down_far, near_steps, first_low, first_rows)
+    half_rows = gather_tree(first_low, row_steps[:-1])
+    down_near = gather_tree(down_far, near_steps, first_low, half_rows)
+    up_ready = gather_tree(split(up_near, 1, 2)[0], ctx_steps, first_low, half_rows)
+    half_rows = after(half_rows, down_near, up_ready)
+    first_rows = gather_tree(half_rows, row_steps[-1:])
     mquery = low((matmul(first_rows, mquery_full) + memory_qbias) * 0.125)
-    mquery = after(mquery, down_near)
     cross_mixed, cross_mixed_t, cross_lse = attend(width, mquery, mkv)
-    up_full = gather_tree(up_near, ctx_steps, first_low, cross_mixed)
+    up_parts = [
+        up_ready,
+        gather_tree(split(up_near, 1, 2)[1], ctx_steps, half_rows, cross_mixed),
+    ]
+    cross_mixed = after(cross_mixed, up_parts[1])
     cross_part = scatter_tree(
         lambda s: contract("rk,dk->rd", cross_mixed[s], mout_full), rows, row_steps[-1:]
     )
-    cross_part = after(cross_part, up_full)
     cross_share = scatter_more(cross_part, row_steps[:-1])
     second, normed_two, rstd_two = layer_norm(
         first + cross_share + memory_obias, gain_memory, shift_memory
     )
-    second_low = low(second)
-    down_full = gather_tree(down_near, ctx_steps, cross_part, second_low)
-    second_rows = after(gather_rows(second_low), down_full)
+    down_ready = gather_tree(split(down_near, 1, 2)[0], ctx_steps, cross_mixed, cross_part)
+    second_low = after(low(second), down_ready)
+    half_second = gather_tree(second_low, row_steps[:-1])
+    down_parts = [
+        down_ready,
+        gather_tree(split(down_near, 1, 2)[1], ctx_steps, second_low, half_second),
+    ]
+    second_rows = gather_tree(after(half_second, down_parts[1]), row_steps[-1:])
+    up_full = lax.optimization_barrier(
+        jnp.concatenate([after(up_parts[0], cross_part), up_parts[1]], axis=1)
+    )
     act, slope = gelu_and_slope(matmul(second_rows, up_full) + up_bias)
     act_low, slope_low = low(act), low(slope)
-    dense_share = scatter_rows(lambda s: contract("rf,df->rd", act_low[s], down_full))
+
+    def dense_term(s):
+        terms = [
+            contract("rf,df->rd", a, part)
+            for a, part in zip(split(act_low[s], 1, 2), down_parts, strict=True)
+        ]
+        return terms[0] + terms[1]
+
+    dense_part = scatter_tree(dense_term, rows, row_steps[-1:])
+    dense_share = scatter_more(dense_part, row_steps[:-1])
+    down_full = lax.optimization_barrier(
+        jnp.concatenate([after(down_parts[0], dense_part), down_parts[1]], axis=1)
+    )
     result, normed_three, rstd_three = layer_norm(
         second + dense_share + down_bias, gain_dense, shift_dense
     )
@@ -594,7 +619,9 @@
     )
     mquery_pre = mquery_back * 0.125
     down_near_grad = scatter_more(down_part, near_steps, None, mquery_pre)
-    up_part = scatter_tree(weight_terms((second_rows, hidden_low)), model, ctx_steps, mquery_pre)
+    up_part = scatter_tree(
+        weight_terms((second_rows, hidden_low)), model, ctx_steps, mquery_pre, cross_low
+    )
     first_part = scatter_tree(
         lambda s: contract("rk,dk->rd", mquery_pre[s], mquery_full), rows, row_steps[-1:]
     )

time: 444 us -> 428 us (0.964)
  waiting for transfers between devices: 191 us -> 168 us
  local copies, waits for them, and re-layouts: 32.9 us -> 41 us
  other arithmetic: 52.9 us -> 48 us
  starting transfers between devices: 72.9 us -> 77.8 us
    ppermute x66 -> x68, waiting for transfers between devices: 191 us -> 168 us  [swap(): lax.ppermute(array, axis, [(i, i ^ bit) for i in range(lax.axis_size(axis...]
    ppermute x66 -> x68, starting transfers between devices: 66.3 us -> 72.8 us  [swap(): lax.ppermute(array, axis, [(i, i ^ bit) for i in range(lax.axis_size(axis...]
    unnamed x239 -> x259, local copies, waits for them, and re-layouts: 20 us -> 26.1 us
    concatenate x20 -> x17, other arithmetic: 18.3 us -> 13.5 us  [gather_tree(): jnp.concatenate([after(array, used if n == len(steps) - 1 else None), arr...]
    dot_general x32 -> x34, matrix products: 31.2 us -> 34 us  [contract(): return jnp.einsum(form, left, right, preferred_element_type=jnp.float32)]
  transfers between devices with their start and end apart: 68 -> 70, of which waited for: 35 -> 40; matrix products, arithmetic and copies ran while one was open for 24% -> 24% of each run, Pallas kernels for 7% -> 7%
where the time goes in v4:
time: 428 us; the launch traced here: 421 us
  waiting for transfers between devices  168 us (39%)
  starting transfers between devices  77.8 us (18%)
  matrix products  52 us (12%)
  other arithmetic  48 us (11%)
  local copies, waits for them, and re-layouts  41 us (10%)
  Pallas kernels  30.6 us (7%)
    ppermute x68, waiting for transfers between devices, swap(): lax.ppermute(array, axis, [(i, i ^ bit) for i in range(lax.axis_size(axis...  168 us
    ppermute x68, starting transfers between devices, swap(): lax.ppermute(array, axis, [(i, i ^ bit) for i in range(lax.axis_size(axis...  72.8 us
    dot_general x34, matrix products, contract(): return jnp.einsum(form, left, right, preferred_element_type=jnp.float32)  34 us
    unnamed x259, local copies, waits for them, and re-layouts  26.1 us
    dot_general x8, matrix products, matmul(): return jnp.dot(left, right, preferred_element_type=jnp.float32)  18.1 us
    pallas_call x3, Pallas kernels, attend_back(): pl.pallas_call(partial(attend_back_kernel, width, kind), in_specs=specs,...  18 us
    concatenate x17, other arithmetic, gather_tree(): jnp.concatenate([after(array, used if n == len(steps) - 1 else None), arr...  13.5 us
    pallas_call x2, Pallas kernels, attend(): pl.pallas_call(partial(attend_kernel, width, masked), in_specs=specs, out...  12.6 us
  transfers between devices with their start and end apart: 70, of which 40 were waited for; matrix products, arithmetic and copies ran while one was open for 24% of the time, Pallas kernels for 7%

profile of v4, /device:TPU:0, one launch (start us, length us, event | category | flops | bytes accessed | tf_op | source)
XLA Modules:
  0.0 421.1 jit_solution(9949493745612539884)
XLA Ops:
  1.8 4.1 collective-permute-start.2
  5.9 3.4 collective-permute-start.9
  28.4 6.8 %collective-permute-done.3 = bf16[256,768]{1,0:T(8,128)(2,1)S(1)} collective-permute-done((bf16[256,768]{1,0:T(8,128)(2,1)S(1)}, bf16[256,768]{1,0:T(8,128)(2,1)S(1)}, u32[]{:S(2)}, u32[]{:S(2)}) %collective-permute-start.3) | collective-permute-done | bytes 393248 | tf_op jit(solution)/shard_map/ppermute | solution.py:37
  44.7 5.6 %collective-permute-done.7 = bf16[128,1024]{0,1:T(8,128)(2,1)S(1)} collective-permute-done((bf16[128,1024]{0,1:T(8,128)(2,1)}, bf16[128,1024]{0,1:T(8,128)(2,1)S(1)}, u32[]{:S(2)}, u32[]{:S(2)}) %collective-permute-start.7) | collective-permute-done | bytes 262176 | tf_op jit(solution)/shard_map/ppermute | solution.py:37
  58.7 2.9 multiply_convert_fusion.2.refs_2_.refs_3_
  69.6 8.2 %shard_map.484 = (bf16[1024,256]{1,0:T(8,128)(2,1)S(1)}, f32[256,1024]{1,0:T(8,128)S(1)}, f32[4,1024]{1,0:T(4,128)S(1)}) custom-call(s32[5]{0:T(128)S(1)} %pad_add_fusion.1.refs_0_, s32[1,1024]{1,0:T(1,128)S(1)} %maximum_subtract_fusion.refs_1_, bf16[1024,768]{1,0:T(8,128)(2,1)S(1)} %multiply_convert_fusion.2.refs_2_.refs_3_, ...), custom_call_target="tpu_custom_call" | custom-call | flops 12884901888 | bytes 2097152 | tf_op jit(solution)/shard_map/pallas_call | solution.py:327
  82.3 2.8 collective-permute-start.20
  88.1 6.9 %collective-permute-done.18 = bf16[128,1024]{0,1:T(8,128)(2,1)S(1)} collective-permute-done((bf16[128,1024]{0,1:T(8,128)(2,1)S(1)}, bf16[128,1024]{0,1:T(8,128)(2,1)S(1)}, u32[]{:S(2)}, u32[]{:S(2)}) %collective-permute-start.18) | collective-permute-done | bytes 262176 | tf_op jit(solution)/shard_map/ppermute | solution.py:37
  95.1 4.8 %collective-permute-done.17 = bf16[256,1024]{1,0:T(8,128)(2,1)S(1)} collective-permute-done((bf16[256,1024]{1,0:T(8,128)(2,1)S(1)}, bf16[256,1024]{1,0:T(8,128)(2,1)S(1)}, u32[]{:S(2)}, u32[]{:S(2)}) %collective-permute-start.17) | collective-permute-done | bytes 524320 | tf_op jit(solution)/shard_map/ppermute | solution.py:37
  107.9 8.4 %collective-permute-done.21 = bf16[256,1024]{1,0:T(8,128)(2,1)S(1)} collective-permute-done((bf16[256,1024]{1,0:T(8,128)(2,1)S(1)}, bf16[256,1024]{1,0:T(8,128)(2,1)S(1)}, u32[]{:S(2)}, u32[]{:S(2)}) %collective-permute-start.21) | collective-permute-done | bytes 524320 | tf_op jit(solution)/shard_map/ppermute | solution.py:37
  123.0 4.4 %shard_map.485 = (bf16[1024,256]{1,0:T(8,128)(2,1)S(1)}, f32[256,1024]{1,0:T(8,128)S(1)}, f32[4,1024]{1,0:T(4,128)S(1)}) custom-call(bf16[1024,256]{1,0:T(8,128)(2,1)S(1)} %fusion.9.refs_0_, bf16[512,512]{1,0:T(8,128)(2,1)S(1)} %pad_maximum_fusion.21.refs_1_.refs_4_), custom_call_target="tpu_custom_call" | custom-call | flops 6442450944 | bytes 2097152 | tf_op jit(solution)/shard_map/pallas_call | solution.py:327
  127.5 5.0 %collective-permute-done.25 = bf16[512,512]{1,0:T(8,128)(2,1)S(1)} collective-permute-done((bf16[512,512]{1,0:T(8,128)(2,1)S(1)}, bf16[512,512]{1,0:T(8,128)(2,1)S(1)}, u32[]{:S(2)}, u32[]{:S(2)}) %collective-permute-start.25) | collective-permute-done | bytes 524320 | tf_op jit(solution)/shard_map/ppermute | solution.py:37
  137.4 10.2 %collective-permute-done.28 = bf16[512,512]{0,1:T(8,128)(2,1)S(1)} collective-permute-done((bf16[512,512]{0,1:T(8,128)(2,1)S(1)}, bf16[512,512]{0,1:T(8,128)(2,1)S(1)}, u32[]{:S(2)}, u32[]{:S(2)}) %collective-permute-start.28) | collective-permute-done | bytes 524320 | tf_op jit(solution)/shard_map/ppermute | solution.py:37
  147.6 2.7 collective-permute-done.27
  153.9 10.7 %collective-permute-done.29 = bf16[256,1024]{1,0:T(8,128)(2,1)S(1)} collective-permute-done((bf16[256,1024]{1,0:T(8,128)(2,1)S(1)}, bf16[256,1024]{1,0:T(8,128)(2,1)S(1)}, u32[]{:S(2)}, u32[]{:S(2)}) %collective-permute-start.29) | collective-permute-done | bytes 524320 | tf_op jit(solution)/shard_map/ppermute | solution.py:37
  168.1 3.4 multiply_convert_fusion.1
  177.8 12.8 %collective-permute-done.33 = bf16[256,1024]{1,0:T(8,128)(2,1)S(1)} collective-permute-done((bf16[256,1024]{1,0:T(8,128)(2,1)S(1)}, bf16[256,1024]{1,0:T(8,128)(2,1)S(1)}, u32[]{:S(2)}, u32[]{:S(2)}) %collective-permute-start.33) | collective-permute-done | bytes 524320 | tf_op jit(solution)/shard_map/ppermute | solution.py:37
  193.5 12.1 %collective-permute-done.34 = bf16[256,1024]{1,0:T(8,128)(2,1)S(1)} collective-permute-done((bf16[256,1024]{1,0:T(8,128)(2,1)S(1)}, bf16[256,1024]{1,0:T(8,128)(2,1)S(1)}, u32[]{:S(2)}, u32[]{:S(2)}) %collective-permute-start.34) | collective-permute-done | bytes 524320 | tf_op jit(solution)/shard_map/ppermute | solution.py:37
  208.4 6.6 %convert_reduce_fusion = (f32[1024]{0:T(1024)S(1)}, bf16[1024,1024]{1,0:T(8,128)(2,1)S(1)}) fusion(f32[1024,1024]{1,0:T(8,128)S(1)} %get-tuple-element.428, f32[1024]{0:T(1024)S(1)} %copy-done.110, bf16[1024,1024]{0,1:T(8,128)(2,1)S(1)} %pad_maximum_fusion.4, bf16[512,1024]{1,0:T(8,128)(2,1)S(1)} %collective-permute-done.35, ...), kind=kOutput, calls=%fused_computation.6 | convolution fusion | flops 2169502720 | bytes 10493952 | tf_op jit(solution)/shard_map/dot_general | solution.py:21
  232.0 9.0 %collective-permute-done.37 = bf16[256,1024]{1,0:T(8,128)(2,1)S(1)} collective-permute-done((bf16[256,1024]{1,0:T(8,128)(2,1)S(1)}, bf16[256,1024]{1,0:T(8,128)(2,1)S(1)}, u32[]{:S(2)}, u32[]{:S(2)}) %collective-permute-start.37) | collective-permute-done | bytes 524320 | tf_op jit(solution)/shard_map/ppermute | solution.py:37
  245.6 10.6 %collective-permute-done.38 = bf16[256,1024]{1,0:T(8,128)(2,1)S(1)} collective-permute-done((bf16[256,1024]{1,0:T(8,128)(2,1)S(1)}, bf16[256,1024]{1,0:T(8,128)(2,1)S(1)}, u32[]{:S(2)}, u32[]{:S(2)}) %collective-permute-start.38) | collective-permute-done | bytes 524320 | tf_op jit(solution)/shard_map/ppermute | solution.py:37
  260.4 6.6 %shard_map.486 = (bf16[1024,256]{1,0:T(8,128)(2,1)S(1)}, f32[512,512]{1,0:T(8,128)S(1)}) custom-call(bf16[1024,256]{1,0:T(8,128)(2,1)S(1)} %fusion.9.refs_0_, bf16[1024,256]{1,0:T(8,128)(2,1)S(1)} %convolution_convert_fusion.8.refs_1_, f32[256,1024]{1,0:T(8,128)S(1)} %copy-done.5, f32[4,1024]{1,0:T(4,128)S(1)} %get-tuple-element.130.refs_3_, ...), custom_call_target="tpu_custom_call" | custom-call | flops 8589934592 | bytes 4194304 | tf_op jit(solution)/shard_map/pallas_call | solution.py:354
  270.9 6.0 %collective-permute-done.59 = bf16[512,1024]{1,0:T(8,128)(2,1)S(1)} collective-permute-done((bf16[512,1024]{1,0:T(8,128)(2,1)S(1)}, bf16[512,1024]{1,0:T(8,128)(2,1)S(1)}, u32[]{:S(2)}, u32[]{:S(2)}) %collective-permute-start.59) | collective-permute-done | bytes 1048608 | tf_op jit(solution)/shard_map/ppermute | solution.py:37
  294.1 2.7 collective-permute-done.41
  300.1 3.4 collective-permute-done.60
  310.5 4.0 collective-permute-done.65
  335.3 4.8 %collective-permute-start.55 = (bf16[512,256]{1,0:T(8,128)(2,1)}, bf16[512,256]{1,0:T(8,128)(2,1)}, u32[]{:S(2)}, u32[]{:S(2)}) collective-permute-start(bf16[512,256]{1,0:T(8,128)(2,1)} %convolution_convert_fusion.9), channel_id=1, source_target_pairs={{0,4},{4,0},{1,5},{5,1},{2,6},{6,2},{3,7},{7,3},{8,12},{12,8},{9,1... | collective-permute-start | bytes 786440 | tf_op jit(solution)/shard_map/ppermute | solution.py:37
  345.7 8.2 %collective-permute-done.46 = bf16[256,1024]{0,1:T(8,128)(2,1)S(1)} collective-permute-done((bf16[256,1024]{0,1:T(8,128)(2,1)S(1)}, bf16[256,1024]{0,1:T(8,128)(2,1)S(1)}, u32[]{:S(2)}, u32[]{:S(2)}) %collective-permute-start.46) | collective-permute-done | bytes 524320 | tf_op jit(solution)/shard_map/ppermute | solution.py:37
  354.0 10.4 %shard_map.488 = (bf16[1024,256]{1,0:T(8,128)(2,1)S(1)}, bf16[1024,512]{1,0:T(8,128)(2,1)S(1)}) custom-call(s32[5]{0:T(128)S(1)} %pad_add_fusion.1.refs_0_, s32[1,1024]{1,0:T(1,128)S(1)} %maximum_subtract_fusion.refs_1_, f32[256,1024]{1,0:T(8,128)S(1)} %get-tuple-element.138.refs_2_, bf16[1024,768]{1,0:T(8,128)(2,1)S(1)} %copy-done.3, ...), custom_call_target="tpu_custom_call" | custom-call | flops 17179869184 | bytes 4194304 | tf_op jit(solution)/shard_map/pallas_call | solution.py:354
  404.0 3.4 collective-permute-done.57
  409.7 3.1 collective-permute-start.54
  414.6 5.3 %collective-permute-done.54 = bf16[128,768]{1,0:T(8,128)(2,1)S(1)} collective-permute-done((bf16[128,768]{1,0:T(8,128)(2,1)S(1)}, bf16[128,768]{1,0:T(8,128)(2,1)S(1)}, u32[]{:S(2)}, u32[]{:S(2)}) %collective-permute-start.54) | collective-permute-done | bytes 196640 | tf_op jit(solution)/shard_map/ppermute | solution.py:37
  (645 shorter events, 217.9 us)
Async XLA Ops:
  1.8 21.8 %collective-permute-start.2 = (bf16[128,768]{1,0:T(8,128)(2,1)S(1)}, bf16[128,768]{1,0:T(8,128)(2,1)S(1)}, u32[]{:S(2)}, u32[]{:S(2)}) collective-permute-start(bf16[128,768]{1,0:T(8,128)(2,1)S(1)} %fusion.87), channel_id=1, source_target_pairs={{0,16},{8,24},{16,0},{24,8},{1,17},{9,25},{17,1},{25,9},{2,18},{10... | collective-permute-start | bytes 589832 | tf_op jit(solution)/shard_map/ppermute | solution.py:37
  5.9 19.7 %collective-permute-start.9 = (bf16[256,1024]{1,0:T(8,128)(2,1)}, bf16[256,1024]{1,0:T(8,128)(2,1)S(1)}, u32[]{:S(2)}, u32[]{:S(2)}) collective-permute-start(bf16[256,1024]{1,0:T(8,128)(2,1)} %bitcast.116), channel_id=1, source_target_pairs={{0,4},{1,5},{2,6},{3,7},{8,12},{9,13},{10,14},{11,15},{16,20},{17,... | collective-permute-start | bytes 1572872 | tf_op jit(solution)/shard_map/ppermute | solution.py:43
  11.1 14.8 %collective-permute-start = (bf16[256,1024]{1,0:T(8,128)(2,1)S(1)}, bf16[256,1024]{1,0:T(8,128)(2,1)}, u32[]{:S(2)}, u32[]{:S(2)}) collective-permute-start(bf16[256,1024]{1,0:T(8,128)(2,1)S(1)} %constant_dynamic-update-slice_fusion), channel_id=1, source_target_pairs={{0,2},{1,3},{2,0},{3,1},{4,6},{5,7},{6,4},{7,5},{8,10},{9,11},{10,... | collective-permute-start | bytes 1572872 | tf_op jit(solution)/shard_map/ppermute | solution.py:37
  28.0 27.6 %collective-permute-start.1 = (bf16[512,1024]{1,0:T(8,128)(2,1)}, bf16[512,1024]{1,0:T(8,128)(2,1)}, u32[]{:S(2)}, u32[]{:S(2)}) collective-permute-start(bf16[512,1024]{1,0:T(8,128)(2,1)} %pad_maximum_fusion.10), channel_id=1, source_target_pairs={{0,1},{1,0},{2,3},{3,2},{4,5},{5,4},{6,7},{7,6},{8,9},{9,8},{10,11... | collective-permute-start | bytes 3145736 | tf_op jit(solution)/shard_map/ppermute | solution.py:37
  36.2 17.8 %collective-permute-start.4 = (bf16[512,768]{1,0:T(8,128)(2,1)}, bf16[512,768]{1,0:T(8,128)(2,1)}, u32[]{:S(2)}, u32[]{:S(2)}) collective-permute-start(bf16[512,768]{1,0:T(8,128)(2,1)} %pad_maximum_fusion.18), channel_id=1, source_target_pairs={{0,4},{4,0},{1,5},{5,1},{2,6},{6,2},{3,7},{7,3},{8,12},{12,8},{9,1... | collective-permute-start | bytes 2359304 | tf_op jit(solution)/shard_map/ppermute | solution.py:37
  36.2 15.1 %collective-permute-start.10 = (bf16[256,1024]{1,0:T(8,128)(2,1)S(1)}, bf16[256,1024]{1,0:T(8,128)(2,1)S(1)}, u32[]{:S(2)}, u32[]{:S(2)}) collective-permute-start(bf16[256,1024]{1,0:T(8,128)(2,1)S(1)} %constant_dynamic-update-slice_fusion.10), channel_id=1, source_target_pairs={{0,2},{1,3},{2,0},{3,1},{4,6},{5,7},{6,4},{7,5},{8,10},{9,11},{10,... | collective-permute-start | bytes 1572872 | tf_op jit(solution)/shard_map/ppermute | solution.py:37
  51.4 15.4 %collective-permute-start.11 = (bf16[512,1024]{1,0:T(8,128)(2,1)S(1)}, bf16[512,1024]{1,0:T(8,128)(2,1)S(1)}, u32[]{:S(2)}, u32[]{:S(2)}) collective-permute-start(bf16[512,1024]{1,0:T(8,128)(2,1)S(1)} %pad_maximum_fusion.11), channel_id=1, source_target_pairs={{0,1},{1,0},{2,3},{3,2},{4,5},{5,4},{6,7},{7,6},{8,9},{9,8},{10,11... | collective-permute-start | bytes 3145736 | tf_op jit(solution)/shard_map/ppermute | solution.py:37
  55.3 22.9 %collective-permute-start.14 = (bf16[512,256]{0,1:T(8,128)(2,1)S(1)}, bf16[512,256]{0,1:T(8,128)(2,1)S(1)}, u32[]{:S(2)}, u32[]{:S(2)}) collective-permute-start(bf16[512,256]{0,1:T(8,128)(2,1)S(1)} %pad_maximum_fusion.23), channel_id=1, source_target_pairs={{0,4},{4,0},{1,5},{5,1},{2,6},{6,2},{3,7},{7,3},{8,12},{12,8},{9,1... | collective-permute-start | bytes 786440 | tf_op jit(solution)/shard_map/ppermute | solution.py:37
  63.3 14.6 %collective-permute-start.13 = (bf16[128,1024]{1,0:T(8,128)(2,1)S(1)}, bf16[128,1024]{1,0:T(8,128)(2,1)S(1)}, u32[]{:S(2)}, u32[]{:S(2)}) collective-permute-start(bf16[128,1024]{1,0:T(8,128)(2,1)S(1)} %constant_dynamic-slice_fusion), channel_id=1, source_target_pairs={{0,16},{8,24},{16,0},{24,8},{1,17},{9,25},{17,1},{25,9},{2,18},{10... | collective-permute-start | bytes 786440 | tf_op jit(solution)/shard_map/ppermute | solution.py:37
  80.4 14.6 %collective-permute-start.18 = (bf16[128,1024]{0,1:T(8,128)(2,1)S(1)}, bf16[128,1024]{0,1:T(8,128)(2,1)S(1)}, u32[]{:S(2)}, u32[]{:S(2)}) collective-permute-start(bf16[128,1024]{0,1:T(8,128)(2,1)S(1)} %dynamic-slice_bitcast_fusion), channel_id=1, source_target_pairs={{0,16},{8,24},{16,0},{24,8},{1,17},{9,25},{17,1},{25,9},{2,18},{10... | collective-permute-start | bytes 786440 | tf_op jit(solution)/shard_map/ppermute | solution.py:37
  80.5 19.4 %collective-permute-start.17 = (bf16[256,1024]{1,0:T(8,128)(2,1)S(1)}, bf16[256,1024]{1,0:T(8,128)(2,1)S(1)}, u32[]{:S(2)}, u32[]{:S(2)}) collective-permute-start(bf16[256,1024]{1,0:T(8,128)(2,1)S(1)} %constant_dynamic-update-slice_fusion.20), channel_id=1, source_target_pairs={{0,8},{8,0},{16,24},{24,16},{1,9},{9,1},{17,25},{25,17},{2,10},{10... | collective-permute-start | bytes 1572872 | tf_op jit(solution)/shard_map/ppermute | solution.py:37
  82.3 17.7 %collective-permute-start.20 = (bf16[512,512]{0,1:T(8,128)(2,1)S(1)}, bf16[512,512]{0,1:T(8,128)(2,1)S(1)}, u32[]{:S(2)}, u32[]{:S(2)}) collective-permute-start(bf16[512,512]{0,1:T(8,128)(2,1)S(1)} %get-tuple-element.110), channel_id=1, source_target_pairs={{0,4},{4,0},{1,5},{5,1},{2,6},{6,2},{3,7},{7,3},{8,12},{12,8},{9,1... | collective-permute-start | bytes 1572872 | tf_op jit(solution)/shard_map/ppermute | solution.py:37
  86.0 16.3 %collective-permute-start.19 = (bf16[256,512]{1,0:T(8,128)(2,1)S(1)}, bf16[256,512]{1,0:T(8,128)(2,1)S(1)}, u32[]{:S(2)}, u32[]{:S(2)}) collective-permute-start(bf16[256,512]{1,0:T(8,128)(2,1)S(1)} %fusion.10), channel_id=1, source_target_pairs={{0,4},{4,0},{1,5},{5,1},{2,6},{6,2},{3,7},{7,3},{8,12},{12,8},{9,1... | collective-permute-start | bytes 786440 | tf_op jit(solution)/shard_map/ppermute | solution.py:37
  86.2 16.2 %collective-permute-start.16 = (bf16[256,1024]{1,0:T(8,128)(2,1)S(1)}, bf16[256,1024]{1,0:T(8,128)(2,1)S(1)}, u32[]{:S(2)}, u32[]{:S(2)}) collective-permute-start(bf16[256,1024]{1,0:T(8,128)(2,1)S(1)} %slice.1373), channel_id=1, source_target_pairs={{0,2},{1,3},{2,0},{3,1},{4,6},{5,7},{6,4},{7,5},{8,10},{9,11},{10,... | collective-permute-start | bytes 1572872 | tf_op jit(solution)/shard_map/ppermute | solution.py:37
  118.2 14.3 %collective-permute-start.25 = (bf16[512,512]{1,0:T(8,128)(2,1)S(1)}, bf16[512,512]{1,0:T(8,128)(2,1)S(1)}, u32[]{:S(2)}, u32[]{:S(2)}) collective-permute-start(bf16[512,512]{1,0:T(8,128)(2,1)S(1)} %get-tuple-element.119), channel_id=1, source_target_pairs={{0,4},{4,0},{1,5},{5,1},{2,6},{6,2},{3,7},{7,3},{8,12},{12,8},{9,1... | collective-permute-start | bytes 1572872 | tf_op jit(solution)/shard_map/ppermute | solution.py:37
  133.1 14.4 %collective-permute-start.28 = (bf16[512,512]{0,1:T(8,128)(2,1)S(1)}, bf16[512,512]{0,1:T(8,128)(2,1)S(1)}, u32[]{:S(2)}, u32[]{:S(2)}) collective-permute-start(bf16[512,512]{0,1:T(8,128)(2,1)S(1)} %get-tuple-element.122), channel_id=1, source_target_pairs={{0,4},{4,0},{1,5},{5,1},{2,6},{6,2},{3,7},{7,3},{8,12},{12,8},{9,1... | collective-permute-start | bytes 1572872 | tf_op jit(solution)/shard_map/ppermute | solution.py:37
  136.2 14.0 %collective-permute-start.27 = (bf16[256,1024]{1,0:T(8,128)(2,1)S(1)}, bf16[256,1024]{1,0:T(8,128)(2,1)S(1)}, u32[]{:S(2)}, u32[]{:S(2)}) collective-permute-start(bf16[256,1024]{1,0:T(8,128)(2,1)S(1)} %slice.1372), channel_id=1, source_target_pairs={{0,2},{1,3},{2,0},{3,1},{4,6},{5,7},{6,4},{7,5},{8,10},{9,11},{10,... | collective-permute-start | bytes 1572872 | tf_op jit(solution)/shard_map/ppermute | solution.py:37
  176.6 14.0 %collective-permute-start.33 = (bf16[256,1024]{1,0:T(8,128)(2,1)S(1)}, bf16[256,1024]{1,0:T(8,128)(2,1)S(1)}, u32[]{:S(2)}, u32[]{:S(2)}) collective-permute-start(bf16[256,1024]{1,0:T(8,128)(2,1)S(1)} %slice.1371), channel_id=1, source_target_pairs={{0,2},{1,3},{2,0},{3,1},{4,6},{5,7},{6,4},{7,5},{8,10},{9,11},{10,... | collective-permute-start | bytes 1572872 | tf_op jit(solution)/shard_map/ppermute | solution.py:37
  226.8 14.3 %collective-permute-start.37 = (bf16[256,1024]{1,0:T(8,128)(2,1)S(1)}, bf16[256,1024]{1,0:T(8,128)(2,1)S(1)}, u32[]{:S(2)}, u32[]{:S(2)}) collective-permute-start(bf16[256,1024]{1,0:T(8,128)(2,1)S(1)} %slice.1370), channel_id=1, source_target_pairs={{0,2},{1,3},{2,0},{3,1},{4,6},{5,7},{6,4},{7,5},{8,10},{9,11},{10,... | collective-permute-start | bytes 1572872 | tf_op jit(solution)/shard_map/ppermute | solution.py:37
  229.2 38.5 %collective-permute-start.62 = (bf16[512,1024]{1,0:T(8,128)(2,1)S(1)}, bf16[512,1024]{1,0:T(8,128)(2,1)S(1)}, u32[]{:S(2)}, u32[]{:S(2)}) collective-permute-start(bf16[512,1024]{1,0:T(8,128)(2,1)S(1)} %convolution_convert_fusion), channel_id=1, source_target_pairs={{0,4},{4,0},{1,5},{5,1},{2,6},{6,2},{3,7},{7,3},{8,12},{12,8},{9,1... | collective-permute-start | bytes 3145736 | tf_op jit(solution)/shard_map/ppermute | solution.py:37
  243.9 33.1 %collective-permute-start.59 = (bf16[512,1024]{1,0:T(8,128)(2,1)S(1)}, bf16[512,1024]{1,0:T(8,128)(2,1)S(1)}, u32[]{:S(2)}, u32[]{:S(2)}) collective-permute-start(bf16[512,1024]{1,0:T(8,128)(2,1)S(1)} %convolution_convert_fusion.1), channel_id=1, source_target_pairs={{0,4},{4,0},{1,5},{5,1},{2,6},{6,2},{3,7},{7,3},{8,12},{12,8},{9,1... | collective-permute-start | bytes 3145736 | tf_op jit(solution)/shard_map/ppermute | solution.py:37
  268.2 14.3 %collective-permute-start.63 = (bf16[256,1024]{1,0:T(8,128)(2,1)S(1)}, bf16[256,1024]{1,0:T(8,128)(2,1)S(1)}, u32[]{:S(2)}, u32[]{:S(2)}) collective-permute-start(bf16[256,1024]{1,0:T(8,128)(2,1)S(1)} %slice.1365), channel_id=1, source_target_pairs={{0,8},{8,0},{16,24},{24,16},{1,9},{9,1},{17,25},{25,17},{2,10},{10... | collective-permute-start | bytes 1572872 | tf_op jit(solution)/shard_map/ppermute | solution.py:37
  284.5 19.0 %collective-permute-start.60 = (bf16[256,1024]{1,0:T(8,128)(2,1)}, bf16[256,1024]{1,0:T(8,128)(2,1)}, u32[]{:S(2)}, u32[]{:S(2)}) collective-permute-start(bf16[256,1024]{1,0:T(8,128)(2,1)} %slice.1366), channel_id=1, source_target_pairs={{0,8},{8,0},{16,24},{24,16},{1,9},{9,1},{17,25},{25,17},{2,10},{10... | collective-permute-start | bytes 1572872 | tf_op jit(solution)/shard_map/ppermute | solution.py:37
  286.0 30.1 %collective-permute-start.64 = (bf16[128,1024]{1,0:T(8,128)(2,1)}, bf16[128,1024]{1,0:T(8,128)(2,1)S(1)}, u32[]{:S(2)}, u32[]{:S(2)}) collective-permute-start(bf16[128,1024]{1,0:T(8,128)(2,1)} %slice.1375), channel_id=1, source_target_pairs={{0,16},{8,24},{16,0},{24,8},{1,17},{9,25},{17,1},{25,9},{2,18},{10... | collective-permute-start | bytes 786440 | tf_op jit(solution)/shard_map/ppermute | solution.py:37
  289.4 16.7 %collective-permute-start.50 = (bf16[128,1024]{1,0:T(8,128)(2,1)}, bf16[128,1024]{1,0:T(8,128)(2,1)}, u32[]{:S(2)}, u32[]{:S(2)}) collective-permute-start(bf16[128,1024]{1,0:T(8,128)(2,1)} %convolution_convert_fusion.10), channel_id=1, source_target_pairs={{0,1},{1,0},{2,3},{3,2},{4,5},{5,4},{6,7},{7,6},{8,9},{9,8},{10,11... | collective-permute-start | bytes 786440 | tf_op jit(solution)/shard_map/ppermute | solution.py:37
  290.8 35.0 %collective-permute-start.45 = (bf16[512,1024]{0,1:T(8,128)(2,1)}, bf16[512,1024]{0,1:T(8,128)(2,1)}, u32[]{:S(2)}, u32[]{:S(2)}) collective-permute-start(bf16[512,1024]{0,1:T(8,128)(2,1)} %pad_maximum_fusion.15), channel_id=1, source_target_pairs={{0,4},{4,0},{1,5},{5,1},{2,6},{6,2},{3,7},{7,3},{8,12},{12,8},{9,1... | collective-permute-start | bytes 3145736 | tf_op jit(solution)/shard_map/ppermute | solution.py:37
  299.0 20.5 %collective-permute-start.42 = (bf16[256,1024]{1,0:T(8,128)(2,1)S(1)}, bf16[256,1024]{1,0:T(8,128)(2,1)}, u32[]{:S(2)}, u32[]{:S(2)}) collective-permute-start(bf16[256,1024]{1,0:T(8,128)(2,1)S(1)} %get-tuple-element.293), channel_id=1, source_target_pairs={{0,2},{1,3},{2,0},{3,1},{4,6},{5,7},{6,4},{7,5},{8,10},{9,11},{10,... | collective-permute-start | bytes 1572872 | tf_op jit(solution)/shard_map/ppermute | solution.py:37
  314.5 28.7 %collective-permute-start.61 = (bf16[128,1024]{1,0:T(8,128)(2,1)}, bf16[128,1024]{1,0:T(8,128)(2,1)}, u32[]{:S(2)}, u32[]{:S(2)}) collective-permute-start(bf16[128,1024]{1,0:T(8,128)(2,1)} %slice.1376), channel_id=1, source_target_pairs={{0,16},{8,24},{16,0},{24,8},{1,17},{9,25},{17,1},{25,9},{2,18},{10... | collective-permute-start | bytes 786440 | tf_op jit(solution)/shard_map/ppermute | solution.py:37
  333.6 38.2 %collective-permute-start.47 = (bf16[1024,512]{1,0:T(8,128)(2,1)S(1)}, bf16[1024,512]{1,0:T(8,128)(2,1)S(1)}, u32[]{:S(2)}, u32[]{:S(2)}) collective-permute-start(bf16[1024,512]{1,0:T(8,128)(2,1)S(1)} %get-tuple-element.139), channel_id=1, source_target_pairs={{4,0},{5,1},{6,2},{7,3},{12,8},{13,9},{14,10},{15,11},{20,16},{21,... | collective-permute-start | bytes 3145736 | tf_op jit(solution)/shard_map/ppermute | solution.py:43
  335.3 53.9 %collective-permute-start.55 = (bf16[512,256]{1,0:T(8,128)(2,1)}, bf16[512,256]{1,0:T(8,128)(2,1)}, u32[]{:S(2)}, u32[]{:S(2)}) collective-permute-start(bf16[512,256]{1,0:T(8,128)(2,1)} %convolution_convert_fusion.9), channel_id=1, source_target_pairs={{0,4},{4,0},{1,5},{5,1},{2,6},{6,2},{3,7},{7,3},{8,12},{12,8},{9,1... | collective-permute-start | bytes 786440 | tf_op jit(solution)/shard_map/ppermute | solution.py:37
  368.0 26.4 %collective-permute-start.52 = (bf16[512,768]{1,0:T(8,128)(2,1)}, bf16[512,768]{1,0:T(8,128)(2,1)S(1)}, u32[]{:S(2)}, u32[]{:S(2)}) collective-permute-start(bf16[512,768]{1,0:T(8,128)(2,1)} %add_convert_fusion.4), channel_id=1, source_target_pairs={{0,4},{4,0},{1,5},{5,1},{2,6},{6,2},{3,7},{7,3},{8,12},{12,8},{9,1... | collective-permute-start | bytes 2359304 | tf_op jit(solution)/shard_map/ppermute | solution.py:37
  387.4 25.5 %collective-permute-start.49 = (bf16[256,1024]{1,0:T(8,128)(2,1)}, bf16[256,1024]{1,0:T(8,128)(2,1)}, u32[]{:S(2)}, u32[]{:S(2)}) collective-permute-start(bf16[256,1024]{1,0:T(8,128)(2,1)} %slice.1367), channel_id=1, source_target_pairs={{0,2},{1,3},{2,0},{3,1},{4,6},{5,7},{6,4},{7,5},{8,10},{9,11},{10,... | collective-permute-start | bytes 1572872 | tf_op jit(solution)/shard_map/ppermute | solution.py:37
  (158 other events, 1218.3 us)

commit v5 on v4

--- a/solution.py
+++ b/solution.py
@@ -4,6 +4,7 @@
 import jax.numpy as jnp
 from jax import lax
 from jax.experimental import pallas as pl
+from jax.experimental.layout import Layout, with_layout_constraint
 from jax.experimental.pallas import tpu as pltpu
 from jax.sharding import PartitionSpec as P
 
@@ -74,10 +75,12 @@
     return total
 
 
-def scatter_tree(make, size, steps, used=None, start=None):
+def scatter_tree(make, size, steps, used=None, start=None, far=None):
     axis, bit = steps[-1]
     half = size // 2
-    arrived = swap(after(low(make(slice(half, size))), start), axis, bit)
+    if far is None:
+        far = low(make(slice(half, size)))
+    arrived = swap(after(far, start), axis, bit)
     total = after(make(slice(0, half)), used) + wide(arrived)
     return scatter_more(total, steps[:-1])
 
@@ -467,6 +470,7 @@
     out_far = gather_tree(own_half(out_weight.T), far_steps, qkv_far)
     out_near = gather_tree(out_far, near_steps, qkv_near)
     small_own = jnp.concatenate([memory_key, memory_value, memory_query, memory_out.T], axis=1)
+    small_own = with_layout_constraint(small_own, Layout((0, 1)))
     small_far = gather_tree(own_half(small_own), far_steps, qkv_near)
     up_own = own_half(up_weight)
     down_own = own_half(down_weight.T)
@@ -650,14 +654,19 @@
     query_start, old_back = attend_back(
         width, "old", qkv, grad_self, mixed_t, self_lse, old_kv, meta, lower
     )
-    back = shift(old_back, "ctx", -1)
+    out_terms = weight_terms((self_rows, mixed))
+    out_far = low(out_terms(slice(model // 2, model)))
+    back = shift(after(old_back, out_far), "ctx", -1)
+    out_part = scatter_tree(out_terms, model, ctx_steps, query_start, None, out_far)
     small_near_grads = scatter_more(small_part, near_steps, None, old_back)
-    grad_self_later = after(grad_self, small_near_grads, query_start)
+    grad_self_later = after(grad_self, small_near_grads, query_start, out_part)
     query_back, kv_back = attend_back(
         width, "own", qkv, grad_self_later, mixed_t, self_lse, None, meta, lower, query_start
     )
+    out_near_grads = scatter_more(out_part, near_steps, None, query_back)
     query_pre = query_back * 0.125
     small_grads = scatter_more(small_near_grads, far_steps, None, query_pre)
+    small_grads = with_layout_constraint(small_grads, Layout((0, 1)))
     own_back = jnp.concatenate([query_pre, kv_back], axis=1)
 
     def qkv_terms(s):
@@ -677,8 +686,7 @@
     qkv_grads = scatter_more(
         scatter_tree(qkv_terms, model, ctx_steps, sent), weight_steps[: -len(ctx_steps)]
     )
-    out_part = scatter_tree(weight_terms((self_rows, mixed)), model, ctx_steps, sent)
-    out_grads = scatter_more(out_part, steps_of("shard"))
+    out_grads = scatter_more(out_near_grads, far_steps, None, sent)
 
     everywhere = jnp.stack(
         [

time: 428 us -> 418 us (0.977)
  local copies, waits for them, and re-layouts: 41 us -> 32.1 us
    unnamed x259 -> x251, local copies, waits for them, and re-layouts: 26.1 us -> 16.8 us
  transfers between devices with their start and end apart: 70 -> 70, of which waited for: 40 -> 42; matrix products, arithmetic and copies ran while one was open for 24% -> 23% of each run, Pallas kernels for 7% -> 7%
where the time goes in v5:
time: 418 us; the launch traced here: 412 us
  waiting for transfers between devices  171 us (41%)
  starting transfers between devices  76.9 us (18%)
  other arithmetic  48.7 us (12%)
  matrix products  48.7 us (12%)
  local copies, waits for them, and re-layouts  32.1 us (8%)
  Pallas kernels  30.7 us (7%)
    ppermute x68, waiting for transfers between devices, swap(): lax.ppermute(array, axis, [(i, i ^ bit) for i in range(lax.axis_size(axis...  171 us
    ppermute x68, starting transfers between devices, swap(): lax.ppermute(array, axis, [(i, i ^ bit) for i in range(lax.axis_size(axis...  72.1 us
    dot_general x34, matrix products, contract(): return jnp.einsum(form, left, right, preferred_element_type=jnp.float32)  30.6 us
    dot_general x8, matrix products, matmul(): return jnp.dot(left, right, preferred_element_type=jnp.float32)  18.2 us
    pallas_call x3, Pallas kernels, attend_back(): pl.pallas_call(partial(attend_back_kernel, width, kind), in_specs=specs,...  18.1 us
    unnamed x251, local copies, waits for them, and re-layouts  16.8 us
    concatenate x17, other arithmetic, gather_tree(): jnp.concatenate([after(array, used if n == len(steps) - 1 else None), arr...  13.5 us
    pallas_call x2, Pallas kernels, attend(): pl.pallas_call(partial(attend_kernel, width, masked), in_specs=specs, out...  12.5 us
  transfers between devices with their start and end apart: 70, of which 42 were waited for; matrix products, arithmetic and copies ran while one was open for 23% of the time, Pallas kernels for 7%

profile of v5, /device:TPU:0, one launch (start us, length us, event | category | flops | bytes accessed | tf_op | source)
XLA Modules:
  0.0 411.9 jit_solution(2420013120476020840)
XLA Ops:
  1.8 4.1 collective-permute-start.2
  5.9 3.4 collective-permute-start.9
  26.8 5.0 %collective-permute-done.3 = bf16[256,768]{1,0:T(8,128)(2,1)S(1)} collective-permute-done((bf16[256,768]{1,0:T(8,128)(2,1)S(1)}, bf16[256,768]{1,0:T(8,128)(2,1)S(1)}, u32[]{:S(2)}, u32[]{:S(2)}) %collective-permute-start.3) | collective-permute-done | bytes 393248 | tf_op jit(solution)/shard_map/ppermute | solution.py:38
  41.3 5.9 %collective-permute-done.7 = bf16[128,1024]{1,0:T(8,128)(2,1)S(1)} collective-permute-done((bf16[128,1024]{1,0:T(8,128)(2,1)}, bf16[128,1024]{1,0:T(8,128)(2,1)S(1)}, u32[]{:S(2)}, u32[]{:S(2)}) %collective-permute-start.7) | collective-permute-done | bytes 262176 | tf_op jit(solution)/shard_map/ppermute | solution.py:38
  55.3 2.9 multiply_convert_fusion.2.refs_2_.refs_3_
  66.3 8.1 %shard_map.484 = (bf16[1024,256]{1,0:T(8,128)(2,1)S(1)}, f32[256,1024]{1,0:T(8,128)S(1)}, f32[4,1024]{1,0:T(4,128)S(1)}) custom-call(s32[5]{0:T(128)S(1)} %pad_add_fusion.1.refs_0_, s32[1,1024]{1,0:T(1,128)S(1)} %maximum_subtract_fusion.refs_1_, bf16[1024,768]{1,0:T(8,128)(2,1)S(1)} %multiply_convert_fusion.2.refs_2_.refs_3_, ...), custom_call_target="tpu_custom_call" | custom-call | flops 12884901888 | bytes 2097152 | tf_op jit(solution)/shard_map/pallas_call | solution.py:330
  78.5 3.7 collective-permute-start.20
  84.7 7.0 %collective-permute-done.18 = bf16[128,1024]{0,1:T(8,128)(2,1)S(1)} collective-permute-done((bf16[128,1024]{0,1:T(8,128)(2,1)S(1)}, bf16[128,1024]{0,1:T(8,128)(2,1)S(1)}, u32[]{:S(2)}, u32[]{:S(2)}) %collective-permute-start.18) | collective-permute-done | bytes 262176 | tf_op jit(solution)/shard_map/ppermute | solution.py:38
  91.8 5.3 %collective-permute-done.17 = bf16[256,1024]{1,0:T(8,128)(2,1)S(1)} collective-permute-done((bf16[256,1024]{1,0:T(8,128)(2,1)S(1)}, bf16[256,1024]{1,0:T(8,128)(2,1)S(1)}, u32[]{:S(2)}, u32[]{:S(2)}) %collective-permute-start.17) | collective-permute-done | bytes 524320 | tf_op jit(solution)/shard_map/ppermute | solution.py:38
  104.0 9.4 %collective-permute-done.21 = bf16[256,1024]{1,0:T(8,128)(2,1)S(1)} collective-permute-done((bf16[256,1024]{1,0:T(8,128)(2,1)S(1)}, bf16[256,1024]{1,0:T(8,128)(2,1)S(1)}, u32[]{:S(2)}, u32[]{:S(2)}) %collective-permute-start.21) | collective-permute-done | bytes 524320 | tf_op jit(solution)/shard_map/ppermute | solution.py:38
  119.5 4.4 %shard_map.485 = (bf16[1024,256]{1,0:T(8,128)(2,1)S(1)}, f32[256,1024]{1,0:T(8,128)S(1)}, f32[4,1024]{1,0:T(4,128)S(1)}) custom-call(bf16[1024,256]{1,0:T(8,128)(2,1)S(1)} %fusion.9.refs_0_, bf16[512,512]{1,0:T(8,128)(2,1)S(1)} %pad_maximum_fusion.21.refs_1_.refs_4_), custom_call_target="tpu_custom_call" | custom-call | flops 6442450944 | bytes 2097152 | tf_op jit(solution)/shard_map/pallas_call | solution.py:330
  124.0 5.1 %collective-permute-done.25 = bf16[512,512]{1,0:T(8,128)(2,1)S(1)} collective-permute-done((bf16[512,512]{1,0:T(8,128)(2,1)S(1)}, bf16[512,512]{1,0:T(8,128)(2,1)S(1)}, u32[]{:S(2)}, u32[]{:S(2)}) %collective-permute-start.25) | collective-permute-done | bytes 524320 | tf_op jit(solution)/shard_map/ppermute | solution.py:38
  133.9 10.2 %collective-permute-done.28 = bf16[512,512]{0,1:T(8,128)(2,1)S(1)} collective-permute-done((bf16[512,512]{0,1:T(8,128)(2,1)S(1)}, bf16[512,512]{0,1:T(8,128)(2,1)S(1)}, u32[]{:S(2)}, u32[]{:S(2)}) %collective-permute-start.28) | collective-permute-done | bytes 524320 | tf_op jit(solution)/shard_map/ppermute | solution.py:38
  150.4 10.8 %collective-permute-done.29 = bf16[256,1024]{1,0:T(8,128)(2,1)S(1)} collective-permute-done((bf16[256,1024]{1,0:T(8,128)(2,1)S(1)}, bf16[256,1024]{1,0:T(8,128)(2,1)S(1)}, u32[]{:S(2)}, u32[]{:S(2)}) %collective-permute-start.29) | collective-permute-done | bytes 524320 | tf_op jit(solution)/shard_map/ppermute | solution.py:38
  164.6 3.2 multiply_convert_fusion.1
  174.2 12.7 %collective-permute-done.33 = bf16[256,1024]{1,0:T(8,128)(2,1)S(1)} collective-permute-done((bf16[256,1024]{1,0:T(8,128)(2,1)S(1)}, bf16[256,1024]{1,0:T(8,128)(2,1)S(1)}, u32[]{:S(2)}, u32[]{:S(2)}) %collective-permute-start.33) | collective-permute-done | bytes 524320 | tf_op jit(solution)/shard_map/ppermute | solution.py:38
  189.9 12.0 %collective-permute-done.34 = bf16[256,1024]{1,0:T(8,128)(2,1)S(1)} collective-permute-done((bf16[256,1024]{1,0:T(8,128)(2,1)S(1)}, bf16[256,1024]{1,0:T(8,128)(2,1)S(1)}, u32[]{:S(2)}, u32[]{:S(2)}) %collective-permute-start.34) | collective-permute-done | bytes 524320 | tf_op jit(solution)/shard_map/ppermute | solution.py:38
  204.7 7.0 %convert_reduce_fusion = (f32[1024]{0:T(1024)}, bf16[1024,1024]{1,0:T(8,128)(2,1)S(1)}) fusion(f32[1024,1024]{1,0:T(8,128)S(1)} %get-tuple-element.434, f32[1024]{0:T(1024)S(1)} %copy-done.108, bf16[1024,1024]{0,1:T(8,128)(2,1)S(1)} %pad_maximum_fusion.4, bf16[512,1024]{1,0:T(8,128)(2,1)S(1)} %collective-permute-done.35, ...), kind=kOutput, calls=%fused_computation.6 | convolution fusion | flops 2169502720 | bytes 10493952 | tf_op jit(solution)/shard_map/dot_general | solution.py:22
  228.8 9.0 %collective-permute-done.37 = bf16[256,1024]{1,0:T(8,128)(2,1)S(1)} collective-permute-done((bf16[256,1024]{1,0:T(8,128)(2,1)S(1)}, bf16[256,1024]{1,0:T(8,128)(2,1)S(1)}, u32[]{:S(2)}, u32[]{:S(2)}) %collective-permute-start.37) | collective-permute-done | bytes 524320 | tf_op jit(solution)/shard_map/ppermute | solution.py:38
  242.3 10.5 %collective-permute-done.38 = bf16[256,1024]{1,0:T(8,128)(2,1)S(1)} collective-permute-done((bf16[256,1024]{1,0:T(8,128)(2,1)S(1)}, bf16[256,1024]{1,0:T(8,128)(2,1)S(1)}, u32[]{:S(2)}, u32[]{:S(2)}) %collective-permute-start.38) | collective-permute-done | bytes 524320 | tf_op jit(solution)/shard_map/ppermute | solution.py:38
  257.1 6.6 %shard_map.486 = (bf16[1024,256]{1,0:T(8,128)(2,1)S(1)}, f32[512,512]{1,0:T(8,128)S(1)}) custom-call(bf16[1024,256]{1,0:T(8,128)(2,1)S(1)} %fusion.9.refs_0_, bf16[1024,256]{1,0:T(8,128)(2,1)S(1)} %convolution_convert_fusion.8.refs_1_, f32[256,1024]{1,0:T(8,128)S(1)} %copy-done.5, f32[4,1024]{1,0:T(4,128)S(1)} %get-tuple-element.133.refs_3_, ...), custom_call_target="tpu_custom_call" | custom-call | flops 8589934592 | bytes 4194304 | tf_op jit(solution)/shard_map/pallas_call | solution.py:357
  269.0 4.7 %collective-permute-done.59 = bf16[512,1024]{1,0:T(8,128)(2,1)S(1)} collective-permute-done((bf16[512,1024]{1,0:T(8,128)(2,1)S(1)}, bf16[512,1024]{1,0:T(8,128)(2,1)S(1)}, u32[]{:S(2)}, u32[]{:S(2)}) %collective-permute-start.59) | collective-permute-done | bytes 1048608 | tf_op jit(solution)/shard_map/ppermute | solution.py:38
  296.8 3.4 collective-permute-done.60
  307.4 3.7 collective-permute-done.65
  331.0 4.9 %collective-permute-start.47 = (bf16[512,256]{1,0:T(8,128)(2,1)S(1)}, bf16[512,256]{1,0:T(8,128)(2,1)S(1)}, u32[]{:S(2)}, u32[]{:S(2)}) collective-permute-start(bf16[512,256]{1,0:T(8,128)(2,1)S(1)} %convolution_convert_fusion.10), channel_id=1, source_target_pairs={{0,4},{4,0},{1,5},{5,1},{2,6},{6,2},{3,7},{7,3},{8,12},{12,8},{9,1... | collective-permute-start | bytes 786440 | tf_op jit(solution)/shard_map/ppermute | solution.py:38
  335.8 2.8 collective-permute-start.46
  342.7 3.3 collective-permute-start.56
  345.9 5.5 %collective-permute-done.46 = bf16[256,1024]{1,0:T(8,128)(2,1)S(1)} collective-permute-done((bf16[256,1024]{1,0:T(8,128)(2,1)S(1)}, bf16[256,1024]{1,0:T(8,128)(2,1)S(1)}, u32[]{:S(2)}, u32[]{:S(2)}) %collective-permute-start.46) | collective-permute-done | bytes 524320 | tf_op jit(solution)/shard_map/ppermute | solution.py:38
  351.6 10.4 %shard_map.488 = (bf16[1024,256]{1,0:T(8,128)(2,1)S(1)}, bf16[1024,512]{1,0:T(8,128)(2,1)S(1)}) custom-call(s32[5]{0:T(128)S(1)} %pad_add_fusion.1.refs_0_, s32[1,1024]{1,0:T(1,128)S(1)} %maximum_subtract_fusion.refs_1_, f32[256,1024]{1,0:T(8,128)S(1)} %get-tuple-element.141.refs_2_, bf16[1024,768]{1,0:T(8,128)(2,1)S(1)} %copy-done.3, ...), custom_call_target="tpu_custom_call" | custom-call | flops 17179869184 | bytes 4194304 | tf_op jit(solution)/shard_map/pallas_call | solution.py:357
  373.1 4.6 %collective-permute-done.58 = bf16[128,1024]{1,0:T(8,128)(2,1)S(1)} collective-permute-done((bf16[128,1024]{1,0:T(8,128)(2,1)S(1)}, bf16[128,1024]{1,0:T(8,128)(2,1)S(1)}, u32[]{:S(2)}, u32[]{:S(2)}) %collective-permute-start.58) | collective-permute-done | bytes 262176 | tf_op jit(solution)/shard_map/ppermute | solution.py:38
  394.4 6.3 %collective-permute-done.54 = bf16[256,768]{1,0:T(8,128)(2,1)S(1)} collective-permute-done((bf16[256,768]{1,0:T(8,128)(2,1)S(1)}, bf16[256,768]{1,0:T(8,128)(2,1)S(1)}, u32[]{:S(2)}, u32[]{:S(2)}) %collective-permute-start.54) | collective-permute-done | bytes 393248 | tf_op jit(solution)/shard_map/ppermute | solution.py:38
  404.5 6.3 %collective-permute-done.55 = bf16[128,768]{1,0:T(8,128)(2,1)S(1)} collective-permute-done((bf16[128,768]{1,0:T(8,128)(2,1)S(1)}, bf16[128,768]{1,0:T(8,128)(2,1)S(1)}, u32[]{:S(2)}, u32[]{:S(2)}) %collective-permute-start.55) | collective-permute-done | bytes 196640 | tf_op jit(solution)/shard_map/ppermute | solution.py:38
  (640 shorter events, 206.0 us)
Async XLA Ops:
  1.8 18.5 %collective-permute-start.2 = (bf16[128,768]{1,0:T(8,128)(2,1)S(1)}, bf16[128,768]{1,0:T(8,128)(2,1)S(1)}, u32[]{:S(2)}, u32[]{:S(2)}) collective-permute-start(bf16[128,768]{1,0:T(8,128)(2,1)S(1)} %fusion.87), channel_id=1, source_target_pairs={{0,16},{8,24},{16,0},{24,8},{1,17},{9,25},{17,1},{25,9},{2,18},{10... | collective-permute-start | bytes 589832 | tf_op jit(solution)/shard_map/ppermute | solution.py:38
  5.9 16.4 %collective-permute-start.9 = (bf16[256,1024]{1,0:T(8,128)(2,1)}, bf16[256,1024]{1,0:T(8,128)(2,1)S(1)}, u32[]{:S(2)}, u32[]{:S(2)}) collective-permute-start(bf16[256,1024]{1,0:T(8,128)(2,1)} %bitcast.116), channel_id=1, source_target_pairs={{0,4},{1,5},{2,6},{3,7},{8,12},{9,13},{10,14},{11,15},{16,20},{17,... | collective-permute-start | bytes 1572872 | tf_op jit(solution)/shard_map/ppermute | solution.py:44
  26.5 25.8 %collective-permute-start.1 = (bf16[512,1024]{1,0:T(8,128)(2,1)}, bf16[512,1024]{1,0:T(8,128)(2,1)}, u32[]{:S(2)}, u32[]{:S(2)}) collective-permute-start(bf16[512,1024]{1,0:T(8,128)(2,1)} %pad_maximum_fusion.10), channel_id=1, source_target_pairs={{0,1},{1,0},{2,3},{3,2},{4,5},{5,4},{6,7},{7,6},{8,9},{9,8},{10,11... | collective-permute-start | bytes 3145736 | tf_op jit(solution)/shard_map/ppermute | solution.py:38
  32.8 17.8 %collective-permute-start.4 = (bf16[512,768]{1,0:T(8,128)(2,1)}, bf16[512,768]{1,0:T(8,128)(2,1)}, u32[]{:S(2)}, u32[]{:S(2)}) collective-permute-start(bf16[512,768]{1,0:T(8,128)(2,1)} %pad_maximum_fusion.18), channel_id=1, source_target_pairs={{0,4},{4,0},{1,5},{5,1},{2,6},{6,2},{3,7},{7,3},{8,12},{12,8},{9,1... | collective-permute-start | bytes 2359304 | tf_op jit(solution)/shard_map/ppermute | solution.py:38
  32.9 15.4 %collective-permute-start.10 = (bf16[256,1024]{1,0:T(8,128)(2,1)S(1)}, bf16[256,1024]{1,0:T(8,128)(2,1)S(1)}, u32[]{:S(2)}, u32[]{:S(2)}) collective-permute-start(bf16[256,1024]{1,0:T(8,128)(2,1)S(1)} %constant_dynamic-update-slice_fusion.10), channel_id=1, source_target_pairs={{0,2},{1,3},{2,0},{3,1},{4,6},{5,7},{6,4},{7,5},{8,10},{9,11},{10,... | collective-permute-start | bytes 1572872 | tf_op jit(solution)/shard_map/ppermute | solution.py:38
  48.4 15.2 %collective-permute-start.11 = (bf16[512,1024]{1,0:T(8,128)(2,1)S(1)}, bf16[512,1024]{1,0:T(8,128)(2,1)S(1)}, u32[]{:S(2)}, u32[]{:S(2)}) collective-permute-start(bf16[512,1024]{1,0:T(8,128)(2,1)S(1)} %pad_maximum_fusion.11), channel_id=1, source_target_pairs={{0,1},{1,0},{2,3},{3,2},{4,5},{5,4},{6,7},{7,6},{8,9},{9,8},{10,11... | collective-permute-start | bytes 3145736 | tf_op jit(solution)/shard_map/ppermute | solution.py:38
  52.0 22.8 %collective-permute-start.14 = (bf16[512,256]{0,1:T(8,128)(2,1)S(1)}, bf16[512,256]{0,1:T(8,128)(2,1)S(1)}, u32[]{:S(2)}, u32[]{:S(2)}) collective-permute-start(bf16[512,256]{0,1:T(8,128)(2,1)S(1)} %pad_maximum_fusion.23), channel_id=1, source_target_pairs={{0,4},{4,0},{1,5},{5,1},{2,6},{6,2},{3,7},{7,3},{8,12},{12,8},{9,1... | collective-permute-start | bytes 786440 | tf_op jit(solution)/shard_map/ppermute | solution.py:38
  60.3 14.2 %collective-permute-start.13 = (bf16[128,1024]{1,0:T(8,128)(2,1)S(1)}, bf16[128,1024]{1,0:T(8,128)(2,1)S(1)}, u32[]{:S(2)}, u32[]{:S(2)}) collective-permute-start(bf16[128,1024]{1,0:T(8,128)(2,1)S(1)} %constant_dynamic-slice_fusion), channel_id=1, source_target_pairs={{0,16},{8,24},{16,0},{24,8},{1,17},{9,25},{17,1},{25,9},{2,18},{10... | collective-permute-start | bytes 786440 | tf_op jit(solution)/shard_map/ppermute | solution.py:38
  77.1 14.6 %collective-permute-start.18 = (bf16[128,1024]{0,1:T(8,128)(2,1)S(1)}, bf16[128,1024]{0,1:T(8,128)(2,1)S(1)}, u32[]{:S(2)}, u32[]{:S(2)}) collective-permute-start(bf16[128,1024]{0,1:T(8,128)(2,1)S(1)} %dynamic-slice_bitcast_fusion), channel_id=1, source_target_pairs={{0,16},{8,24},{16,0},{24,8},{1,17},{9,25},{17,1},{25,9},{2,18},{10... | collective-permute-start | bytes 786440 | tf_op jit(solution)/shard_map/ppermute | solution.py:38
  78.0 19.0 %collective-permute-start.17 = (bf16[256,1024]{1,0:T(8,128)(2,1)S(1)}, bf16[256,1024]{1,0:T(8,128)(2,1)S(1)}, u32[]{:S(2)}, u32[]{:S(2)}) collective-permute-start(bf16[256,1024]{1,0:T(8,128)(2,1)S(1)} %constant_dynamic-update-slice_fusion.20), channel_id=1, source_target_pairs={{0,8},{8,0},{16,24},{24,16},{1,9},{9,1},{17,25},{25,17},{2,10},{10... | collective-permute-start | bytes 1572872 | tf_op jit(solution)/shard_map/ppermute | solution.py:38
  78.5 18.6 %collective-permute-start.20 = (bf16[512,512]{1,0:T(8,128)(2,1)S(1)}, bf16[512,512]{1,0:T(8,128)(2,1)S(1)}, u32[]{:S(2)}, u32[]{:S(2)}) collective-permute-start(bf16[512,512]{1,0:T(8,128)(2,1)S(1)} %get-tuple-element.113), channel_id=1, source_target_pairs={{0,4},{4,0},{1,5},{5,1},{2,6},{6,2},{3,7},{7,3},{8,12},{12,8},{9,1... | collective-permute-start | bytes 1572872 | tf_op jit(solution)/shard_map/ppermute | solution.py:38
  83.2 16.4 %collective-permute-start.19 = (bf16[256,512]{1,0:T(8,128)(2,1)S(1)}, bf16[256,512]{1,0:T(8,128)(2,1)S(1)}, u32[]{:S(2)}, u32[]{:S(2)}) collective-permute-start(bf16[256,512]{1,0:T(8,128)(2,1)S(1)} %fusion.10), channel_id=1, source_target_pairs={{0,4},{4,0},{1,5},{5,1},{2,6},{6,2},{3,7},{7,3},{8,12},{12,8},{9,1... | collective-permute-start | bytes 786440 | tf_op jit(solution)/shard_map/ppermute | solution.py:38
  83.4 16.2 %collective-permute-start.16 = (bf16[256,1024]{1,0:T(8,128)(2,1)S(1)}, bf16[256,1024]{1,0:T(8,128)(2,1)S(1)}, u32[]{:S(2)}, u32[]{:S(2)}) collective-permute-start(bf16[256,1024]{1,0:T(8,128)(2,1)S(1)} %slice.1369), channel_id=1, source_target_pairs={{0,2},{1,3},{2,0},{3,1},{4,6},{5,7},{6,4},{7,5},{8,10},{9,11},{10,... | collective-permute-start | bytes 1572872 | tf_op jit(solution)/shard_map/ppermute | solution.py:38
  114.7 14.3 %collective-permute-start.25 = (bf16[512,512]{1,0:T(8,128)(2,1)S(1)}, bf16[512,512]{1,0:T(8,128)(2,1)S(1)}, u32[]{:S(2)}, u32[]{:S(2)}) collective-permute-start(bf16[512,512]{1,0:T(8,128)(2,1)S(1)} %get-tuple-element.122), channel_id=1, source_target_pairs={{0,4},{4,0},{1,5},{5,1},{2,6},{6,2},{3,7},{7,3},{8,12},{12,8},{9,1... | collective-permute-start | bytes 1572872 | tf_op jit(solution)/shard_map/ppermute | solution.py:38
  129.7 14.4 %collective-permute-start.28 = (bf16[512,512]{0,1:T(8,128)(2,1)S(1)}, bf16[512,512]{0,1:T(8,128)(2,1)S(1)}, u32[]{:S(2)}, u32[]{:S(2)}) collective-permute-start(bf16[512,512]{0,1:T(8,128)(2,1)S(1)} %get-tuple-element.125), channel_id=1, source_target_pairs={{0,4},{4,0},{1,5},{5,1},{2,6},{6,2},{3,7},{7,3},{8,12},{12,8},{9,1... | collective-permute-start | bytes 1572872 | tf_op jit(solution)/shard_map/ppermute | solution.py:38
  223.5 14.3 %collective-permute-start.37 = (bf16[256,1024]{1,0:T(8,128)(2,1)S(1)}, bf16[256,1024]{1,0:T(8,128)(2,1)S(1)}, u32[]{:S(2)}, u32[]{:S(2)}) collective-permute-start(bf16[256,1024]{1,0:T(8,128)(2,1)S(1)} %slice.1366), channel_id=1, source_target_pairs={{0,2},{1,3},{2,0},{3,1},{4,6},{5,7},{6,4},{7,5},{8,10},{9,11},{10,... | collective-permute-start | bytes 1572872 | tf_op jit(solution)/shard_map/ppermute | solution.py:38
  226.0 38.4 %collective-permute-start.62 = (bf16[512,1024]{1,0:T(8,128)(2,1)S(1)}, bf16[512,1024]{1,0:T(8,128)(2,1)S(1)}, u32[]{:S(2)}, u32[]{:S(2)}) collective-permute-start(bf16[512,1024]{1,0:T(8,128)(2,1)S(1)} %convolution_convert_fusion), channel_id=1, source_target_pairs={{0,4},{4,0},{1,5},{5,1},{2,6},{6,2},{3,7},{7,3},{8,12},{12,8},{9,1... | collective-permute-start | bytes 3145736 | tf_op jit(solution)/shard_map/ppermute | solution.py:38
  240.7 33.1 %collective-permute-start.59 = (bf16[512,1024]{1,0:T(8,128)(2,1)S(1)}, bf16[512,1024]{1,0:T(8,128)(2,1)S(1)}, u32[]{:S(2)}, u32[]{:S(2)}) collective-permute-start(bf16[512,1024]{1,0:T(8,128)(2,1)S(1)} %convolution_convert_fusion.1), channel_id=1, source_target_pairs={{0,4},{4,0},{1,5},{5,1},{2,6},{6,2},{3,7},{7,3},{8,12},{12,8},{9,1... | collective-permute-start | bytes 3145736 | tf_op jit(solution)/shard_map/ppermute | solution.py:38
  264.8 14.3 %collective-permute-start.63 = (bf16[256,1024]{1,0:T(8,128)(2,1)S(1)}, bf16[256,1024]{1,0:T(8,128)(2,1)S(1)}, u32[]{:S(2)}, u32[]{:S(2)}) collective-permute-start(bf16[256,1024]{1,0:T(8,128)(2,1)S(1)} %slice.1361), channel_id=1, source_target_pairs={{0,8},{8,0},{16,24},{24,16},{1,9},{9,1},{17,25},{25,17},{2,10},{10... | collective-permute-start | bytes 1572872 | tf_op jit(solution)/shard_map/ppermute | solution.py:38
  281.2 19.0 %collective-permute-start.60 = (bf16[256,1024]{1,0:T(8,128)(2,1)}, bf16[256,1024]{1,0:T(8,128)(2,1)}, u32[]{:S(2)}, u32[]{:S(2)}) collective-permute-start(bf16[256,1024]{1,0:T(8,128)(2,1)} %slice.1362), channel_id=1, source_target_pairs={{0,8},{8,0},{16,24},{24,16},{1,9},{9,1},{17,25},{25,17},{2,10},{10... | collective-permute-start | bytes 1572872 | tf_op jit(solution)/shard_map/ppermute | solution.py:38
  282.8 30.3 %collective-permute-start.64 = (bf16[128,1024]{1,0:T(8,128)(2,1)}, bf16[128,1024]{1,0:T(8,128)(2,1)S(1)}, u32[]{:S(2)}, u32[]{:S(2)}) collective-permute-start(bf16[128,1024]{1,0:T(8,128)(2,1)} %slice.1371), channel_id=1, source_target_pairs={{0,16},{8,24},{16,0},{24,8},{1,17},{9,25},{17,1},{25,9},{2,18},{10... | collective-permute-start | bytes 786440 | tf_op jit(solution)/shard_map/ppermute | solution.py:38
  286.3 16.3 %collective-permute-start.51 = (bf16[128,1024]{1,0:T(8,128)(2,1)}, bf16[128,1024]{1,0:T(8,128)(2,1)}, u32[]{:S(2)}, u32[]{:S(2)}) collective-permute-start(bf16[128,1024]{1,0:T(8,128)(2,1)} %convolution_convert_fusion.9), channel_id=1, source_target_pairs={{0,1},{1,0},{2,3},{3,2},{4,5},{5,4},{6,7},{7,6},{8,9},{9,8},{10,11... | collective-permute-start | bytes 786440 | tf_op jit(solution)/shard_map/ppermute | solution.py:38
  287.8 36.9 %collective-permute-start.45 = (bf16[512,1024]{1,0:T(8,128)(2,1)}, bf16[512,1024]{1,0:T(8,128)(2,1)}, u32[]{:S(2)}, u32[]{:S(2)}) collective-permute-start(bf16[512,1024]{1,0:T(8,128)(2,1)} %pad_maximum_fusion.15), channel_id=1, source_target_pairs={{0,4},{4,0},{1,5},{5,1},{2,6},{6,2},{3,7},{7,3},{8,12},{12,8},{9,1... | collective-permute-start | bytes 3145736 | tf_op jit(solution)/shard_map/ppermute | solution.py:38
  295.6 21.0 %collective-permute-start.42 = (bf16[256,1024]{1,0:T(8,128)(2,1)S(1)}, bf16[256,1024]{1,0:T(8,128)(2,1)}, u32[]{:S(2)}, u32[]{:S(2)}) collective-permute-start(bf16[256,1024]{1,0:T(8,128)(2,1)S(1)} %get-tuple-element.299), channel_id=1, source_target_pairs={{0,2},{1,3},{2,0},{3,1},{4,6},{5,7},{6,4},{7,5},{8,10},{9,11},{10,... | collective-permute-start | bytes 1572872 | tf_op jit(solution)/shard_map/ppermute | solution.py:38
  311.1 29.2 %collective-permute-start.61 = (bf16[128,1024]{1,0:T(8,128)(2,1)}, bf16[128,1024]{1,0:T(8,128)(2,1)}, u32[]{:S(2)}, u32[]{:S(2)}) collective-permute-start(bf16[128,1024]{1,0:T(8,128)(2,1)} %slice.1372), channel_id=1, source_target_pairs={{0,16},{8,24},{16,0},{24,8},{1,17},{9,25},{17,1},{25,9},{2,18},{10... | collective-permute-start | bytes 786440 | tf_op jit(solution)/shard_map/ppermute | solution.py:38
  335.8 15.5 %collective-permute-start.46 = (bf16[256,1024]{1,0:T(8,128)(2,1)S(1)}, bf16[256,1024]{1,0:T(8,128)(2,1)S(1)}, u32[]{:S(2)}, u32[]{:S(2)}) collective-permute-start(bf16[256,1024]{1,0:T(8,128)(2,1)S(1)} %slice.1364), channel_id=1, source_target_pairs={{0,8},{8,0},{16,24},{24,16},{1,9},{9,1},{17,25},{25,17},{2,10},{10... | collective-permute-start | bytes 1572872 | tf_op jit(solution)/shard_map/ppermute | solution.py:38
  338.8 31.0 %collective-permute-start.48 = (bf16[1024,512]{1,0:T(8,128)(2,1)S(1)}, bf16[1024,512]{1,0:T(8,128)(2,1)S(1)}, u32[]{:S(2)}, u32[]{:S(2)}) collective-permute-start(bf16[1024,512]{1,0:T(8,128)(2,1)S(1)} %get-tuple-element.148), channel_id=1, source_target_pairs={{4,0},{5,1},{6,2},{7,3},{12,8},{13,9},{14,10},{15,11},{20,16},{21,... | collective-permute-start | bytes 3145736 | tf_op jit(solution)/shard_map/ppermute | solution.py:44
  342.7 19.5 %collective-permute-start.56 = (bf16[256,256]{1,0:T(8,128)(2,1)S(1)}, bf16[256,256]{1,0:T(8,128)(2,1)S(1)}, u32[]{:S(2)}, u32[]{:S(2)}) collective-permute-start(bf16[256,256]{1,0:T(8,128)(2,1)S(1)} %slice.1376), channel_id=1, source_target_pairs={{0,8},{8,0},{16,24},{24,16},{1,9},{9,1},{17,25},{25,17},{2,10},{10... | collective-permute-start | bytes 393224 | tf_op jit(solution)/shard_map/ppermute | solution.py:38
  362.4 27.5 %collective-permute-start.57 = (bf16[128,256]{1,0:T(8,128)(2,1)S(1)}, bf16[128,256]{1,0:T(8,128)(2,1)S(1)}, u32[]{:S(2)}, u32[]{:S(2)}) collective-permute-start(bf16[128,256]{1,0:T(8,128)(2,1)S(1)} %slice.1378), channel_id=1, source_target_pairs={{0,16},{8,24},{16,0},{24,8},{1,17},{9,25},{17,1},{25,9},{2,18},{10... | collective-permute-start | bytes 196616 | tf_op jit(solution)/shard_map/ppermute | solution.py:38
  363.1 14.7 %collective-permute-start.58 = (bf16[128,1024]{1,0:T(8,128)(2,1)S(1)}, bf16[128,1024]{1,0:T(8,128)(2,1)S(1)}, u32[]{:S(2)}, u32[]{:S(2)}) collective-permute-start(bf16[128,1024]{1,0:T(8,128)(2,1)S(1)} %slice.1373), channel_id=1, source_target_pairs={{0,16},{8,24},{16,0},{24,8},{1,17},{9,25},{17,1},{25,9},{2,18},{10... | collective-permute-start | bytes 786440 | tf_op jit(solution)/shard_map/ppermute | solution.py:38
  367.3 17.7 %collective-permute-start.53 = (bf16[512,768]{1,0:T(8,128)(2,1)}, bf16[512,768]{1,0:T(8,128)(2,1)S(1)}, u32[]{:S(2)}, u32[]{:S(2)}) collective-permute-start(bf16[512,768]{1,0:T(8,128)(2,1)} %add_convert_fusion.4), channel_id=1, source_target_pairs={{0,4},{4,0},{1,5},{5,1},{2,6},{6,2},{3,7},{7,3},{8,12},{12,8},{9,1... | collective-permute-start | bytes 2359304 | tf_op jit(solution)/shard_map/ppermute | solution.py:38
  381.6 21.3 %collective-permute-start.50 = (bf16[256,1024]{1,0:T(8,128)(2,1)}, bf16[256,1024]{1,0:T(8,128)(2,1)}, u32[]{:S(2)}, u32[]{:S(2)}) collective-permute-start(bf16[256,1024]{1,0:T(8,128)(2,1)} %slice.1363), channel_id=1, source_target_pairs={{0,2},{1,3},{2,0},{3,1},{4,6},{5,7},{6,4},{7,5},{8,10},{9,11},{10,... | collective-permute-start | bytes 1572872 | tf_op jit(solution)/shard_map/ppermute | solution.py:38
  (157 other events, 1237.2 us)

commit v6 on v5

--- a/solution.py
+++ b/solution.py
@@ -608,7 +608,10 @@
     )
     dense_low = low(grad_three)
     dense_rows = gather_rows(dense_low)
+    down_terms = weight_terms((dense_rows, act_low))
+    down_far_term = low(down_terms(slice(model // 2, model)))
     hidden_low = low(matmul(dense_rows, down_full) * wide(slope_low))
+    hidden_low = after(hidden_low, down_far_term)
     second_share = scatter_rows(lambda s: contract("rf,df->rd", hidden_low[s], up_full))
     grad_two, gain_memory_grad, shift_memory_grad = norm_back(
         grad_three + second_share, normed_two, rstd_two, gain_memory
@@ -616,7 +619,8 @@
 
     cross_low = low(grad_two)
     cross_rows = gather_rows(cross_low)
-    down_part = scatter_tree(weight_terms((dense_rows, act_low)), model, ctx_steps, cross_rows)
+    down_part = scatter_tree(down_terms, model, ctx_steps, cross_low, None, down_far_term)
+    cross_rows = after(cross_rows, down_part)
     grad_cross_mixed = low(matmul(cross_rows, mout_full))
     mquery_back, mkv_sum = attend_back(
         width, "cross", mquery, grad_cross_mixed, cross_mixed_t, cross_lse, mkv
@@ -663,6 +667,8 @@
     query_back, kv_back = attend_back(
         width, "own", qkv, grad_self_later, mixed_t, self_lse, None, meta, lower, query_start
     )
+    out_near_grads = scatter_more(out_part, near_steps, None, query_back)
+    query_pre = query_back * 0.125
     out_near_grads = scatter_more(out_part, near_steps, None, query_back)
     query_pre = query_back * 0.125
     small_grads = scatter_more(small_near_grads, far_steps, None, query_pre)

time: 418 us -> 416 us (level)
    unnamed x251 -> x247, local copies, waits for them, and re-layouts: 16.8 us -> 15.4 us
  transfers between devices with their start and end apart: 70 -> 70, of which waited for: 42 -> 41; matrix products, arithmetic and copies ran while one was open for 23% -> 23% of each run, Pallas kernels for 7% -> 7%
where the time goes in v6:
time: 416 us; the launch traced here: 410 us
  waiting for transfers between devices  171 us (41%)
  starting transfers between devices  79.9 us (19%)
  matrix products  48.8 us (12%)
  other arithmetic  46.8 us (11%)
  local copies, waits for them, and re-layouts  31.4 us (8%)
  Pallas kernels  27.8 us (7%)
    ppermute x68, waiting for transfers between devices, swap(): lax.ppermute(array, axis, [(i, i ^ bit) for i in range(lax.axis_size(axis...  171 us
    ppermute x68, starting transfers between devices, swap(): lax.ppermute(array, axis, [(i, i ^ bit) for i in range(lax.axis_size(axis...  75 us
    dot_general x34, matrix products, contract(): return jnp.einsum(form, left, right, preferred_element_type=jnp.float32)  31 us
    dot_general x8, matrix products, matmul(): return jnp.dot(left, right, preferred_element_type=jnp.float32)  17.8 us
    pallas_call x3, Pallas kernels, attend_back(): pl.pallas_call(partial(attend_back_kernel, width, kind), in_specs=specs,...  16.5 us
    unnamed x247, local copies, waits for them, and re-layouts  15.4 us
    concatenate x17, other arithmetic, gather_tree(): jnp.concatenate([after(array, used if n == len(steps) - 1 else None), arr...  11.8 us
    pallas_call x2, Pallas kernels, attend(): pl.pallas_call(partial(attend_kernel, width, masked), in_specs=specs, out...  11.3 us
  transfers between devices with their start and end apart: 70, of which 41 were waited for; matrix products, arithmetic and copies ran while one was open for 23% of the time, Pallas kernels for 7%

profile of v6, /device:TPU:0, one launch (start us, length us, event | category | flops | bytes accessed | tf_op | source)
XLA Modules:
  0.0 409.7 jit_solution(10685055238649504056)
XLA Ops:
  1.8 4.1 %collective-permute-start.2 = (bf16[128,768]{1,0:T(8,128)(2,1)S(1)}, bf16[128,768]{1,0:T(8,128)(2,1)S(1)}, u32[]{:S(2)}, u32[]{:S(2)}) collective-permute-start(bf16[128,768]{1,0:T(8,128)(2,1)S(1)} %fusion.87), channel_id=1, source_target_pairs={{0,16},{8,24},{16,0},{24,8},{1,17},{9,25},{17,1},{25,9},{2,18},{10... | collective-permute-start | bytes 589832 | tf_op jit(solution)/shard_map/ppermute | solution.py:38
  5.9 3.4 collective-permute-start.9
  26.8 5.0 %collective-permute-done.3 = bf16[256,768]{1,0:T(8,128)(2,1)S(1)} collective-permute-done((bf16[256,768]{1,0:T(8,128)(2,1)S(1)}, bf16[256,768]{1,0:T(8,128)(2,1)S(1)}, u32[]{:S(2)}, u32[]{:S(2)}) %collective-permute-start.3) | collective-permute-done | bytes 393248 | tf_op jit(solution)/shard_map/ppermute | solution.py:38
  41.4 5.8 %collective-permute-done.7 = bf16[128,1024]{1,0:T(8,128)(2,1)S(1)} collective-permute-done((bf16[128,1024]{1,0:T(8,128)(2,1)}, bf16[128,1024]{1,0:T(8,128)(2,1)S(1)}, u32[]{:S(2)}, u32[]{:S(2)}) %collective-permute-start.7) | collective-permute-done | bytes 262176 | tf_op jit(solution)/shard_map/ppermute | solution.py:38
  55.4 2.9 multiply_convert_fusion.2.refs_2_.refs_3_
  66.3 6.9 %shard_map.484 = (bf16[1024,256]{1,0:T(8,128)(2,1)S(1)}, f32[256,1024]{1,0:T(8,128)S(1)}, f32[4,1024]{1,0:T(4,128)S(1)}) custom-call(s32[5]{0:T(128)S(1)} %pad_add_fusion.1.refs_0_, s32[1,1024]{1,0:T(1,128)S(1)} %maximum_subtract_fusion.refs_1_, bf16[1024,768]{1,0:T(8,128)(2,1)S(1)} %multiply_convert_fusion.2.refs_2_.refs_3_, ...), custom_call_target="tpu_custom_call" | custom-call | flops 12884901888 | bytes 2097152 | tf_op jit(solution)/shard_map/pallas_call | solution.py:330
  78.5 3.8 collective-permute-start.20
  84.8 5.9 %collective-permute-done.18 = bf16[128,1024]{0,1:T(8,128)(2,1)S(1)} collective-permute-done((bf16[128,1024]{0,1:T(8,128)(2,1)S(1)}, bf16[128,1024]{0,1:T(8,128)(2,1)S(1)}, u32[]{:S(2)}, u32[]{:S(2)}) %collective-permute-start.18) | collective-permute-done | bytes 262176 | tf_op jit(solution)/shard_map/ppermute | solution.py:38
  90.7 5.4 %collective-permute-done.17 = bf16[256,1024]{1,0:T(8,128)(2,1)S(1)} collective-permute-done((bf16[256,1024]{1,0:T(8,128)(2,1)S(1)}, bf16[256,1024]{1,0:T(8,128)(2,1)S(1)}, u32[]{:S(2)}, u32[]{:S(2)}) %collective-permute-start.17) | collective-permute-done | bytes 524320 | tf_op jit(solution)/shard_map/ppermute | solution.py:38
  96.2 3.4 collective-permute-done.19
  104.1 9.5 %collective-permute-done.21 = bf16[256,1024]{1,0:T(8,128)(2,1)S(1)} collective-permute-done((bf16[256,1024]{1,0:T(8,128)(2,1)S(1)}, bf16[256,1024]{1,0:T(8,128)(2,1)S(1)}, u32[]{:S(2)}, u32[]{:S(2)}) %collective-permute-start.21) | collective-permute-done | bytes 524320 | tf_op jit(solution)/shard_map/ppermute | solution.py:38
  119.6 4.4 %shard_map.485 = (bf16[1024,256]{1,0:T(8,128)(2,1)S(1)}, f32[256,1024]{1,0:T(8,128)S(1)}, f32[4,1024]{1,0:T(4,128)S(1)}) custom-call(bf16[1024,256]{1,0:T(8,128)(2,1)S(1)} %fusion.9.refs_0_, bf16[512,512]{1,0:T(8,128)(2,1)S(1)} %pad_maximum_fusion.21.refs_1_.refs_4_), custom_call_target="tpu_custom_call" | custom-call | flops 6442450944 | bytes 2097152 | tf_op jit(solution)/shard_map/pallas_call | solution.py:330
  124.1 5.1 %collective-permute-done.25 = bf16[512,512]{1,0:T(8,128)(2,1)S(1)} collective-permute-done((bf16[512,512]{1,0:T(8,128)(2,1)S(1)}, bf16[512,512]{1,0:T(8,128)(2,1)S(1)}, u32[]{:S(2)}, u32[]{:S(2)}) %collective-permute-start.25) | collective-permute-done | bytes 524320 | tf_op jit(solution)/shard_map/ppermute | solution.py:38
  134.0 10.2 %collective-permute-done.28 = bf16[512,512]{0,1:T(8,128)(2,1)S(1)} collective-permute-done((bf16[512,512]{0,1:T(8,128)(2,1)S(1)}, bf16[512,512]{0,1:T(8,128)(2,1)S(1)}, u32[]{:S(2)}, u32[]{:S(2)}) %collective-permute-start.28) | collective-permute-done | bytes 524320 | tf_op jit(solution)/shard_map/ppermute | solution.py:38
  150.5 10.8 %collective-permute-done.29 = bf16[256,1024]{1,0:T(8,128)(2,1)S(1)} collective-permute-done((bf16[256,1024]{1,0:T(8,128)(2,1)S(1)}, bf16[256,1024]{1,0:T(8,128)(2,1)S(1)}, u32[]{:S(2)}, u32[]{:S(2)}) %collective-permute-start.29) | collective-permute-done | bytes 524320 | tf_op jit(solution)/shard_map/ppermute | solution.py:38
  164.8 3.4 multiply_convert_fusion.1
  174.5 12.7 %collective-permute-done.33 = bf16[256,1024]{1,0:T(8,128)(2,1)S(1)} collective-permute-done((bf16[256,1024]{1,0:T(8,128)(2,1)S(1)}, bf16[256,1024]{1,0:T(8,128)(2,1)S(1)}, u32[]{:S(2)}, u32[]{:S(2)}) %collective-permute-start.33) | collective-permute-done | bytes 524320 | tf_op jit(solution)/shard_map/ppermute | solution.py:38
  190.2 12.0 %collective-permute-done.34 = bf16[256,1024]{1,0:T(8,128)(2,1)S(1)} collective-permute-done((bf16[256,1024]{1,0:T(8,128)(2,1)S(1)}, bf16[256,1024]{1,0:T(8,128)(2,1)S(1)}, u32[]{:S(2)}, u32[]{:S(2)}) %collective-permute-start.34) | collective-permute-done | bytes 524320 | tf_op jit(solution)/shard_map/ppermute | solution.py:38
  207.5 6.5 %multiply_convert_fusion = bf16[1024,1024]{1,0:T(8,128)(2,1)S(1)} fusion(bf16[1024,1024]{0,1:T(8,128)(2,1)S(1)} %pad_maximum_fusion.4, f32[1024,1024]{1,0:T(8,128)S(1)} %get-tuple-element.438, f32[1024]{0:T(1024)S(1)} %copy-done.106, bf16[512,1024]{1,0:T(8,128)(2,1)S(1)} %collective-permute-done.35, bf16[256,1024]{1,0:T(8,128)(2,1)S(1)} %collective-permute-done.34, ...), kind=kOutput, calls=%fused_computation.7 | convolution fusion | flops 2167406592 | bytes 10489856 | tf_op jit(solution)/shard_map/dot_general | solution.py:22
  218.9 3.2 fusion.32
  229.8 10.6 %collective-permute-done.37 = bf16[256,1024]{1,0:T(8,128)(2,1)S(1)} collective-permute-done((bf16[256,1024]{1,0:T(8,128)(2,1)S(1)}, bf16[256,1024]{1,0:T(8,128)(2,1)S(1)}, u32[]{:S(2)}, u32[]{:S(2)}) %collective-permute-start.37) | collective-permute-done | bytes 524320 | tf_op jit(solution)/shard_map/ppermute | solution.py:38
  246.9 8.2 %collective-permute-done.38 = bf16[256,1024]{1,0:T(8,128)(2,1)S(1)} collective-permute-done((bf16[256,1024]{1,0:T(8,128)(2,1)S(1)}, bf16[256,1024]{1,0:T(8,128)(2,1)S(1)}, u32[]{:S(2)}, u32[]{:S(2)}) %collective-permute-start.38) | collective-permute-done | bytes 524320 | tf_op jit(solution)/shard_map/ppermute | solution.py:38
  259.4 6.6 %shard_map.486 = (bf16[1024,256]{1,0:T(8,128)(2,1)S(1)}, f32[512,512]{1,0:T(8,128)S(1)}) custom-call(bf16[1024,256]{1,0:T(8,128)(2,1)S(1)} %fusion.9.refs_0_, bf16[1024,256]{1,0:T(8,128)(2,1)S(1)} %convolution_convert_fusion.8.refs_1_, f32[256,1024]{1,0:T(8,128)S(1)} %copy-done.5, f32[4,1024]{1,0:T(4,128)S(1)} %get-tuple-element.138.refs_3_, ...), custom_call_target="tpu_custom_call" | custom-call | flops 8589934592 | bytes 4194304 | tf_op jit(solution)/shard_map/pallas_call | solution.py:357
  299.4 8.3 %collective-permute-done.65 = f32[9,1024]{1,0:T(8,128)S(1)} collective-permute-done((f32[9,1024]{1,0:T(8,128)S(1)}, f32[9,1024]{1,0:T(8,128)S(1)}, u32[]{:S(2)}, u32[]{:S(2)}) %collective-permute-start.65) | collective-permute-done | bytes 36896 | tf_op jit(solution)/shard_map/ppermute | solution.py:38
  328.3 4.1 %collective-permute-start.48 = (bf16[512,256]{1,0:T(8,128)(2,1)S(1)}, bf16[512,256]{1,0:T(8,128)(2,1)S(1)}, u32[]{:S(2)}, u32[]{:S(2)}) collective-permute-start(bf16[512,256]{1,0:T(8,128)(2,1)S(1)} %convolution_convert_fusion.10), channel_id=1, source_target_pairs={{0,4},{4,0},{1,5},{5,1},{2,6},{6,2},{3,7},{7,3},{8,12},{12,8},{9,1... | collective-permute-start | bytes 786440 | tf_op jit(solution)/shard_map/ppermute | solution.py:38
  332.4 3.0 collective-permute-start.47
  339.2 3.5 collective-permute-start.57
  342.7 5.5 %collective-permute-done.47 = bf16[256,1024]{1,0:T(8,128)(2,1)S(1)} collective-permute-done((bf16[256,1024]{1,0:T(8,128)(2,1)S(1)}, bf16[256,1024]{1,0:T(8,128)(2,1)S(1)}, u32[]{:S(2)}, u32[]{:S(2)}) %collective-permute-start.47) | collective-permute-done | bytes 524320 | tf_op jit(solution)/shard_map/ppermute | solution.py:38
  348.3 8.7 %shard_map.488 = (bf16[1024,256]{1,0:T(8,128)(2,1)S(1)}, bf16[1024,512]{1,0:T(8,128)(2,1)S(1)}) custom-call(s32[5]{0:T(128)S(1)} %pad_add_fusion.1.refs_0_, s32[1,1024]{1,0:T(1,128)S(1)} %maximum_subtract_fusion.refs_1_, f32[256,1024]{1,0:T(8,128)S(1)} %get-tuple-element.146.refs_2_, bf16[1024,768]{1,0:T(8,128)(2,1)S(1)} %copy-done.3, ...), custom_call_target="tpu_custom_call" | custom-call | flops 17179869184 | bytes 4194304 | tf_op jit(solution)/shard_map/pallas_call | solution.py:357
  370.5 3.9 collective-permute-done.59
  391.4 6.9 %collective-permute-done.55 = bf16[256,768]{1,0:T(8,128)(2,1)S(1)} collective-permute-done((bf16[256,768]{1,0:T(8,128)(2,1)S(1)}, bf16[256,768]{1,0:T(8,128)(2,1)S(1)}, u32[]{:S(2)}, u32[]{:S(2)}) %collective-permute-start.55) | collective-permute-done | bytes 393248 | tf_op jit(solution)/shard_map/ppermute | solution.py:38
  402.1 6.4 %collective-permute-done.56 = bf16[128,768]{1,0:T(8,128)(2,1)S(1)} collective-permute-done((bf16[128,768]{1,0:T(8,128)(2,1)S(1)}, bf16[128,768]{1,0:T(8,128)(2,1)S(1)}, u32[]{:S(2)}, u32[]{:S(2)}) %collective-permute-start.56) | collective-permute-done | bytes 196640 | tf_op jit(solution)/shard_map/ppermute | solution.py:38
  (637 shorter events, 205.6 us)
Async XLA Ops:
  1.8 18.5 %collective-permute-start.2 = (bf16[128,768]{1,0:T(8,128)(2,1)S(1)}, bf16[128,768]{1,0:T(8,128)(2,1)S(1)}, u32[]{:S(2)}, u32[]{:S(2)}) collective-permute-start(bf16[128,768]{1,0:T(8,128)(2,1)S(1)} %fusion.87), channel_id=1, source_target_pairs={{0,16},{8,24},{16,0},{24,8},{1,17},{9,25},{17,1},{25,9},{2,18},{10... | collective-permute-start | bytes 589832 | tf_op jit(solution)/shard_map/ppermute | solution.py:38
  5.9 16.4 %collective-permute-start.9 = (bf16[256,1024]{1,0:T(8,128)(2,1)}, bf16[256,1024]{1,0:T(8,128)(2,1)S(1)}, u32[]{:S(2)}, u32[]{:S(2)}) collective-permute-start(bf16[256,1024]{1,0:T(8,128)(2,1)} %bitcast.117), channel_id=1, source_target_pairs={{0,4},{1,5},{2,6},{3,7},{8,12},{9,13},{10,14},{11,15},{16,20},{17,... | collective-permute-start | bytes 1572872 | tf_op jit(solution)/shard_map/ppermute | solution.py:44
  26.5 25.8 %collective-permute-start.1 = (bf16[512,1024]{1,0:T(8,128)(2,1)}, bf16[512,1024]{1,0:T(8,128)(2,1)}, u32[]{:S(2)}, u32[]{:S(2)}) collective-permute-start(bf16[512,1024]{1,0:T(8,128)(2,1)} %pad_maximum_fusion.10), channel_id=1, source_target_pairs={{0,1},{1,0},{2,3},{3,2},{4,5},{5,4},{6,7},{7,6},{8,9},{9,8},{10,11... | collective-permute-start | bytes 3145736 | tf_op jit(solution)/shard_map/ppermute | solution.py:38
  32.9 17.8 %collective-permute-start.4 = (bf16[512,768]{1,0:T(8,128)(2,1)}, bf16[512,768]{1,0:T(8,128)(2,1)}, u32[]{:S(2)}, u32[]{:S(2)}) collective-permute-start(bf16[512,768]{1,0:T(8,128)(2,1)} %pad_maximum_fusion.18), channel_id=1, source_target_pairs={{0,4},{4,0},{1,5},{5,1},{2,6},{6,2},{3,7},{7,3},{8,12},{12,8},{9,1... | collective-permute-start | bytes 2359304 | tf_op jit(solution)/shard_map/ppermute | solution.py:38
  32.9 15.4 %collective-permute-start.10 = (bf16[256,1024]{1,0:T(8,128)(2,1)S(1)}, bf16[256,1024]{1,0:T(8,128)(2,1)S(1)}, u32[]{:S(2)}, u32[]{:S(2)}) collective-permute-start(bf16[256,1024]{1,0:T(8,128)(2,1)S(1)} %constant_dynamic-update-slice_fusion.10), channel_id=1, source_target_pairs={{0,2},{1,3},{2,0},{3,1},{4,6},{5,7},{6,4},{7,5},{8,10},{9,11},{10,... | collective-permute-start | bytes 1572872 | tf_op jit(solution)/shard_map/ppermute | solution.py:38
  48.4 15.2 %collective-permute-start.11 = (bf16[512,1024]{1,0:T(8,128)(2,1)S(1)}, bf16[512,1024]{1,0:T(8,128)(2,1)S(1)}, u32[]{:S(2)}, u32[]{:S(2)}) collective-permute-start(bf16[512,1024]{1,0:T(8,128)(2,1)S(1)} %pad_maximum_fusion.11), channel_id=1, source_target_pairs={{0,1},{1,0},{2,3},{3,2},{4,5},{5,4},{6,7},{7,6},{8,9},{9,8},{10,11... | collective-permute-start | bytes 3145736 | tf_op jit(solution)/shard_map/ppermute | solution.py:38
  52.0 21.9 %collective-permute-start.14 = (bf16[512,256]{0,1:T(8,128)(2,1)S(1)}, bf16[512,256]{0,1:T(8,128)(2,1)S(1)}, u32[]{:S(2)}, u32[]{:S(2)}) collective-permute-start(bf16[512,256]{0,1:T(8,128)(2,1)S(1)} %pad_maximum_fusion.23), channel_id=1, source_target_pairs={{0,4},{4,0},{1,5},{5,1},{2,6},{6,2},{3,7},{7,3},{8,12},{12,8},{9,1... | collective-permute-start | bytes 786440 | tf_op jit(solution)/shard_map/ppermute | solution.py:38
  75.9 14.7 %collective-permute-start.18 = (bf16[128,1024]{0,1:T(8,128)(2,1)S(1)}, bf16[128,1024]{0,1:T(8,128)(2,1)S(1)}, u32[]{:S(2)}, u32[]{:S(2)}) collective-permute-start(bf16[128,1024]{0,1:T(8,128)(2,1)S(1)} %dynamic-slice_bitcast_fusion), channel_id=1, source_target_pairs={{0,16},{8,24},{16,0},{24,8},{1,17},{9,25},{17,1},{25,9},{2,18},{10... | collective-permute-start | bytes 786440 | tf_op jit(solution)/shard_map/ppermute | solution.py:38
  78.1 18.0 %collective-permute-start.17 = (bf16[256,1024]{1,0:T(8,128)(2,1)S(1)}, bf16[256,1024]{1,0:T(8,128)(2,1)S(1)}, u32[]{:S(2)}, u32[]{:S(2)}) collective-permute-start(bf16[256,1024]{1,0:T(8,128)(2,1)S(1)} %constant_dynamic-update-slice_fusion.20), channel_id=1, source_target_pairs={{0,8},{8,0},{16,24},{24,16},{1,9},{9,1},{17,25},{25,17},{2,10},{10... | collective-permute-start | bytes 1572872 | tf_op jit(solution)/shard_map/ppermute | solution.py:38
  78.5 17.6 %collective-permute-start.20 = (bf16[512,512]{1,0:T(8,128)(2,1)S(1)}, bf16[512,512]{1,0:T(8,128)(2,1)S(1)}, u32[]{:S(2)}, u32[]{:S(2)}) collective-permute-start(bf16[512,512]{1,0:T(8,128)(2,1)S(1)} %get-tuple-element.115), channel_id=1, source_target_pairs={{0,4},{4,0},{1,5},{5,1},{2,6},{6,2},{3,7},{7,3},{8,12},{12,8},{9,1... | collective-permute-start | bytes 1572872 | tf_op jit(solution)/shard_map/ppermute | solution.py:38
  83.3 16.4 %collective-permute-start.19 = (bf16[256,512]{1,0:T(8,128)(2,1)S(1)}, bf16[256,512]{1,0:T(8,128)(2,1)S(1)}, u32[]{:S(2)}, u32[]{:S(2)}) collective-permute-start(bf16[256,512]{1,0:T(8,128)(2,1)S(1)} %fusion.10), channel_id=1, source_target_pairs={{0,4},{4,0},{1,5},{5,1},{2,6},{6,2},{3,7},{7,3},{8,12},{12,8},{9,1... | collective-permute-start | bytes 786440 | tf_op jit(solution)/shard_map/ppermute | solution.py:38
  83.5 16.2 %collective-permute-start.16 = (bf16[256,1024]{1,0:T(8,128)(2,1)S(1)}, bf16[256,1024]{1,0:T(8,128)(2,1)S(1)}, u32[]{:S(2)}, u32[]{:S(2)}) collective-permute-start(bf16[256,1024]{1,0:T(8,128)(2,1)S(1)} %slice.1365), channel_id=1, source_target_pairs={{0,2},{1,3},{2,0},{3,1},{4,6},{5,7},{6,4},{7,5},{8,10},{9,11},{10,... | collective-permute-start | bytes 1572872 | tf_op jit(solution)/shard_map/ppermute | solution.py:38
  114.8 14.3 %collective-permute-start.25 = (bf16[512,512]{1,0:T(8,128)(2,1)S(1)}, bf16[512,512]{1,0:T(8,128)(2,1)S(1)}, u32[]{:S(2)}, u32[]{:S(2)}) collective-permute-start(bf16[512,512]{1,0:T(8,128)(2,1)S(1)} %get-tuple-element.124), channel_id=1, source_target_pairs={{0,4},{4,0},{1,5},{5,1},{2,6},{6,2},{3,7},{7,3},{8,12},{12,8},{9,1... | collective-permute-start | bytes 1572872 | tf_op jit(solution)/shard_map/ppermute | solution.py:38
  129.8 14.4 %collective-permute-start.28 = (bf16[512,512]{0,1:T(8,128)(2,1)S(1)}, bf16[512,512]{0,1:T(8,128)(2,1)S(1)}, u32[]{:S(2)}, u32[]{:S(2)}) collective-permute-start(bf16[512,512]{0,1:T(8,128)(2,1)S(1)} %get-tuple-element.127), channel_id=1, source_target_pairs={{0,4},{4,0},{1,5},{5,1},{2,6},{6,2},{3,7},{7,3},{8,12},{12,8},{9,1... | collective-permute-start | bytes 1572872 | tf_op jit(solution)/shard_map/ppermute | solution.py:38
  173.2 14.0 %collective-permute-start.33 = (bf16[256,1024]{1,0:T(8,128)(2,1)S(1)}, bf16[256,1024]{1,0:T(8,128)(2,1)S(1)}, u32[]{:S(2)}, u32[]{:S(2)}) collective-permute-start(bf16[256,1024]{1,0:T(8,128)(2,1)S(1)} %slice.1363), channel_id=1, source_target_pairs={{0,2},{1,3},{2,0},{3,1},{4,6},{5,7},{6,4},{7,5},{8,10},{9,11},{10,... | collective-permute-start | bytes 1572872 | tf_op jit(solution)/shard_map/ppermute | solution.py:38
  217.4 25.7 %collective-permute-start.40 = (bf16[512,1024]{1,0:T(8,128)(2,1)}, bf16[512,1024]{1,0:T(8,128)(2,1)S(1)}, u32[]{:S(2)}, u32[]{:S(2)}) collective-permute-start(bf16[512,1024]{1,0:T(8,128)(2,1)} %convolution_convert_fusion.3), channel_id=1, source_target_pairs={{0,4},{4,0},{1,5},{5,1},{2,6},{6,2},{3,7},{7,3},{8,12},{12,8},{9,1... | collective-permute-start | bytes 3145736 | tf_op jit(solution)/shard_map/ppermute | solution.py:38
  226.3 14.0 %collective-permute-start.37 = (bf16[256,1024]{1,0:T(8,128)(2,1)S(1)}, bf16[256,1024]{1,0:T(8,128)(2,1)S(1)}, u32[]{:S(2)}, u32[]{:S(2)}) collective-permute-start(bf16[256,1024]{1,0:T(8,128)(2,1)S(1)} %slice.1362), channel_id=1, source_target_pairs={{0,2},{1,3},{2,0},{3,1},{4,6},{5,7},{6,4},{7,5},{8,10},{9,11},{10,... | collective-permute-start | bytes 1572872 | tf_op jit(solution)/shard_map/ppermute | solution.py:38
  243.7 24.7 %collective-permute-start.60 = (bf16[512,1024]{1,0:T(8,128)(2,1)S(1)}, bf16[512,1024]{1,0:T(8,128)(2,1)S(1)}, u32[]{:S(2)}, u32[]{:S(2)}) collective-permute-start(bf16[512,1024]{1,0:T(8,128)(2,1)S(1)} %convolution_convert_fusion), channel_id=1, source_target_pairs={{0,4},{4,0},{1,5},{5,1},{2,6},{6,2},{3,7},{7,3},{8,12},{12,8},{9,1... | collective-permute-start | bytes 3145736 | tf_op jit(solution)/shard_map/ppermute | solution.py:38
  245.2 23.5 %collective-permute-start.63 = (bf16[256,1024]{1,0:T(8,128)(2,1)S(1)}, bf16[256,1024]{1,0:T(8,128)(2,1)S(1)}, u32[]{:S(2)}, u32[]{:S(2)}) collective-permute-start(bf16[256,1024]{1,0:T(8,128)(2,1)S(1)} %slice.1357), channel_id=1, source_target_pairs={{0,8},{8,0},{16,24},{24,16},{1,9},{9,1},{17,25},{25,17},{2,10},{10... | collective-permute-start | bytes 1572872 | tf_op jit(solution)/shard_map/ppermute | solution.py:38
  277.0 30.8 %collective-permute-start.64 = (bf16[128,1024]{1,0:T(8,128)(2,1)}, bf16[128,1024]{1,0:T(8,128)(2,1)S(1)}, u32[]{:S(2)}, u32[]{:S(2)}) collective-permute-start(bf16[128,1024]{1,0:T(8,128)(2,1)} %slice.1367), channel_id=1, source_target_pairs={{0,16},{8,24},{16,0},{24,8},{1,17},{9,25},{17,1},{25,9},{2,18},{10... | collective-permute-start | bytes 786440 | tf_op jit(solution)/shard_map/ppermute | solution.py:38
  280.6 16.6 %collective-permute-start.61 = (bf16[256,1024]{1,0:T(8,128)(2,1)}, bf16[256,1024]{1,0:T(8,128)(2,1)}, u32[]{:S(2)}, u32[]{:S(2)}) collective-permute-start(bf16[256,1024]{1,0:T(8,128)(2,1)} %slice.1358), channel_id=1, source_target_pairs={{0,8},{8,0},{16,24},{24,16},{1,9},{9,1},{17,25},{25,17},{2,10},{10... | collective-permute-start | bytes 1572872 | tf_op jit(solution)/shard_map/ppermute | solution.py:38
  284.8 37.2 %collective-permute-start.46 = (bf16[512,1024]{1,0:T(8,128)(2,1)}, bf16[512,1024]{1,0:T(8,128)(2,1)}, u32[]{:S(2)}, u32[]{:S(2)}) collective-permute-start(bf16[512,1024]{1,0:T(8,128)(2,1)} %pad_maximum_fusion.15), channel_id=1, source_target_pairs={{0,4},{4,0},{1,5},{5,1},{2,6},{6,2},{3,7},{7,3},{8,12},{12,8},{9,1... | collective-permute-start | bytes 3145736 | tf_op jit(solution)/shard_map/ppermute | solution.py:38
  289.3 23.6 %collective-permute-start.53 = (bf16[64,1024]{1,0:T(8,128)(2,1)}, bf16[64,1024]{1,0:T(8,128)(2,1)}, u32[]{:S(2)}, u32[]{:S(2)}) collective-permute-start(bf16[64,1024]{1,0:T(8,128)(2,1)} %slice.1373), channel_id=1, source_target_pairs={{0,2},{1,3},{2,0},{3,1},{4,6},{5,7},{6,4},{7,5},{8,10},{9,11},{10,... | collective-permute-start | bytes 393224 | tf_op jit(solution)/shard_map/ppermute | solution.py:38
  293.5 20.4 %collective-permute-start.43 = (bf16[256,1024]{1,0:T(8,128)(2,1)S(1)}, bf16[256,1024]{1,0:T(8,128)(2,1)}, u32[]{:S(2)}, u32[]{:S(2)}) collective-permute-start(bf16[256,1024]{1,0:T(8,128)(2,1)S(1)} %get-tuple-element.303), channel_id=1, source_target_pairs={{0,2},{1,3},{2,0},{3,1},{4,6},{5,7},{6,4},{7,5},{8,10},{9,11},{10,... | collective-permute-start | bytes 1572872 | tf_op jit(solution)/shard_map/ppermute | solution.py:38
  309.6 27.4 %collective-permute-start.62 = (bf16[128,1024]{1,0:T(8,128)(2,1)}, bf16[128,1024]{1,0:T(8,128)(2,1)S(1)}, u32[]{:S(2)}, u32[]{:S(2)}) collective-permute-start(bf16[128,1024]{1,0:T(8,128)(2,1)} %slice.1368), channel_id=1, source_target_pairs={{0,16},{8,24},{16,0},{24,8},{1,17},{9,25},{17,1},{25,9},{2,18},{10... | collective-permute-start | bytes 786440 | tf_op jit(solution)/shard_map/ppermute | solution.py:38
  332.4 15.8 %collective-permute-start.47 = (bf16[256,1024]{1,0:T(8,128)(2,1)S(1)}, bf16[256,1024]{1,0:T(8,128)(2,1)S(1)}, u32[]{:S(2)}, u32[]{:S(2)}) collective-permute-start(bf16[256,1024]{1,0:T(8,128)(2,1)S(1)} %slice.1360), channel_id=1, source_target_pairs={{0,8},{8,0},{16,24},{24,16},{1,9},{9,1},{17,25},{25,17},{2,10},{10... | collective-permute-start | bytes 1572872 | tf_op jit(solution)/shard_map/ppermute | solution.py:38
  335.6 31.6 %collective-permute-start.49 = (bf16[1024,512]{1,0:T(8,128)(2,1)S(1)}, bf16[1024,512]{1,0:T(8,128)(2,1)S(1)}, u32[]{:S(2)}, u32[]{:S(2)}) collective-permute-start(bf16[1024,512]{1,0:T(8,128)(2,1)S(1)} %get-tuple-element.153), channel_id=1, source_target_pairs={{4,0},{5,1},{6,2},{7,3},{12,8},{13,9},{14,10},{15,11},{20,16},{21,... | collective-permute-start | bytes 3145736 | tf_op jit(solution)/shard_map/ppermute | solution.py:44
  339.2 18.0 %collective-permute-start.57 = (bf16[256,256]{1,0:T(8,128)(2,1)S(1)}, bf16[256,256]{1,0:T(8,128)(2,1)S(1)}, u32[]{:S(2)}, u32[]{:S(2)}) collective-permute-start(bf16[256,256]{1,0:T(8,128)(2,1)S(1)} %slice.1372), channel_id=1, source_target_pairs={{0,8},{8,0},{16,24},{24,16},{1,9},{9,1},{17,25},{25,17},{2,10},{10... | collective-permute-start | bytes 393224 | tf_op jit(solution)/shard_map/ppermute | solution.py:38
  358.0 29.4 %collective-permute-start.58 = (bf16[128,256]{1,0:T(8,128)(2,1)}, bf16[128,256]{1,0:T(8,128)(2,1)S(1)}, u32[]{:S(2)}, u32[]{:S(2)}) collective-permute-start(bf16[128,256]{1,0:T(8,128)(2,1)} %slice.1374), channel_id=1, source_target_pairs={{0,16},{8,24},{16,0},{24,8},{1,17},{9,25},{17,1},{25,9},{2,18},{10... | collective-permute-start | bytes 196616 | tf_op jit(solution)/shard_map/ppermute | solution.py:38
  358.9 15.6 %collective-permute-start.59 = (bf16[128,1024]{1,0:T(8,128)(2,1)S(1)}, bf16[128,1024]{1,0:T(8,128)(2,1)S(1)}, u32[]{:S(2)}, u32[]{:S(2)}) collective-permute-start(bf16[128,1024]{1,0:T(8,128)(2,1)S(1)} %slice.1369), channel_id=1, source_target_pairs={{0,16},{8,24},{16,0},{24,8},{1,17},{9,25},{17,1},{25,9},{2,18},{10... | collective-permute-start | bytes 786440 | tf_op jit(solution)/shard_map/ppermute | solution.py:38
  363.0 18.9 %collective-permute-start.54 = (bf16[512,768]{1,0:T(8,128)(2,1)}, bf16[512,768]{1,0:T(8,128)(2,1)S(1)}, u32[]{:S(2)}, u32[]{:S(2)}) collective-permute-start(bf16[512,768]{1,0:T(8,128)(2,1)} %add_convert_fusion.4), channel_id=1, source_target_pairs={{0,4},{4,0},{1,5},{5,1},{2,6},{6,2},{3,7},{7,3},{8,12},{12,8},{9,1... | collective-permute-start | bytes 2359304 | tf_op jit(solution)/shard_map/ppermute | solution.py:38
  378.3 22.1 %collective-permute-start.51 = (bf16[256,1024]{1,0:T(8,128)(2,1)}, bf16[256,1024]{1,0:T(8,128)(2,1)}, u32[]{:S(2)}, u32[]{:S(2)}) collective-permute-start(bf16[256,1024]{1,0:T(8,128)(2,1)} %slice.1359), channel_id=1, source_target_pairs={{0,2},{1,3},{2,0},{3,1},{4,6},{5,7},{6,4},{7,5},{8,10},{9,11},{10,... | collective-permute-start | bytes 1572872 | tf_op jit(solution)/shard_map/ppermute | solution.py:38
  (155 other events, 1245.3 us)
